TPU v7x, 256 devices: a whole 4x4x8 slice. The times are simulated.
256 devices in a mesh: dp: 16 (over z, core), ctx: 4 (over y), tp: 4 (over x).
Axes of the slice: x: 4, y: 4, z: 8, core: 2. Of those that a mesh axis runs over, the one named last changes fastest.
Arguments:
- tokens_in: bfloat16 [8192, 5120], P(('dp', 'ctx'), 'tp'), may hold values from -6 to 6
- grad_out: bfloat16 [8192, 5120], P(('dp', 'ctx'), 'tp'), may hold values from -3 to 3
- router_logit: float32 [8192], P(('dp', 'ctx')), may hold values from -6 to 6
- expert_index: int32 [8192, 1], P(('dp', 'ctx')), may hold values from 0 to 7; in each aligned block of 128 rows (0 to 127, 128 to 255, ...) at most 20 rows name the same one
- gate_half: bfloat16 [16, 5120, 2048], P(('ctx', 'tp'), None, 'dp'), may hold values from -0.078125 to 0.078125
- up_half: bfloat16 [16, 5120, 2048], P(('ctx', 'tp'), None, 'dp'), may hold values from -0.078125 to 0.078125
- down_half: bfloat16 [16, 2048, 5120], P(('ctx', 'tp'), 'dp'), may hold values from -0.09375 to 0.09375
Outputs:
- input_grad: bfloat16 [8192, 5120], P(('dp', 'ctx'), 'tp')
- logit_grad: bfloat16 [8192], P(('dp', 'ctx'))
- gate_grad: bfloat16 [16, 5120, 2048], P(('ctx', 'tp'), None, 'dp')
- up_grad: bfloat16 [16, 5120, 2048], P(('ctx', 'tp'), None, 'dp')
- down_grad: bfloat16 [16, 2048, 5120], P(('ctx', 'tp'), 'dp')
Inputs may be any that keep to these rules, and one draw needn't show every extreme that they name: `expert_index`: in each aligned block of 128 rows no expert is named by more than 20 rows, a bound that some block reaches.
All inputs are finite; a program needn't handle non-finite values.
Results may differ from a plain program's by a relative error of at most 0.025.
Values may be sent and summed in bfloat16 or wider, within the bound.
No kernel may reach another device: no remote copies, remote signals or barrier semaphores. Data moves between devices by JAX's collectives and lax.ppermute only.
A program may use at most 128 MiB of HBM per device.

v0:
```python
import jax
import jax.numpy as jnp
from jax import lax
from jax.sharding import PartitionSpec as P

HALF = 10


def from_partner(block, axis, bit):
    count = lax.axis_size(axis)
    route = []
    for low in range(count):
        high = low | 1 << bit
        if high != low and high < count:
            route += [(low, high), (high, low)]
    return lax.ppermute(block, axis, route)


def body(tokens_in, grad_out, router_logit, expert_index, gate_half, up_half, down_half):
    n_ctx = lax.axis_size("ctx")
    n_tp = lax.axis_size("tp")
    n_dev = n_ctx * n_tp
    n_exp = n_dev // 2
    tok_rows, part_width = tokens_in.shape
    width = part_width * n_tp
    slots = n_dev * HALF
    inner = (((1,), (1,)), ((), ()))
    outer = (((0,), (0,)), ((), ()))
    route = expert_index[:, 0]
    hit = (route[:, None] == jnp.arange(n_exp, dtype=jnp.int32)[None, :]).astype(jnp.int32)
    before = jnp.cumsum(hit, axis=0) - hit
    rank = jnp.sum(before * hit, axis=1)
    target = 2 * route + rank // HALF
    within = rank % HALF
    weight = jax.nn.sigmoid(router_logit).astype(jnp.bfloat16)
    place_out = within * n_dev + target
    columns = jnp.arange(slots, dtype=jnp.int32)[None, :]
    pick = (place_out[:, None] == columns).astype(jnp.bfloat16)

    def spread(values):
        return lax.dot_general(pick, values, outer, preferred_element_type=jnp.float32).astype(
            jnp.bfloat16
        )

    send_x = spread(tokens_in)
    send_dy = spread(grad_out)
    send_w = spread(weight[:, None])
    recv = (
        lax.all_to_all(
            send_x.reshape(HALF, n_dev, part_width),
            ("ctx", "tp"),
            split_axis=1,
            concat_axis=2,
            tiled=True,
        ),
        lax.all_to_all(
            send_dy.reshape(HALF, n_dev, part_width),
            ("ctx", "tp"),
            split_axis=1,
            concat_axis=2,
            tiled=True,
        ),
        lax.all_to_all(
            send_w.reshape(HALF, n_dev, 1), ("ctx", "tp"), split_axis=1, concat_axis=2, tiled=True
        ),
    )
    rows_x = recv[0].reshape(HALF * n_ctx, width)
    rows_dy = recv[1].reshape(HALF * n_ctx, width)
    rows_w = recv[2].reshape(HALF, n_ctx, n_tp)[:, :, 0].reshape(HALF * n_ctx)
    own = (gate_half[0], up_half[0], down_half[0])
    other = from_partner((own[0], own[1], own[2]), "tp", 0)
    all_x, all_dy, all_w = (
        lax.all_gather(rows_x, "dp", axis=0, tiled=True),
        lax.all_gather(rows_dy, "dp", axis=0, tiled=True),
        lax.all_gather(rows_w, "dp", axis=0, tiled=True),
    )
    member = lax.axis_index("tp") % 2
    first = member == 0

    def join(mine, theirs, axis):
        return jnp.where(
            first, jnp.concatenate([mine, theirs], axis), jnp.concatenate([theirs, mine], axis)
        )

    w_gate = join(own[0], other[0], 1)
    w_up = join(own[1], other[1], 1)
    w_down = join(own[2], other[2], 0)
    gate = jnp.dot(all_x, w_gate, preferred_element_type=jnp.float32)
    up = jnp.dot(all_x, w_up, preferred_element_type=jnp.float32)
    sig = jax.nn.sigmoid(gate)
    act = gate * sig
    hidden = act * up
    back = lax.dot_general(all_dy, w_down, inner, preferred_element_type=jnp.float32)
    router_part = jnp.sum(hidden * back, axis=1)
    scale = all_w.astype(jnp.float32)[:, None]
    grad_h = scale * back
    d_gate = (grad_h * up * sig * (1.0 + gate * (1.0 - sig))).astype(jnp.bfloat16)
    d_up = (grad_h * act).astype(jnp.bfloat16)
    scaled = (scale * hidden).astype(jnp.bfloat16)
    input_part = lax.dot_general(d_gate, w_gate, inner, preferred_element_type=jnp.float32)
    input_part = input_part + lax.dot_general(d_up, w_up, inner, preferred_element_type=jnp.float32)
    gate_sum = lax.dot_general(all_x, d_gate, outer, preferred_element_type=jnp.float32)
    up_sum = lax.dot_general(all_x, d_up, outer, preferred_element_type=jnp.float32)
    down_sum = lax.dot_general(scaled, all_dy, outer, preferred_element_type=jnp.float32)
    half_cols = gate_half.shape[2]
    mine_start = member * half_cols
    theirs_start = (1 - member) * half_cols

    def cols(matrix, start, axis):
        return lax.dynamic_slice_in_dim(matrix, start, half_cols, axis)

    give = (
        cols(gate_sum, theirs_start, 1).astype(jnp.bfloat16),
        cols(up_sum, theirs_start, 1).astype(jnp.bfloat16),
        cols(down_sum, theirs_start, 0).astype(jnp.bfloat16),
    )
    got = from_partner((give[0], give[1], give[2]), "tp", 0)
    gate_grad = (cols(gate_sum, mine_start, 1) + got[0].astype(jnp.float32)).astype(jnp.bfloat16)[
        None
    ]
    up_grad = (cols(up_sum, mine_start, 1) + got[1].astype(jnp.float32)).astype(jnp.bfloat16)[None]
    down_grad = (cols(down_sum, mine_start, 0) + got[2].astype(jnp.float32)).astype(jnp.bfloat16)[
        None
    ]
    input_sum, router_sum = (
        lax.psum_scatter(
            input_part.astype(jnp.bfloat16), "dp", scatter_dimension=0, tiled=True
        ).astype(jnp.float32),
        lax.psum_scatter(
            router_part.astype(jnp.bfloat16), "dp", scatter_dimension=0, tiled=True
        ).astype(jnp.float32),
    )
    own_w = rows_w.astype(jnp.float32)
    back_x = input_sum.astype(jnp.bfloat16)
    back_g = (router_sum * own_w * (1.0 - own_w)).astype(jnp.bfloat16)
    ship_x = back_x.reshape(HALF, n_dev, part_width)
    ship_g = jnp.broadcast_to(back_g.reshape(HALF, n_ctx, 1, 1), (HALF, n_ctx, n_tp, 1)).reshape(
        HALF, n_dev, 1
    )
    landed = (
        lax.all_to_all(ship_x, ("ctx", "tp"), split_axis=1, concat_axis=1, tiled=True),
        lax.all_to_all(ship_g, ("ctx", "tp"), split_axis=1, concat_axis=1, tiled=True),
    )
    flat_x = landed[0].reshape(slots, part_width)
    flat_g = landed[1].reshape(slots, 1)
    take = (place_out[:, None] == columns).astype(jnp.bfloat16)
    input_grad = jnp.dot(take, flat_x, preferred_element_type=jnp.float32).astype(jnp.bfloat16)
    logit_grad = jnp.dot(take, flat_g, preferred_element_type=jnp.float32)[:, 0].astype(
        jnp.bfloat16
    )
    return (input_grad, logit_grad, gate_grad, up_grad, down_grad)


def solution(mesh):
    in_specs = (
        P(("dp", "ctx"), "tp"),
        P(("dp", "ctx"), "tp"),
        P(("dp", "ctx")),
        P(("dp", "ctx"), None),
        P(("ctx", "tp"), None, "dp"),
        P(("ctx", "tp"), None, "dp"),
        P(("ctx", "tp"), "dp", None),
    )
    out_specs = (
        P(("dp", "ctx"), "tp"),
        P(("dp", "ctx")),
        P(("ctx", "tp"), None, "dp"),
        P(("ctx", "tp"), None, "dp"),
        P(("ctx", "tp"), "dp", None),
    )
    return jax.shard_map(body, mesh=mesh, in_specs=in_specs, out_specs=out_specs, check_vma=False)
```

profile of v0, /device:TPU:2, one launch (start us, length us, event | category | flops | bytes accessed | tf_op | source)
XLA Modules:
  0.0 306.1 jit_solution(11693822269275741734)
XLA Ops:
  7.2 0.8 fusion.24
  8.0 0.2 reduce_window_sum.11
  8.2 0.8 select_reduce_fusion
  9.0 0.7 fusion.36
  9.7 0.4 convolution_convert_fusion
  10.1 0.1 copy.31
  10.2 18.8 %all_to_all.37 = bf16[10,16,1280]{2,0,1:T(8,128)(2,1)S(1)} all-to-all(bf16[10,16,1280]{2,0,1:T(8,128)(2,1)S(1)} %copy.31), channel_id=1, replica_groups=mesh['dp'=16,'ctx'=4,'tp'=4] {'ctx','tp'}, dimensions={1} | all-to-all | bytes 819200 | tf_op jit(solution)/shard_map/all_to_all | solution.py:49
  29.1 0.1 copy.32
  29.2 1.0 reshape.125
  30.3 0.4 convolution_convert_fusion.1
  30.7 0.1 copy.29
  30.9 15.0 %all_to_all.38 = bf16[10,16,1280]{2,0,1:T(8,128)(2,1)S(1)} all-to-all(bf16[10,16,1280]{2,0,1:T(8,128)(2,1)S(1)} %copy.29), channel_id=1, replica_groups=mesh['dp'=16,'ctx'=4,'tp'=4] {'ctx','tp'}, dimensions={1} | all-to-all | bytes 819200 | tf_op jit(solution)/shard_map/all_to_all | solution.py:56
  45.9 0.1 copy.30
  46.0 1.0 reshape.123
  47.0 1.5 collective-permute-start.2
  48.6 0.6 collective-permute-start.1
  49.2 0.2 fusion.18
  49.4 0.1 reshape.120
  49.5 0.7 copy.27
  50.2 4.7 %all-to-all-start = ((bf16[10,16,1]{0,2,1:T(2,128)(2,1)}), bf16[10,16,1]{0,2,1:T(2,128)(2,1)S(1)}, u32[]{:S(2)}, u32[]{:S(2)}) async-start(bf16[10,16,1]{0,2,1:T(2,128)(2,1)} %copy.27), calls=%async_computation | async-start | bytes 16384 | tf_op jit(solution)/shard_map/all_to_all | solution.py:63
  54.9 0.3 collective-permute-start
  55.2 0.6 fusion.46
  56.5 51.2 %all-to-all-done = bf16[10,16,1]{0,2,1:T(2,128)(2,1)S(1)} async-done(((bf16[10,16,1]{0,2,1:T(2,128)(2,1)}), bf16[10,16,1]{0,2,1:T(2,128)(2,1)S(1)}, u32[]{:S(2)}, u32[]{:S(2)}) %all-to-all-start) | async-done | bytes 352 | tf_op jit(solution)/shard_map/all_to_all | solution.py:63
  107.6 0.1 copy.28
  107.7 0.1 reshape.129
  107.8 0.2 dynamic-update-slice
  108.1 7.0 %fusion.12 = f32[640,256]{0,1:T(8,128)} fusion(bf16[640,5120]{1,0:T(8,128)(2,1)} %all-gather.5.cloned.1.call-done, bf16[5120,128]{1,0:T(8,128)(2,1)} %collective-permute-done.2, bf16[5120,128]{1,0:T(8,128)(2,1)S(1)} %bitcast.75, pred[]{:T(512)S(6)} %eq.52), kind=kOutput, calls=%fused_computation.31 | convolution fusion | flops 1689518080 | bytes 9830401 | tf_op jit(solution)/shard_map/dot_general | solution.py:88
  115.1 4.1 %fusion.14 = f32[640,256]{0,1:T(8,128)S(1)} fusion(bf16[640,5120]{1,0:T(8,128)(2,1)S(1)} %copy-done.2, bf16[5120,128]{1,0:T(8,128)(2,1)} %collective-permute-done.1, bf16[5120,128]{1,0:T(8,128)(2,1)S(1)} %bitcast.72, pred[]{:T(512)S(6)} %eq.52), kind=kOutput, calls=%fused_computation.33 | convolution fusion | flops 1689518080 | bytes 9830401 | tf_op jit(solution)/shard_map/dot_general | solution.py:89
  119.2 12.4 %collective-permute-done = bf16[128,5120]{1,0:T(8,128)(2,1)} collective-permute-done((bf16[128,5120]{1,0:T(8,128)(2,1)}, bf16[128,5120]{1,0:T(8,128)(2,1)}, u32[]{:S(2)}, u32[]{:S(2)}) %collective-permute-start) | collective-permute-done | bytes 1310752 | tf_op jit(solution)/shard_map/ppermute | solution.py:16
  131.7 7.6 %multiply_reduce_fusion = (bf16[640]{0:T(1024)(128)(2,1)S(1)}, f32[640,256]{0,1:T(8,128)}) fusion(f32[640,256]{0,1:T(8,128)S(1)} %fusion.14, f32[640,256]{0,1:T(8,128)S(1)} %copy-done.10, bf16[640,5120]{1,0:T(8,128)(2,1)} %all-gather.3.cloned.1.call-done, bf16[128,5120]{1,0:T(8,128)(2,1)} %collective-permute-done, bf16[128,5120]{1,0:T(8,128)(2,1)} %bitcast.82, ...), kind=kOutput, calls=%fused_computation.26 | convolution fusion | flops 1690664320 | bytes 11142401 | tf_op jit(solution)/shard_map/dot_general | solution.py:93
  139.2 26.3 %all-reduce.2 = (bf16[640]{0:T(1024)(128)(2,1)S(1)}, bf16[640]{0:T(1024)(128)(2,1)S(1)}) all-reduce(bf16[640]{0:T(1024)(128)(2,1)S(1)} %dynamic-update-slice, bf16[640]{0:T(1024)(128)(2,1)S(1)} %get-tuple-element.11), channel_id=1, replica_groups=mesh['dp'=16,'ctx'=4,'tp'=4] {'dp'}, use_global_device_ids=true, to_apply=%add | all-reduce | flops 1280 | bytes 5120
  165.5 1.8 multiply_convert_fusion.2
  167.4 8.5 %fusion.13 = f32[640,5120]{1,0:T(8,128)} fusion(bf16[640,256]{0,1:T(8,128)(2,1)S(1)} %get-tuple-element.8, bf16[5120,128]{1,0:T(8,128)(2,1)} %collective-permute-done.1, bf16[5120,128]{1,0:T(8,128)(2,1)S(1)} %bitcast.73, pred[]{:T(512)S(6)} %eq.52), kind=kOutput, calls=%fused_computation.32 | convolution fusion | flops 1689518080 | bytes 16056321 | tf_op jit(solution)/shard_map/dot_general | solution.py:101
  175.8 10.2 %add_convert_fusion = bf16[640,5120]{1,0:T(8,128)(2,1)} fusion(f32[640,5120]{1,0:T(8,128)} %fusion.13, bf16[640,256]{0,1:T(8,128)(2,1)S(1)} %get-tuple-element.7, bf16[5120,128]{1,0:T(8,128)(2,1)} %collective-permute-done.2, bf16[5120,128]{1,0:T(8,128)(2,1)S(1)} %bitcast.76, pred[]{:T(512)S(6)} %eq.52), kind=kOutput, calls=%fused_computation | convolution fusion | flops 1696071680 | bytes 22609920 | tf_op jit(solution)/shard_map/dot_general | solution.py:100
  186.8 0.1 fusion.37
  186.8 0.1 broadcast_in_dim.24
  186.9 0.1 copy.35
  187.1 0.6 copy.36
  187.7 4.8 %all-to-all-start.4 = ((bf16[10,16,1]{0,2,1:T(2,128)(2,1)}), bf16[10,16,1]{0,2,1:T(2,128)(2,1)S(1)}, u32[]{:S(2)}, u32[]{:S(2)}) async-start(bf16[10,16,1]{0,2,1:T(2,128)(2,1)} %copy.36), calls=%async_computation.5 | async-start | bytes 16384 | tf_op jit(solution)/shard_map/all_to_all | solution.py:142
  192.5 5.9 %fusion.15 = f32[256,5120]{1,0:T(8,128)S(1)} fusion(bf16[640,5120]{1,0:T(8,128)(2,1)} %all-gather.3.cloned.1.call-done, f32[640]{0:T(1024)S(1)} %convert_element_type.83, f32[640,256]{0,1:T(8,128)} %copy-done.11, f32[640,256]{0,1:T(8,128)} %fusion.12), kind=kOutput, calls=%fused_computation.34 | convolution fusion | flops 1678868480 | bytes 13109760 | tf_op jit(solution)/shard_map/dot_general | solution.py:104
  198.4 1.4 dynamic-slice_convert_fusion
  199.8 1.4 copy-done.6
  201.2 2.3 fusion.48
  203.6 1.4 dynamic-slice_convert_fusion.1
  205.0 2.3 fusion.47
  207.4 0.2 dynamic-slice_convert_fusion.2
  207.6 2.1 copy-done.4
  209.7 2.0 collective-permute-start.3
  211.7 0.1 collective-permute-start.4
  211.7 0.1 copy.37
  211.8 0.1 reshape.136
  211.9 0.8 fusion.10
  212.7 20.5 %collective-permute-done.5 = bf16[128,5120]{1,0:T(8,128)(2,1)} collective-permute-done((bf16[128,5120]{1,0:T(8,128)(2,1)}, bf16[128,5120]{1,0:T(8,128)(2,1)}, u32[]{:S(2)}, u32[]{:S(2)}) %collective-permute-start.5) | collective-permute-done | bytes 1310752 | tf_op jit(solution)/shard_map/ppermute | solution.py:16
  233.1 3.5 %fusion.9 = bf16[1,128,5120]{2,1,0:T(8,128)(2,1)} fusion(bf16[128,5120]{1,0:T(8,128)(2,1)} %collective-permute-done.5, f32[256,5120]{1,0:T(8,128)} %copy-done.6, s32[]{:T(128)S(6)} %select_n.70), kind=kLoop, calls=%fused_computation.22 | loop fusion | flops 1966080 | bytes 5242884 | tf_op jit(solution)/shard_map/broadcast_in_dim | solution.py:122
  236.6 24.6 %collective-permute-done.3 = bf16[5120,128]{1,0:T(8,128)(2,1)} collective-permute-done((bf16[5120,128]{1,0:T(8,128)(2,1)S(1)}, bf16[5120,128]{1,0:T(8,128)(2,1)}, u32[]{:S(2)}, u32[]{:S(2)}) %collective-permute-start.3) | collective-permute-done | bytes 1310752 | tf_op jit(solution)/shard_map/ppermute | solution.py:16
  261.2 2.7 fusion.7
  263.9 1.3 reshape.126
  265.2 1.0 copy.33
  266.2 7.2 %all-to-all-start.3 = ((bf16[10,16,1280]{2,0,1:T(8,128)(2,1)}), bf16[10,16,1280]{2,0,1:T(8,128)(2,1)S(1)}, u32[]{:S(2)}, u32[]{:S(2)}) async-start(bf16[10,16,1280]{2,0,1:T(8,128)(2,1)} %copy.33), calls=%async_computation.4 | async-start | bytes 1310720 | tf_op jit(solution)/shard_map/all_to_all | solution.py:141
  273.4 15.8 %collective-permute-done.4 = bf16[5120,128]{1,0:T(8,128)(2,1)S(1)} collective-permute-done((bf16[5120,128]{1,0:T(8,128)(2,1)}, bf16[5120,128]{1,0:T(8,128)(2,1)S(1)}, u32[]{:S(2)}, u32[]{:S(2)}) %collective-permute-start.4) | collective-permute-done | bytes 1310752 | tf_op jit(solution)/shard_map/ppermute | solution.py:16
  289.2 3.1 fusion.8
  292.2 6.2 %all-to-all-done.3 = bf16[10,16,1280]{2,0,1:T(8,128)(2,1)S(1)} async-done(((bf16[10,16,1280]{2,0,1:T(8,128)(2,1)}), bf16[10,16,1280]{2,0,1:T(8,128)(2,1)S(1)}, u32[]{:S(2)}, u32[]{:S(2)}) %all-to-all-start.3) | async-done | bytes 409632 | tf_op jit(solution)/shard_map/all_to_all | solution.py:141
  298.4 0.1 copy.34
  298.5 1.0 convolution_convert_fusion.2
  (52 shorter events, 0.4 us)
Async XLA Ops:
  7.2 2.5 copy-start
  7.2 100.9 %all-gather.5.cloned.1.call-start = ((), (), s32[]{:S(2)}) async-start(), calls=%async_computation.7 | async-start | bytes 6963200 | tf_op jit(solution)/shard_map/all_gather | solution.py:73
  10.1 20.3 %copy-start.12 = (bf16[128,1280]{1,0:T(8,128)(2,1)S(1)}, bf16[128,1280]{1,0:T(8,128)(2,1)}, u32[]{:S(2)}) copy-start(bf16[128,1280]{1,0:T(8,128)(2,1)} %param.8) | copy-start | bytes 983044
  30.2 16.8 %copy-start.8 = (bf16[1,5120,128]{2,1,0:T(8,128)(2,1)S(1)}, bf16[1,5120,128]{2,1,0:T(8,128)(2,1)}, u32[]{:S(2)}) copy-start(bf16[1,5120,128]{2,1,0:T(8,128)(2,1)} %param.11) | copy-start | bytes 3932164
  30.3 18.3 %copy-start.7 = (bf16[1,5120,128]{2,1,0:T(8,128)(2,1)S(1)}, bf16[1,5120,128]{2,1,0:T(8,128)(2,1)}, u32[]{:S(2)}) copy-start(bf16[1,5120,128]{2,1,0:T(8,128)(2,1)} %param.12) | copy-start | bytes 3932164
  30.3 18.9 %copy-start.14 = (f32[128]{0:T(128)S(1)}, f32[128]{0:T(128)}, u32[]{:S(2)}) copy-start(f32[128]{0:T(128)} %param.9) | copy-start | bytes 1540
  30.3 25.0 %copy-start.13 = (u32[256]{0:T(256)S(1)}, u32[256]{0:T(256)}, u32[]{:S(2)}) copy-start(u32[256]{0:T(256)} %constant.59) | copy-start | bytes 3076
  30.3 101.4 %all-gather.3.cloned.1.call-start = ((), (), s32[]{:S(2)}) async-start(), calls=%async_computation.6 | async-start | bytes 6963200 | tf_op jit(solution)/shard_map/all_gather | solution.py:74
  47.0 61.1 %collective-permute-start.2 = (bf16[5120,128]{1,0:T(8,128)(2,1)S(1)}, bf16[5120,128]{1,0:T(8,128)(2,1)}, u32[]{:S(2)}, u32[]{:S(2)}) collective-permute-start(bf16[5120,128]{1,0:T(8,128)(2,1)S(1)} %bitcast.74), channel_id=1, source_target_pairs={{0,1},{1,0},{2,3},{3,2},{4,5},{5,4},{6,7},{7,6},{8,9},{9,8},{10,11... | collective-permute-start | bytes 3932168 | tf_op jit(solution)/shard_map/ppermute | solution.py:16
  48.6 66.5 %collective-permute-start.1 = (bf16[5120,128]{1,0:T(8,128)(2,1)S(1)}, bf16[5120,128]{1,0:T(8,128)(2,1)}, u32[]{:S(2)}, u32[]{:S(2)}) collective-permute-start(bf16[5120,128]{1,0:T(8,128)(2,1)S(1)} %bitcast.71), channel_id=1, source_target_pairs={{0,1},{1,0},{2,3},{3,2},{4,5},{5,4},{6,7},{7,6},{8,9},{9,8},{10,11... | collective-permute-start | bytes 3932168 | tf_op jit(solution)/shard_map/ppermute | solution.py:16
  50.2 57.5 %all-to-all-start = ((bf16[10,16,1]{0,2,1:T(2,128)(2,1)}), bf16[10,16,1]{0,2,1:T(2,128)(2,1)S(1)}, u32[]{:S(2)}, u32[]{:S(2)}) async-start(bf16[10,16,1]{0,2,1:T(2,128)(2,1)} %copy.27), calls=%async_computation | async-start | bytes 16384 | tf_op jit(solution)/shard_map/all_to_all | solution.py:63
  54.9 209.0 %reduce-scatter.2.cloned.1.call-start = ((), (), s32[]{:S(2)}) async-start(), calls=%async_computation.8 | async-start | bytes 6963200 | tf_op jit(solution)/shard_map/reduce_scatter | solution.py:126
  54.9 76.7 %collective-permute-start = (bf16[128,5120]{1,0:T(8,128)(2,1)}, bf16[128,5120]{1,0:T(8,128)(2,1)}, u32[]{:S(2)}, u32[]{:S(2)}) collective-permute-start(bf16[128,5120]{1,0:T(8,128)(2,1)} %bitcast.81), channel_id=1, source_target_pairs={{0,1},{1,0},{2,3},{3,2},{4,5},{5,4},{6,7},{7,6},{8,9},{9,8},{10,11... | collective-permute-start | bytes 3932168 | tf_op jit(solution)/shard_map/ppermute | solution.py:16
  108.1 7.0 %copy-start.2 = (bf16[640,5120]{1,0:T(8,128)(2,1)S(1)}, bf16[640,5120]{1,0:T(8,128)(2,1)}, u32[]{:S(2)}) copy-start(bf16[640,5120]{1,0:T(8,128)(2,1)} %all-gather.5.cloned.1.call-done) | copy-start | bytes 19660804
  115.1 16.6 %copy-start.10 = (f32[640,256]{0,1:T(8,128)S(1)}, f32[640,256]{0,1:T(8,128)}, u32[]{:S(2)}) copy-start(f32[640,256]{0,1:T(8,128)} %fusion.12) | copy-start | bytes 1966084
  119.2 20.0 %copy-start.11 = (f32[640,256]{0,1:T(8,128)}, f32[640,256]{0,1:T(8,128)S(1)}, u32[]{:S(2)}) copy-start(f32[640,256]{0,1:T(8,128)S(1)} %fusion.14) | copy-start | bytes 1966084
  167.4 8.5 %copy-start.9 = (bf16[1,5120,128]{2,1,0:T(8,128)(2,1)S(1)}, bf16[1,5120,128]{2,1,0:T(8,128)(2,1)}, u32[]{:S(2)}) copy-start(bf16[1,5120,128]{2,1,0:T(8,128)(2,1)} %param.11) | copy-start | bytes 3932164
  187.7 13.6 %slice-start = ((s8[6553600]{0:T(1024)(128)(4,1)}), s8[2359296]{0:T(1024)(128)(4,1)S(1)}, s32[]{:S(2)}) async-start(s8[6553600]{0:T(1024)(128)(4,1)} %bitcast.66), calls=%async_computation.9 | async-start | bytes 4718592
  187.7 24.1 %all-to-all-start.4 = ((bf16[10,16,1]{0,2,1:T(2,128)(2,1)}), bf16[10,16,1]{0,2,1:T(2,128)(2,1)S(1)}, u32[]{:S(2)}, u32[]{:S(2)}) async-start(bf16[10,16,1]{0,2,1:T(2,128)(2,1)} %copy.36), calls=%async_computation.5 | async-start | bytes 16384 | tf_op jit(solution)/shard_map/all_to_all | solution.py:142
  192.5 8.8 %slice-start.1 = ((s8[6553600]{0:T(1024)(128)(4,1)}), s8[4194304]{0:T(1024)(128)(4,1)S(1)}, s32[]{:S(2)}) async-start(s8[6553600]{0:T(1024)(128)(4,1)} %bitcast.66), calls=%async_computation.10 | async-start | bytes 8388608
  198.4 2.8 copy-start.6
  201.2 32.0 %collective-permute-start.5 = (bf16[128,5120]{1,0:T(8,128)(2,1)}, bf16[128,5120]{1,0:T(8,128)(2,1)}, u32[]{:S(2)}, u32[]{:S(2)}) collective-permute-start(bf16[128,5120]{1,0:T(8,128)(2,1)} %dynamic-slice_convert_fusion), channel_id=1, source_target_pairs={{0,1},{1,0},{2,3},{3,2},{4,5},{5,4},{6,7},{7,6},{8,9},{9,8},{10,11... | collective-permute-start | bytes 3932168 | tf_op jit(solution)/shard_map/ppermute | solution.py:16
  203.6 3.8 %copy-start.3 = (f32[5120,256]{1,0:T(8,128)}, f32[5120,256]{1,0:T(8,128)S(1)}, u32[]{:S(2)}) copy-start(f32[5120,256]{1,0:T(8,128)S(1)} %fusion.48) | copy-start | bytes 15728644
  207.4 2.3 copy-start.4
  209.7 51.5 %collective-permute-start.3 = (bf16[5120,128]{1,0:T(8,128)(2,1)S(1)}, bf16[5120,128]{1,0:T(8,128)(2,1)}, u32[]{:S(2)}, u32[]{:S(2)}) collective-permute-start(bf16[5120,128]{1,0:T(8,128)(2,1)S(1)} %dynamic-slice_convert_fusion.2), channel_id=1, source_target_pairs={{0,1},{1,0},{2,3},{3,2},{4,5},{5,4},{6,7},{7,6},{8,9},{9,8},{10,11... | collective-permute-start | bytes 3932168 | tf_op jit(solution)/shard_map/ppermute | solution.py:16
  211.7 77.5 %collective-permute-start.4 = (bf16[5120,128]{1,0:T(8,128)(2,1)}, bf16[5120,128]{1,0:T(8,128)(2,1)S(1)}, u32[]{:S(2)}, u32[]{:S(2)}) collective-permute-start(bf16[5120,128]{1,0:T(8,128)(2,1)} %dynamic-slice_convert_fusion.1), channel_id=1, source_target_pairs={{0,1},{1,0},{2,3},{3,2},{4,5},{5,4},{6,7},{7,6},{8,9},{9,8},{10,11... | collective-permute-start | bytes 3932168 | tf_op jit(solution)/shard_map/ppermute | solution.py:16
  212.6 48.6 %copy-start.5 = (f32[5120,256]{1,0:T(8,128)S(1)}, f32[5120,256]{1,0:T(8,128)}, u32[]{:S(2)}) copy-start(f32[5120,256]{1,0:T(8,128)} %copy-done.4) | copy-start | bytes 15728644
  266.2 32.2 %all-to-all-start.3 = ((bf16[10,16,1280]{2,0,1:T(8,128)(2,1)}), bf16[10,16,1280]{2,0,1:T(8,128)(2,1)S(1)}, u32[]{:S(2)}, u32[]{:S(2)}) async-start(bf16[10,16,1280]{2,0,1:T(8,128)(2,1)} %copy.33), calls=%async_computation.4 | async-start | bytes 1310720 | tf_op jit(solution)/shard_map/all_to_all | solution.py:141
  273.4 26.2 %copy-start.1 = (bf16[128,1280]{1,0:T(8,128)(2,1)S(1)}, bf16[128,1280]{1,0:T(8,128)(2,1)}, u32[]{:S(2)}) copy-start(bf16[128,1280]{1,0:T(8,128)(2,1)} %param.7) | copy-start | bytes 983044
Sparse Core Ops, SparseCore 0:
  30.4 47.3 all-gather.4
  80.2 45.8 all-gather.2
  186.2 64.5 reduce-scatter.1
where the time goes:
time: 308 us; the launch traced here: 306 us
  waiting for transfers between devices  131 us (43%)
  blocking collectives  60.1 us (20%)
  matrix products  50.7 us (16%)
  starting transfers between devices  21.4 us (7%)
  between operations  15.3 us (5%)
  local copies, waits for them, and re-layouts  14.3 us (5%)
  other arithmetic  13.6 us (4%)
    ppermute x6, waiting for transfers between devices, from_partner(): return lax.ppermute(block, axis, route)  73.4 us
    all_to_all x1, waiting for transfers between devices, body(): lax.all_to_all(send_w.reshape(HALF, n_dev, 1), ('ctx', 'tp'), split_axis=...  51.2 us
    unnamed x1, blocking collectives  26.3 us
    all_to_all x1, blocking collectives, body(): lax.all_to_all(send_x.reshape(HALF, n_dev, part_width), ('ctx', 'tp'), sp...  18.8 us
    all_to_all x1, blocking collectives, body(): lax.all_to_all(send_dy.reshape(HALF, n_dev, part_width), ('ctx', 'tp'), s...  15 us
    dot_general x1, matrix products, body(): lax.dot_general(d_gate, w_gate, inner, preferred_element_type=jnp.float32)  10.2 us
    dot_general x1, matrix products, body(): lax.dot_general(d_up, w_up, inner, preferred_element_type=jnp.float32)  8.46 us
    dot_general x1, matrix products, body(): lax.dot_general(all_dy, w_down, inner, preferred_element_type=jnp.float32)  7.59 us
  transfers between devices with their start and end apart: 12, of which 6 were waited for; matrix products, arithmetic and copies ran while one was open for 14% of the time, Pallas kernels for 0%

commit v1 on v0

v1 whole, which is shorter than its diff:
```python
import jax
import jax.numpy as jnp
from jax import lax
from jax.experimental import pallas as pl
from jax.experimental.pallas import tpu as pltpu
from jax.sharding import Mesh, PartitionSpec as P

HALF = 10
LANES = 128
BLOCK = 512
INNER = (((1,), (1,)), ((), ()))
OUTER = (((0,), (0,)), ((), ()))
F32 = jnp.float32
BF16 = jnp.bfloat16


def params():
    return pltpu.CompilerParams(vmem_limit_bytes=40 << 20)


def cost(flops, moved):
    return pl.CostEstimate(flops=int(flops), bytes_accessed=int(moved), transcendentals=0)


def hidden_kernel(x_ref, dy_ref, g0, g1, u0, u1, d0, d1, d_ref, s_ref, r_ref, gate_a, up_a, back_a):
    step = pl.program_id(0)

    @pl.when(step == 0)
    def _():
        gate_a[...] = jnp.zeros_like(gate_a)
        up_a[...] = jnp.zeros_like(up_a)
        back_a[...] = jnp.zeros_like(back_a)

    x = x_ref[...]
    dy = dy_ref[...]
    w_gate = jnp.concatenate([g0[...], g1[...]], 1)
    w_up = jnp.concatenate([u0[...], u1[...]], 1)
    w_down = jnp.concatenate([d0[...], d1[...]], 0)
    gate_a[...] += jnp.dot(x, w_gate, preferred_element_type=F32)
    up_a[...] += jnp.dot(x, w_up, preferred_element_type=F32)
    back_a[...] += lax.dot_general(dy, w_down, INNER, preferred_element_type=F32)

    @pl.when(step == pl.num_programs(0) - 1)
    def _():
        gate = gate_a[...]
        up = up_a[...]
        back = back_a[...]
        sig = jax.nn.sigmoid(gate)
        act = gate * sig
        hidden = act * up
        d_gate = (back * up * sig * (1.0 + gate * (1.0 - sig))).astype(BF16)
        d_up = (back * act).astype(BF16)
        half = gate.shape[1] // 2
        d_ref[:, :half] = d_gate[:, :half]
        d_ref[:, half : 2 * half] = d_up[:, :half]
        d_ref[:, 2 * half : 3 * half] = d_gate[:, half:]
        d_ref[:, 3 * half :] = d_up[:, half:]
        s_ref[...] = hidden.astype(BF16)
        total = jnp.sum(hidden * back, axis=1, keepdims=True)
        r_ref[...] = jnp.broadcast_to(total, r_ref.shape).astype(BF16)


def hidden_part(both, own, other):
    rows, wide = both.shape
    width = wide // 2
    half = own[0].shape[1]
    steps = width // BLOCK
    whole = lambda i: (0, 0)
    tall = pl.BlockSpec((BLOCK, half), lambda i: (i, 0))
    flat = pl.BlockSpec((half, BLOCK), lambda i: (0, i))
    return pl.pallas_call(
        hidden_kernel,
        grid=(steps,),
        in_specs=[
            pl.BlockSpec((rows, BLOCK), lambda i: (0, i)),
            pl.BlockSpec((rows, BLOCK), lambda i: (0, i + steps)),
            tall,
            tall,
            tall,
            tall,
            flat,
            flat,
        ],
        out_specs=[
            pl.BlockSpec((rows, 4 * half), whole),
            pl.BlockSpec((rows, 2 * half), whole),
            pl.BlockSpec((rows, LANES), whole),
        ],
        out_shape=[
            jax.ShapeDtypeStruct((rows, 4 * half), BF16),
            jax.ShapeDtypeStruct((rows, 2 * half), BF16),
            jax.ShapeDtypeStruct((rows, LANES), BF16),
        ],
        scratch_shapes=[pltpu.VMEM((rows, 2 * half), F32)] * 3,
        compiler_params=params(),
        cost_estimate=cost(12 * rows * width * half, 4 * rows * width),
        name="hidden_part",
    )(both, both, own[0], other[0], own[1], other[1], own[2], other[2])


def input_kernel(with_add, d_ref, r_ref, g0, u0, g1, u1, *rest):
    out_ref = rest[-1]
    step = pl.program_id(0)
    last = pl.num_programs(0) - 1

    @pl.when(step < last)
    def _():
        weights = jnp.concatenate([g0[...], u0[...], g1[...], u1[...]], 1)
        part = lax.dot_general(d_ref[...], weights, INNER, preferred_element_type=F32)
        if with_add:
            part = part + rest[0][...].astype(F32)
        out_ref[...] = part.astype(BF16)

    @pl.when(step == last)
    def _():
        part = r_ref[...].astype(F32)
        if with_add:
            part = part + rest[0][:, :LANES].astype(F32)
        out_ref[:, :LANES] = part.astype(BF16)


def input_part(d, router, own, other, addend=None):
    rows = d.shape[0]
    width, half = own[0].shape
    block = 1024
    steps = width // block
    whole = lambda i: (0, 0)
    tall = pl.BlockSpec((block, half), lambda i: (jnp.minimum(i, steps - 1), 0))
    strip = pl.BlockSpec((rows, block), lambda i: (0, i))
    operands = [d, router, own[0], own[1], other[0], other[1]]
    specs = [pl.BlockSpec((rows, 4 * half), whole), pl.BlockSpec((rows, LANES), whole)] + [tall] * 4
    if addend is not None:
        operands.append(addend)
        specs.append(strip)
    return pl.pallas_call(
        lambda *refs: input_kernel(addend is not None, *refs),
        grid=(steps + 1,),
        in_specs=specs,
        out_specs=strip,
        out_shape=jax.ShapeDtypeStruct((rows, width + LANES), BF16),
        compiler_params=params(),
        cost_estimate=cost(8 * rows * width * half, 2 * rows * width + 8 * width * half),
        name="input_part",
    )(*operands)


def weight_kernel(x_ref, dy_ref, d_ref, s_ref, gate_ref, up_ref, down_ref):
    half = gate_ref.shape[1]
    both = lax.dot_general(x_ref[...], d_ref[...], OUTER, preferred_element_type=F32)
    gate_ref[...] = both[:, :half].astype(gate_ref.dtype)
    up_ref[...] = both[:, half:].astype(up_ref.dtype)
    down = lax.dot_general(s_ref[...], dy_ref[...], OUTER, preferred_element_type=F32)
    down_ref[...] = down.astype(down_ref.dtype)


def weight_part(both, d, scaled, which, dtype):
    rows, wide = both.shape
    width = wide // 2
    half = scaled.shape[1] // 2
    steps = width // BLOCK
    tall = pl.BlockSpec((BLOCK, half), lambda i: (i, 0))
    return pl.pallas_call(
        weight_kernel,
        grid=(steps,),
        in_specs=[
            pl.BlockSpec((rows, BLOCK), lambda i: (0, i)),
            pl.BlockSpec((rows, BLOCK), lambda i: (0, i + steps)),
            pl.BlockSpec((rows, 2 * half), lambda i: (0, which)),
            pl.BlockSpec((rows, half), lambda i: (0, which)),
        ],
        out_specs=[tall, tall, pl.BlockSpec((half, BLOCK), lambda i: (0, i))],
        out_shape=[
            jax.ShapeDtypeStruct((width, half), dtype),
            jax.ShapeDtypeStruct((width, half), dtype),
            jax.ShapeDtypeStruct((half, width), dtype),
        ],
        compiler_params=params(),
        cost_estimate=cost(6 * rows * width * half, 4 * rows * width),
        name="weight_part",
    )(both, both, d, scaled)


def flip(value, axis):
    count = lax.axis_size(axis)
    return lax.ppermute(value, axis, [(i, i ^ 1) for i in range(count)])


def body(tokens_in, grad_out, router_logit, expert_index, gate_half, up_half, down_half):
    n_z = lax.axis_size("z")
    n_core = lax.axis_size("core")
    n_ctx = lax.axis_size("ctx")
    n_tp = lax.axis_size("tp")
    n_dev = n_ctx * n_tp
    n_exp = n_dev // 2
    tok_rows, part_width = tokens_in.shape
    width = part_width * n_tp
    slots = n_dev * HALF
    held = n_ctx * HALF
    route = expert_index[:, 0]
    hit = (route[:, None] == jnp.arange(n_exp, dtype=jnp.int32)[None, :]).astype(jnp.int32)
    before = jnp.cumsum(hit, axis=0) - hit
    rank = jnp.sum(before * hit, axis=1)
    target = 2 * route + rank // HALF
    place = target * HALF + rank % HALF
    weight = jax.nn.sigmoid(router_logit).astype(BF16).astype(F32)
    columns = jnp.arange(slots, dtype=jnp.int32)[None, :]
    pick = (place[:, None] == columns).astype(BF16)
    scaled_dy = (grad_out.astype(F32) * weight[:, None]).astype(BF16)
    send = lax.dot_general(
        pick,
        jnp.concatenate([tokens_in, scaled_dy], 1),
        OUTER,
        preferred_element_type=F32,
    ).astype(BF16)
    recv = lax.all_to_all(send, ("ctx", "tp"), split_axis=0, concat_axis=0, tiled=True)
    mine = (
        recv.reshape(n_ctx, n_tp, HALF, 2, part_width)
        .transpose(0, 2, 3, 1, 4)
        .reshape(held, 2 * width)
    )
    own = (gate_half[0], up_half[0], down_half[0])
    held_own = lax.optimization_barrier((own, recv))[0]
    other = tuple(flip(w, "tp") for w in held_own)
    both = lax.all_gather(mine, ("z", "core"), axis=0, tiled=True)
    d, scaled, router = hidden_part(both, own, other)
    give = weight_part(both, d, scaled, 1, BF16)
    got = tuple(flip(g, "tp") for g in give)
    core = lax.axis_index("core")

    def by_core(values):
        parts = values.reshape(n_z, n_core, held, values.shape[1])
        pick_core = lambda c: lax.dynamic_index_in_dim(parts, c, 1, False).reshape(
            n_z * held, values.shape[1]
        )
        return pick_core(core), pick_core(1 - core)

    d_in, _ = lax.optimization_barrier((d, give[0]))
    d_own, d_oth = by_core(d_in)
    r_own, r_oth = by_core(router)
    part_oth = input_part(d_oth, r_oth, own, other)
    from_core = flip(part_oth, "core")
    part = input_part(d_own, r_own, own, other, from_core)
    d_keep, _ = lax.optimization_barrier((d, part))
    keep = weight_part(both, d_keep, scaled, 0, F32)
    summed = lax.optimization_barrier(
        lax.psum_scatter(part, "z", scatter_dimension=0, tiled=True)
    )
    back_x = summed[:, :width].reshape(n_ctx, HALF, n_tp, part_width).transpose(0, 2, 1, 3)
    back_r = jnp.broadcast_to(
        summed[:, width:].reshape(n_ctx, 1, HALF, LANES), (n_ctx, n_tp, HALF, LANES)
    )
    ship = jnp.concatenate([back_x, back_r], 3).reshape(slots, part_width + LANES)
    landed = lax.all_to_all(ship, ("ctx", "tp"), split_axis=0, concat_axis=0, tiled=True)
    home = jnp.dot(pick, landed, preferred_element_type=F32)
    input_grad = home[:, :part_width].astype(BF16)
    logit_grad = (home[:, part_width] * (1.0 - weight)).astype(BF16)
    grads = tuple((k + g.astype(F32)).astype(BF16)[None] for k, g in zip(keep, got))
    return (input_grad, logit_grad) + grads


def solution(mesh):
    n_dp = mesh.shape["dp"]
    fine = Mesh(
        mesh.devices.reshape(n_dp // 2, 2, mesh.shape["ctx"], mesh.shape["tp"]),
        ("z", "core", "ctx", "tp"),
    )
    dp = ("z", "core")
    token = dp + ("ctx",)
    in_specs = (
        P(token, "tp"),
        P(token, "tp"),
        P(token),
        P(token, None),
        P(("ctx", "tp"), None, dp),
        P(("ctx", "tp"), None, dp),
        P(("ctx", "tp"), dp, None),
    )
    out_specs = (
        P(token, "tp"),
        P(token),
        P(("ctx", "tp"), None, dp),
        P(("ctx", "tp"), None, dp),
        P(("ctx", "tp"), dp, None),
    )
    return jax.shard_map(body, mesh=fine, in_specs=in_specs, out_specs=out_specs, check_vma=False)
```

time: 308 us -> 278 us (0.903)
  matrix products: 50.7 us -> 1.76 us
  Pallas kernels: 0 us -> 45.2 us
  blocking collectives: 60.1 us -> 25.9 us
  waiting for transfers between devices: 131 us -> 154 us
  starting transfers between devices: 21.4 us -> 12.4 us
  other arithmetic: 13.6 us -> 10.2 us
  local copies, waits for them, and re-layouts: 14.3 us -> 11.1 us
    ppermute x6 -> x7, waiting for transfers between devices: 73.4 us -> 150 us  [flip(): return lax.ppermute(value, axis, [(i, i ^ 1) for i in range(count)])]
    all_to_all x3 -> x1, waiting for transfers between devices: 57.3 us -> 4.09 us  [body(): lax.all_to_all(ship, ('ctx', 'tp'), split_axis=0, concat_axis=0, tiled=True)]
    dot_general x13 -> x2, matrix products: 50.7 us -> 1.76 us  [the longest x1 1.45 us: body(): lax.dot_general(pick, jnp.concatenate([tokens_in, scaled_dy], 1), OUTER,...]
    pallas_call x0 -> x5, Pallas kernels: none -> 45.2 us  [the longest x2 21.8 us: weight_part(): pl.pallas_call(weight_kernel, grid=(steps,), in_specs=[pl.BlockSpec((rows...]
    unnamed x1 -> x0, blocking collectives: 26.3 us -> none
    all_to_all x3 -> x1, starting transfers between devices: 16.7 us -> 5 us  [body(): lax.all_to_all(ship, ('ctx', 'tp'), split_axis=0, concat_axis=0, tiled=True)]
    all_to_all x2 -> x1, blocking collectives: 33.8 us -> 25.9 us  [body(): lax.all_to_all(send, ('ctx', 'tp'), split_axis=0, concat_axis=0, tiled=True)]
    broadcast_in_dim x3, other arithmetic: 9.23 us -> 5.25 us  [body(): (k + g.astype(F32)).astype(BF16)[None]]
  transfers between devices with their start and end apart: 12 -> 10, of which waited for: 6 -> 8; matrix products, arithmetic and copies ran while one was open for 14% -> 3% of each run, Pallas kernels for 0% -> 4%
where the time goes in v1:
time: 278 us; the launch traced here: 275 us
  waiting for transfers between devices  154 us (55%)
  Pallas kernels  45.2 us (16%)
  blocking collectives  25.9 us (9%)
  between operations  14.2 us (5%)
  starting transfers between devices  12.4 us (4%)
  local copies, waits for them, and re-layouts  11.1 us (4%)
  other arithmetic  10.2 us (4%)
    ppermute x7, waiting for transfers between devices, flip(): return lax.ppermute(value, axis, [(i, i ^ 1) for i in range(count)])  150 us
    all_to_all x1, blocking collectives, body(): lax.all_to_all(send, ('ctx', 'tp'), split_axis=0, concat_axis=0, tiled=True)  25.9 us
    pallas_call x2, Pallas kernels, weight_part(): pl.pallas_call(weight_kernel, grid=(steps,), in_specs=[pl.BlockSpec((rows...  21.8 us
    pallas_call x1, Pallas kernels, hidden_part(): pl.pallas_call(hidden_kernel, grid=(steps,), in_specs=[pl.BlockSpec((rows...  12.2 us
    pallas_call x2, Pallas kernels, input_part(): pl.pallas_call(lambda *refs: input_kernel(addend is not None, *refs), gri...  11.3 us
    ppermute x7, starting transfers between devices, flip(): return lax.ppermute(value, axis, [(i, i ^ 1) for i in range(count)])  7.3 us
  transfers between devices with their start and end apart: 10, of which 8 were waited for; matrix products, arithmetic and copies ran while one was open for 3% of the time, Pallas kernels for 4%

profile of v1, /device:TPU:2, one launch (start us, length us, event | category | flops | bytes accessed | tf_op | source)
XLA Modules:
  0.0 275.2 jit_solution(17255553070214660286)
XLA Ops:
  7.2 0.0 all-gather.2.cloned.1.call-start
  7.2 0.7 convert_convert_fusion
  7.9 0.7 fusion.9
  8.6 0.2 reduce_window_sum.11
  8.8 0.8 select_reduce_fusion
  9.6 0.7 fusion.12
  10.3 1.1 multiply_convert_fusion
  11.4 1.5 convolution_convert_fusion
  12.9 0.3 all_to_all.14
  13.2 25.9 %all_to_all.21 = bf16[16,10,2560]{2,1,0:T(8,128)(2,1)S(1)} all-to-all(bf16[16,10,2560]{2,1,0:T(8,128)(2,1)S(1)} %all_to_all.14), channel_id=1, replica_groups=mesh['z'=8,'core'=2,'ctx'=4,'tp'=4] {'ctx','tp'}, dimensions={0} | all-to-all | bytes 1638400 | tf_op jit(solution)/shard_map/all_to_all | solution.py:215
  39.1 1.2 reshape.110
  40.2 0.0 copy-start.1
  40.3 1.6 copy.26
  41.8 0.0 copy-start
  41.8 1.5 reshape.102
  43.3 0.0 all-gather.2.cloned.1.call-update
  43.4 0.0 reduce-scatter.4.cloned.1.call-start
  43.4 0.0 copy-done
  43.4 1.5 collective-permute-start
  45.0 0.0 copy-done.1
  45.0 0.6 collective-permute-start.1
  45.5 1.5 collective-permute-start.2
  47.0 28.3 %collective-permute-done.g1.refs_4_ = bf16[5120,128]{1,0:T(8,128)(2,1)} collective-permute-done((bf16[5120,128]{1,0:T(8,128)(2,1)S(1)}, bf16[5120,128]{1,0:T(8,128)(2,1)}, u32[]{:S(2)}, u32[]{:S(2)}) %collective-permute-start) | collective-permute-done | bytes 1310752 | tf_op jit(solution)/shard_map/ppermute | solution.py:185
  75.3 28.1 %collective-permute-done.1.u1.refs_5_ = bf16[5120,128]{1,0:T(8,128)(2,1)} collective-permute-done((bf16[5120,128]{1,0:T(8,128)(2,1)S(1)}, bf16[5120,128]{1,0:T(8,128)(2,1)}, u32[]{:S(2)}, u32[]{:S(2)}) %collective-permute-start.1) | collective-permute-done | bytes 1310752 | tf_op jit(solution)/shard_map/ppermute | solution.py:185
  103.4 25.7 %collective-permute-done.2.d1 = bf16[128,5120]{1,0:T(8,128)(2,1)} collective-permute-done((bf16[128,5120]{1,0:T(8,128)(2,1)}, bf16[128,5120]{1,0:T(8,128)(2,1)}, u32[]{:S(2)}, u32[]{:S(2)}) %collective-permute-start.2) | collective-permute-done | bytes 1310752 | tf_op jit(solution)/shard_map/ppermute | solution.py:185
  129.2 0.0 all-gather.2.cloned.1.call-done.x_ref.dy_ref
  129.2 0.0 copy-start.2
  129.2 1.3 copy-done.2
  130.5 12.2 %hidden_part.1 = (bf16[640,512]{1,0:T(8,128)(2,1)S(1)}, bf16[640,256]{1,0:T(8,128)(2,1)S(1)}, bf16[640,128]{1,0:T(8,128)(2,1)S(1)}) custom-call(bf16[640,10240]{1,0:T(8,128)(2,1)} %all-gather.2.cloned.1.call-done.x_ref.dy_ref, bf16[640,10240]{1,0:T(8,128)(2,1)} %all-gather.2.cloned.1.call-done.x_ref.dy_ref, bf16[5120,128]{1,0:T(8,128)(2,1)S(1)} %bitcast.56, ...), custom_call_target="tpu_custom_call" | custom-call | flops 5033164800 | bytes 13107200 | tf_op jit(solution)/shard_map/hidden_part/pallas_call | solution.py:71
  142.6 0.0 copy-start.3
  142.7 11.5 %weight_part.2 = (bf16[5120,128]{1,0:T(8,128)(2,1)}, bf16[5120,128]{1,0:T(8,128)(2,1)}, bf16[128,5120]{1,0:T(8,128)(2,1)}) custom-call(bf16[640,10240]{1,0:T(8,128)(2,1)} %all-gather.2.cloned.1.call-done.x_ref.dy_ref, bf16[640,10240]{1,0:T(8,128)(2,1)} %all-gather.2.cloned.1.call-done.x_ref.dy_ref, bf16[640,512]{1,0:T(8,128)(2,1)S(1)} %get-tuple-element.27.d_ref, ...), custom_call_target="tpu_custom_call" | custom-call | flops 2516582400 | bytes 13107200 | tf_op jit(solution)/shard_map/weight_part/pallas_call | solution.py:162
  154.1 0.0 copy-done.3
  154.2 5.1 %input_part.2 = bf16[320,5248]{1,0:T(8,128)(2,1)S(1)} custom-call(bf16[320,512]{1,0:T(8,128)(2,1)S(1)} %bitcast.67, bf16[320,128]{1,0:T(8,128)(2,1)S(1)} %bitcast.69, bf16[5120,128]{1,0:T(8,128)(2,1)S(1)} %bitcast.57, bf16[5120,128]{1,0:T(8,128)(2,1)S(1)} %bitcast.61, bf16[5120,128]{1,0:T(8,128)(2,1)} %collective-permute-done.g1.refs_4_, ...), custom_call_target="tpu_custom_call" | custom-call | flops 1677721600 | bytes 8519680 | tf_op jit(solution)/shard_map/input_part/pallas_call | solution.py:135
  159.3 0.1 collective-permute-start.3
  159.4 6.0 %collective-permute-done.3.refs_6_ = bf16[320,5248]{1,0:T(8,128)(2,1)S(1)} collective-permute-done((bf16[320,5248]{1,0:T(8,128)(2,1)S(1)}, bf16[320,5248]{1,0:T(8,128)(2,1)S(1)}, u32[]{:S(2)}, u32[]{:S(2)}) %collective-permute-start.3) | collective-permute-done | bytes 3358752 | tf_op jit(solution)/shard_map/ppermute | solution.py:185
  165.4 6.2 %input_part.3 = bf16[320,5248]{1,0:T(8,128)(2,1)} custom-call(bf16[320,512]{1,0:T(8,128)(2,1)S(1)} %bitcast.66, bf16[320,128]{1,0:T(8,128)(2,1)S(1)} %bitcast.68, bf16[5120,128]{1,0:T(8,128)(2,1)S(1)} %bitcast.58, bf16[5120,128]{1,0:T(8,128)(2,1)S(1)} %bitcast.62, bf16[5120,128]{1,0:T(8,128)(2,1)} %collective-permute-done.g1.refs_4_, ...), custom_call_target="tpu_custom_call" | custom-call | flops 1677721600 | bytes 8519680 | tf_op jit(solution)/shard_map/input_part/pallas_call | solution.py:135
  171.5 0.0 reduce-scatter.4.cloned.1.call-update
  171.6 1.6 collective-permute-start.4
  173.2 0.5 collective-permute-start.5
  173.7 1.5 collective-permute-start.6
  175.2 0.0 copy-start.4
  175.2 1.0 copy-done.4
  176.2 10.3 %weight_part.3 = (f32[5120,128]{1,0:T(8,128)S(1)}, f32[5120,128]{1,0:T(8,128)S(1)}, f32[128,5120]{1,0:T(8,128)S(1)}) custom-call(bf16[640,10240]{1,0:T(8,128)(2,1)} %all-gather.2.cloned.1.call-done.x_ref.dy_ref, bf16[640,10240]{1,0:T(8,128)(2,1)} %all-gather.2.cloned.1.call-done.x_ref.dy_ref, bf16[640,512]{1,0:T(8,128)(2,1)S(1)} %get-tuple-element.27.d_ref, ...), custom_call_target="tpu_custom_call" | custom-call | flops 2516582400 | bytes 13107200 | tf_op jit(solution)/shard_map/weight_part/pallas_call | solution.py:162
  186.5 17.0 %collective-permute-done.4 = bf16[5120,128]{1,0:T(8,128)(2,1)S(1)} collective-permute-done((bf16[5120,128]{1,0:T(8,128)(2,1)}, bf16[5120,128]{1,0:T(8,128)(2,1)S(1)}, u32[]{:S(2)}, u32[]{:S(2)}) %collective-permute-start.4) | collective-permute-done | bytes 1310752 | tf_op jit(solution)/shard_map/ppermute | solution.py:185
  203.5 1.3 fusion
  204.8 26.8 %collective-permute-done.5 = bf16[5120,128]{1,0:T(8,128)(2,1)S(1)} collective-permute-done((bf16[5120,128]{1,0:T(8,128)(2,1)}, bf16[5120,128]{1,0:T(8,128)(2,1)S(1)}, u32[]{:S(2)}, u32[]{:S(2)}) %collective-permute-start.5) | collective-permute-done | bytes 1310752 | tf_op jit(solution)/shard_map/ppermute | solution.py:185
  231.6 1.3 fusion.1
  232.9 0.0 reduce-scatter.4.cloned.1.call-done
  232.9 0.7 slice.18
  233.6 1.0 slice.17
  234.7 0.3 reshape.109
  234.9 0.1 copy.42
  235.1 0.2 pad_maximum_fusion
  235.3 1.0 copy.36
  236.3 5.0 %all-to-all-start.1 = ((bf16[16,10,1408]{2,1,0:T(8,128)(2,1)}), bf16[16,10,1408]{2,1,0:T(8,128)(2,1)S(1)}, u32[]{:S(2)}, u32[]{:S(2)}) async-start(bf16[16,10,1408]{2,1,0:T(8,128)(2,1)} %bitcast.72), calls=%async_computation.1 | async-start | bytes 1441792 | tf_op jit(solution)/shard_map/all_to_all | solution.py:253
  241.3 18.5 %collective-permute-done.6 = bf16[128,5120]{1,0:T(8,128)(2,1)} collective-permute-done((bf16[128,5120]{1,0:T(8,128)(2,1)}, bf16[128,5120]{1,0:T(8,128)(2,1)}, u32[]{:S(2)}, u32[]{:S(2)}) %collective-permute-start.6) | collective-permute-done | bytes 1310752 | tf_op jit(solution)/shard_map/ppermute | solution.py:185
  259.8 2.6 fusion.2
  262.4 4.1 %all-to-all-done.1 = bf16[16,10,1408]{2,1,0:T(8,128)(2,1)S(1)} async-done(((bf16[16,10,1408]{2,1,0:T(8,128)(2,1)}), bf16[16,10,1408]{2,1,0:T(8,128)(2,1)S(1)}, u32[]{:S(2)}, u32[]{:S(2)}) %all-to-all-start.1) | async-done | bytes 450592 | tf_op jit(solution)/shard_map/all_to_all | solution.py:253
  266.5 0.2 all_to_all.18
  266.6 0.3 fusion.6
  267.0 0.8 slice.23
  267.7 0.1 slice_reduce_fusion
  267.8 0.0 copy-done.5
  267.8 0.5 multiply_convert_fusion.1
  (6 shorter events, 0.1 us)
Async XLA Ops:
  7.2 122.0 %all-gather.2.cloned.1.call-start = ((), (), s32[]{:S(2)}) async-start(), calls=%async_computation.3 | async-start | bytes 13926400 | tf_op jit(solution)/shard_map/all_gather | solution.py:224
  40.2 4.7 %copy-start.1 = (bf16[1,5120,128]{2,1,0:T(8,128)(2,1)S(1)}, bf16[1,5120,128]{2,1,0:T(8,128)(2,1)}, u32[]{:S(2)}) copy-start(bf16[1,5120,128]{2,1,0:T(8,128)(2,1)} %param.12) | copy-start | bytes 3932164
  41.8 1.6 copy-start
  43.4 189.5 %reduce-scatter.4.cloned.1.call-start = ((), (), s32[]{:S(2)}) async-start(), calls=%async_computation.4 | async-start | bytes 3778560
  43.4 31.9 %collective-permute-start = (bf16[5120,128]{1,0:T(8,128)(2,1)S(1)}, bf16[5120,128]{1,0:T(8,128)(2,1)}, u32[]{:S(2)}, u32[]{:S(2)}) collective-permute-start(bf16[5120,128]{1,0:T(8,128)(2,1)S(1)} %bitcast.55), channel_id=1, source_target_pairs={{0,1},{1,0},{2,3},{3,2},{4,5},{5,4},{6,7},{7,6},{8,9},{9,8},{10,11... | collective-permute-start | bytes 3932168 | tf_op jit(solution)/shard_map/ppermute | solution.py:185
  45.0 58.4 %collective-permute-start.1 = (bf16[5120,128]{1,0:T(8,128)(2,1)S(1)}, bf16[5120,128]{1,0:T(8,128)(2,1)}, u32[]{:S(2)}, u32[]{:S(2)}) collective-permute-start(bf16[5120,128]{1,0:T(8,128)(2,1)S(1)} %bitcast.59), channel_id=1, source_target_pairs={{0,1},{1,0},{2,3},{3,2},{4,5},{5,4},{6,7},{7,6},{8,9},{9,8},{10,11... | collective-permute-start | bytes 3932168 | tf_op jit(solution)/shard_map/ppermute | solution.py:185
  45.5 83.6 %collective-permute-start.2 = (bf16[128,5120]{1,0:T(8,128)(2,1)}, bf16[128,5120]{1,0:T(8,128)(2,1)}, u32[]{:S(2)}, u32[]{:S(2)}) collective-permute-start(bf16[128,5120]{1,0:T(8,128)(2,1)} %bitcast.64), channel_id=1, source_target_pairs={{0,1},{1,0},{2,3},{3,2},{4,5},{5,4},{6,7},{7,6},{8,9},{9,8},{10,11... | collective-permute-start | bytes 3932168 | tf_op jit(solution)/shard_map/ppermute | solution.py:185
  129.2 1.3 copy-start.2
  142.6 11.5 %copy-start.3 = (bf16[640,256]{1,0:T(8,128)(2,1)}, bf16[640,256]{1,0:T(8,128)(2,1)S(1)}, u32[]{:S(2)}) copy-start(bf16[640,256]{1,0:T(8,128)(2,1)S(1)} %get-tuple-element.23.s_ref) | copy-start | bytes 983044
  159.3 6.1 %collective-permute-start.3 = (bf16[320,5248]{1,0:T(8,128)(2,1)S(1)}, bf16[320,5248]{1,0:T(8,128)(2,1)S(1)}, u32[]{:S(2)}, u32[]{:S(2)}) collective-permute-start(bf16[320,5248]{1,0:T(8,128)(2,1)S(1)} %input_part.2), channel_id=1, source_target_pairs={{0,16},{16,0},{1,17},{17,1},{2,18},{18,2},{3,19},{19,3},{4,20},{20... | collective-permute-start | bytes 10076168 | tf_op jit(solution)/shard_map/ppermute | solution.py:185
  171.6 31.9 %collective-permute-start.4 = (bf16[5120,128]{1,0:T(8,128)(2,1)}, bf16[5120,128]{1,0:T(8,128)(2,1)S(1)}, u32[]{:S(2)}, u32[]{:S(2)}) collective-permute-start(bf16[5120,128]{1,0:T(8,128)(2,1)} %get-tuple-element.24), channel_id=1, source_target_pairs={{0,1},{1,0},{2,3},{3,2},{4,5},{5,4},{6,7},{7,6},{8,9},{9,8},{10,11... | collective-permute-start | bytes 3932168 | tf_op jit(solution)/shard_map/ppermute | solution.py:185
  173.2 58.4 %collective-permute-start.5 = (bf16[5120,128]{1,0:T(8,128)(2,1)}, bf16[5120,128]{1,0:T(8,128)(2,1)S(1)}, u32[]{:S(2)}, u32[]{:S(2)}) collective-permute-start(bf16[5120,128]{1,0:T(8,128)(2,1)} %get-tuple-element.30), channel_id=1, source_target_pairs={{0,1},{1,0},{2,3},{3,2},{4,5},{5,4},{6,7},{7,6},{8,9},{9,8},{10,11... | collective-permute-start | bytes 3932168 | tf_op jit(solution)/shard_map/ppermute | solution.py:185
  173.7 86.1 %collective-permute-start.6 = (bf16[128,5120]{1,0:T(8,128)(2,1)}, bf16[128,5120]{1,0:T(8,128)(2,1)}, u32[]{:S(2)}, u32[]{:S(2)}) collective-permute-start(bf16[128,5120]{1,0:T(8,128)(2,1)} %get-tuple-element.32), channel_id=1, source_target_pairs={{0,1},{1,0},{2,3},{3,2},{4,5},{5,4},{6,7},{7,6},{8,9},{9,8},{10,11... | collective-permute-start | bytes 3932168 | tf_op jit(solution)/shard_map/ppermute | solution.py:185
  175.2 1.0 copy-start.4
  236.3 30.2 %all-to-all-start.1 = ((bf16[16,10,1408]{2,1,0:T(8,128)(2,1)}), bf16[16,10,1408]{2,1,0:T(8,128)(2,1)S(1)}, u32[]{:S(2)}, u32[]{:S(2)}) async-start(bf16[16,10,1408]{2,1,0:T(8,128)(2,1)} %bitcast.72), calls=%async_computation.1 | async-start | bytes 1441792 | tf_op jit(solution)/shard_map/all_to_all | solution.py:253
  262.4 5.4 %copy-start.5 = (f32[128]{0:T(128)S(1)}, f32[128]{0:T(128)}, u32[]{:S(2)}) copy-start(f32[128]{0:T(128)} %param.9) | copy-start | bytes 1540
Sparse Core Ops, SparseCore 0:
  43.5 78.0 all-gather.1
  171.7 52.6 reduce-scatter.3

commit v2 on v1

v2 whole, which is shorter than its diff:
```python
import jax
import jax.numpy as jnp
from jax import lax
from jax.experimental import pallas as pl
from jax.experimental.pallas import tpu as pltpu
from jax.sharding import Mesh, PartitionSpec as P

HALF = 10
PAD = 16
LANES = 128
BLOCK = 1024
LONG = 70_000_000_000
INNER = (((1,), (1,)), ((), ()))
OUTER = (((0,), (0,)), ((), ()))
F32 = jnp.float32
BF16 = jnp.bfloat16


def call(kernel, name, out_shape, vmem=60, flops=0, **kw):
    return pl.pallas_call(
        kernel,
        out_shape=out_shape,
        compiler_params=pltpu.CompilerParams(vmem_limit_bytes=vmem << 20),
        cost_estimate=pl.CostEstimate(flops=flops, bytes_accessed=0, transcendentals=0),
        name=name,
        **kw,
    )


def struct(shape, dtype):
    return jax.ShapeDtypeStruct(shape, dtype)


def whole(shape):
    return pl.BlockSpec(shape, lambda i: (0,) * len(shape))


def spread_kernel(x_ref, dy_ref, logit_ref, route_ref, send_ref, place_ref, n_dev):
    rows = x_ref.shape[0]
    route = route_ref[...]
    expert = lax.broadcasted_iota(jnp.int32, (n_dev // 2, rows), 0)
    hit = (route == expert).astype(F32)
    row = lax.broadcasted_iota(jnp.int32, (rows, rows), 0)
    col = lax.broadcasted_iota(jnp.int32, (rows, rows), 1)
    earlier = (row < col).astype(BF16)
    before = jnp.dot(hit.astype(BF16), earlier, preferred_element_type=F32)
    rank = jnp.sum(before * hit, axis=0, keepdims=True).astype(jnp.int32)
    member = (rank >= HALF).astype(jnp.int32)
    place = (2 * route + member) * PAD + rank - HALF * member
    place_ref[...] = place
    slot = lax.broadcasted_iota(jnp.int32, (n_dev * PAD, rows), 0)
    pick = (slot == place).astype(F32)
    weight = jax.nn.sigmoid(logit_ref[...]).astype(BF16).astype(F32)
    part = x_ref.shape[1]
    for k, (chosen, value) in enumerate(((pick, x_ref[...]), (pick * weight, dy_ref[...]))):
        out = jnp.dot(chosen.astype(BF16), value, preferred_element_type=F32).astype(BF16)
        for t in range(n_dev):
            send_ref[t, :, k * part : (k + 1) * part] = out[t * PAD : t * PAD + HALF]


def spread(x, dy, logit, route, n_dev):
    rows, part = x.shape
    return call(
        lambda *refs: spread_kernel(*refs, n_dev=n_dev),
        "spread",
        [struct((n_dev, HALF, 2 * part), BF16), struct((1, rows), jnp.int32)],
        vmem=16,
    )(x, dy, logit, route)


def arrange_kernel(recv_ref, out_ref, n_ctx, n_tp):
    part = recv_ref.shape[2] // 2
    for k in range(2):
        for t in range(n_tp):
            rows = [
                recv_ref[c * n_tp + t, :, k * part : (k + 1) * part].astype(F32)
                for c in range(n_ctx)
            ]
            start = (k * n_tp + t) * part
            out_ref[:, start : start + part] = jnp.concatenate(rows, 0).astype(BF16)


def arrange(recv, n_ctx, n_tp):
    part = recv.shape[2] // 2
    return call(
        lambda *refs: arrange_kernel(*refs, n_ctx=n_ctx, n_tp=n_tp),
        "arrange",
        struct((n_ctx * HALF, 2 * part * n_tp), BF16),
        vmem=16,
    )(recv)


def ship_kernel(sum_ref, out_ref, n_ctx, n_tp):
    part = out_ref.shape[2] - LANES
    width = part * n_tp
    router = sum_ref[:, width:].astype(F32)
    for t in range(n_tp):
        value = sum_ref[:, t * part : (t + 1) * part].astype(F32)
        for c in range(n_ctx):
            rows = slice(c * HALF, (c + 1) * HALF)
            out_ref[c * n_tp + t, :, :part] = value[rows].astype(BF16)
            out_ref[c * n_tp + t, :, part:] = router[rows].astype(BF16)


def ship(summed, n_ctx, n_tp):
    part = (summed.shape[1] - LANES) // n_tp
    return call(
        lambda *refs: ship_kernel(*refs, n_ctx=n_ctx, n_tp=n_tp),
        "ship",
        struct((n_ctx * n_tp, HALF, part + LANES), BF16),
        vmem=16,
    )(summed)


def home_kernel(land_ref, place_ref, logit_ref, input_ref, grad_ref):
    n_dev, _, wide = land_ref.shape
    rows, part = input_ref.shape
    fill = jnp.zeros((PAD - HALF, wide), F32)
    flat = []
    for t in range(n_dev):
        flat += [land_ref[t].astype(F32), fill]
    flat = jnp.concatenate(flat, 0).astype(BF16)
    slot = lax.broadcasted_iota(jnp.int32, (n_dev * PAD, rows), 0)
    pick = (slot == place_ref[...]).astype(BF16)
    home = lax.dot_general(pick, flat[:, :part], OUTER, preferred_element_type=F32)
    input_ref[...] = home.astype(BF16)
    router = lax.dot_general(flat[:, part:], pick, OUTER, preferred_element_type=F32)
    weight = jax.nn.sigmoid(logit_ref[...]).astype(BF16).astype(F32)
    grad_ref[...] = (router[:1] * (1.0 - weight)).astype(BF16)


def take_home(landed, place, logit):
    rows = place.shape[1]
    part = landed.shape[2] - LANES
    return call(
        home_kernel,
        "take_home",
        [struct((rows, part), BF16), struct((1, rows), BF16)],
        vmem=16,
    )(landed, place, logit)


def join(parts, axis):
    return jnp.concatenate([p[...] for p in parts], axis)


def gate_up_kernel(*refs):
    x_ref, gates, ups = refs[0], refs[1:5], refs[5:9]
    here_ref, there_ref, gate_ref, up_ref = refs[9:]
    step = pl.program_id(0)
    x = x_ref[...]
    gate_p = jnp.dot(x, join(gates, 1), preferred_element_type=F32)
    up_p = jnp.dot(x, join(ups, 1), preferred_element_type=F32)

    @pl.when(step == 0)
    def _():
        gate_ref[...] = gate_p
        up_ref[...] = up_p

    @pl.when(step > 0)
    def _():
        gate_ref[...] += gate_p
        up_ref[...] += up_p

    @pl.when(step == pl.num_programs(0) - 1)
    def _():
        half = here_ref.shape[1]
        for n, out in enumerate((here_ref, there_ref)):
            cols = slice(n * half, (n + 1) * half)
            gate = gate_ref[:, cols]
            out[...] = (gate * jax.nn.sigmoid(gate) * up_ref[:, cols]).astype(BF16)


def gate_up_part(both, sets):
    rows, wide = both.shape
    width = wide // 2
    unit = sets[0][0].shape[1]
    tall = pl.BlockSpec((BLOCK, unit), lambda i: (i, 0))
    return call(
        gate_up_kernel,
        "gate_up_part",
        [struct((rows, 2 * unit), BF16)] * 2 + [struct((rows, 4 * unit), F32)] * 2,
        grid=(width // BLOCK,),
        in_specs=[pl.BlockSpec((rows, BLOCK), lambda i: (0, i))] + [tall] * 8,
        out_specs=[whole((rows, 2 * unit))] * 2 + [whole((rows, 4 * unit))] * 2,
    )(both, *[s[0] for s in sets], *[s[1] for s in sets])


def back_kernel(*refs):
    dy_ref, downs = refs[0], refs[1:5]
    gate_ref, up_ref, here_ref, there_ref, r_ref, back_a = refs[5:]
    step = pl.program_id(0)
    back_p = lax.dot_general(dy_ref[...], join(downs, 0), INNER, preferred_element_type=F32)

    @pl.when(step == 0)
    def _():
        back_a[...] = back_p

    @pl.when(step > 0)
    def _():
        back_a[...] += back_p

    @pl.when(step == pl.num_programs(0) - 1)
    def _():
        unit = back_a.shape[1] // 4
        total = jnp.zeros((back_a.shape[0], 1), F32)
        for n in range(4):
            cols = slice(n * unit, (n + 1) * unit)
            gate = gate_ref[:, cols]
            up = up_ref[:, cols]
            back = back_a[:, cols]
            sig = jax.nn.sigmoid(gate)
            act = gate * sig
            out = here_ref if n < 2 else there_ref
            base = (n % 2) * 2 * unit
            d_gate = back * up * sig * (1.0 + gate * (1.0 - sig))
            out[:, base : base + unit] = d_gate.astype(BF16)
            out[:, base + unit : base + 2 * unit] = (back * act).astype(BF16)
            total = total + jnp.sum(act * up * back, axis=1, keepdims=True)
        r_ref[...] = jnp.broadcast_to(total, r_ref.shape).astype(BF16)


def back_part(both, downs, gate, up):
    rows, wide = both.shape
    width = wide // 2
    unit = downs[0].shape[0]
    steps = width // BLOCK
    return call(
        back_kernel,
        "back_part",
        [struct((rows, 4 * unit), BF16)] * 2 + [struct((rows, LANES), BF16)],
        grid=(steps,),
        in_specs=[pl.BlockSpec((rows, BLOCK), lambda i: (0, i + steps))]
        + [pl.BlockSpec((unit, BLOCK), lambda i: (0, i))] * 4
        + [whole((rows, 4 * unit))] * 2,
        out_specs=[whole((rows, 4 * unit))] * 2 + [whole((rows, LANES))],
        scratch_shapes=[pltpu.VMEM((rows, 4 * unit), F32)],
    )(both, *downs, gate, up)


def input_kernel(here_ref, there_ref, r_ref, *refs):
    out_ref = refs[-1]
    step = pl.program_id(0)
    last = pl.num_programs(0) - 1

    @pl.when(step < last)
    def _():
        weights = jnp.concatenate([w[...] for w in refs[:-1]], 1)
        d = jnp.concatenate([here_ref[...], there_ref[...]], 1)
        out_ref[...] = lax.dot_general(
            d, weights, INNER, preferred_element_type=F32
        ).astype(BF16)

    @pl.when(step == last)
    def _():
        out_ref[:, :LANES] = r_ref[...]


def input_part(here, there, router, sets):
    rows = here.shape[0]
    width, unit = sets[0][0].shape
    steps = width // BLOCK
    tall = pl.BlockSpec((BLOCK, unit), lambda i: (jnp.minimum(i, steps - 1), 0))
    strip = pl.BlockSpec((rows, BLOCK), lambda i: (0, i))
    weights = [w for s in sets for w in s]
    return call(
        input_kernel,
        "input_part",
        struct((rows, width + LANES), BF16),
        grid=(steps + 1,),
        in_specs=[whole((rows, 4 * unit))] * 2 + [whole((rows, LANES))] + [tall] * 8,
        out_specs=strip,
    )(here, there, router, *weights)


def tall_kernel(x0, x1, d0, d1, gate_ref, up_ref):
    unit = gate_ref.shape[1]
    x = jnp.concatenate([x0[...], x1[...]], 0)
    d = jnp.concatenate([d0[...], d1[...]], 0)
    out = lax.dot_general(x, d, OUTER, preferred_element_type=F32)
    gate_ref[...] = out[:, :unit].astype(gate_ref.dtype)
    up_ref[...] = out[:, unit:].astype(up_ref.dtype)


def tall_part(both, d, which, dtype, flops=0):
    rows, wide = both[0].shape
    width = wide // 2
    unit = d[0].shape[1] // 4
    x_spec = pl.BlockSpec((rows, BLOCK), lambda i: (0, i))
    d_spec = pl.BlockSpec((rows, 2 * unit), lambda i: (0, which))
    return call(
        tall_kernel,
        "tall_part",
        [struct((width, unit), dtype)] * 2,
        grid=(width // BLOCK,),
        in_specs=[x_spec] * 2 + [d_spec] * 2,
        out_specs=[pl.BlockSpec((BLOCK, unit), lambda i: (i, 0))] * 2,
        flops=flops,
    )(*both, *d)


def flat_kernel(y0, y1, s0, s1, *rest):
    down_ref = rest[-1]
    y = jnp.concatenate([y0[...], y1[...]], 0)
    s = jnp.concatenate([s0[...], s1[...]], 0)
    out = lax.dot_general(s, y, OUTER, preferred_element_type=F32)
    if len(rest) > 1:
        out = out + rest[0][...].astype(F32)
    down_ref[...] = out.astype(BF16)


def flat_part(both, s, which, addend=None, flops=0):
    rows, wide = both[0].shape
    width = wide // 2
    unit = s[0].shape[1] // 2
    steps = width // BLOCK
    y_spec = pl.BlockSpec((rows, BLOCK), lambda i: (0, i + steps))
    s_spec = pl.BlockSpec((rows, unit), lambda i: (0, which))
    o_spec = pl.BlockSpec((unit, BLOCK), lambda i: (0, i))
    extra = () if addend is None else (addend,)
    return call(
        flat_kernel,
        "flat_part",
        struct((unit, width), BF16),
        grid=(steps,),
        in_specs=[y_spec] * 2 + [s_spec] * 2 + [o_spec] * len(extra),
        out_specs=o_spec,
        flops=flops,
    )(*both, *s, *extra)


def flip(value, axis):
    count = lax.axis_size(axis)
    return lax.ppermute(value, axis, [(i, i ^ 1) for i in range(count)])


def after(value, first):
    return lax.optimization_barrier((value, first))[0]


def body(tokens_in, grad_out, router_logit, expert_index, gate_half, up_half, down_half):
    n_ctx = lax.axis_size("ctx")
    n_tp = lax.axis_size("tp")
    logit = router_logit[None]
    route = expert_index.reshape(1, -1)
    send, place = spread(tokens_in, grad_out, logit, route, n_ctx * n_tp)
    recv = lax.all_to_all(send, ("ctx", "tp"), split_axis=0, concat_axis=0, tiled=True)
    mine = arrange(recv, n_ctx, n_tp)
    own = (gate_half[0], up_half[0], down_half[0])
    other = tuple(flip(w, "tp") for w in after(own, recv))
    across = lambda group: tuple(flip(w, "core") for w in group)
    groups = (own, other, across(own), across(other))
    sets = tuple(g[:2] for g in groups)
    downs = tuple(g[2] for g in groups)
    here = lax.all_gather(mine, "z", axis=0, tiled=True)
    here, sets, downs = lax.optimization_barrier((here, sets, downs))
    beside = flip(here, "core")
    both = (here, beside)
    s_here, s_there, gate, up = gate_up_part(here, sets)
    s = (s_here, flip(s_there, "core"))
    give_down = flat_part(both, s, 1)
    got_down = flip(give_down, "tp")
    d_here, d_there, router = back_part(after(here, give_down), downs, gate, up)
    part = input_part(d_here, d_there, router, sets)
    summed = lax.optimization_barrier(
        lax.psum_scatter(part, "z", scatter_dimension=0, tiled=True)
    )
    d = after((d_here, flip(d_there, "core")), part)
    give = tall_part(both, d, 1, BF16)
    got = (flip(give[0], "tp"), flip(give[1], "tp"))
    s, d, got_down = lax.optimization_barrier((s, after(d, give[0]), got_down))
    down_grad = flat_part(both, s, 0, got_down, LONG)
    keep = tall_part(both, after(d, down_grad), 0, F32, LONG)
    summed = after(summed, keep[0])
    shipped = ship(summed, n_ctx, n_tp)
    landed = lax.all_to_all(shipped, ("ctx", "tp"), split_axis=0, concat_axis=0, tiled=True)
    input_grad, logit_grad = take_home(landed, place, logit)
    tall_grads = tuple((k + g.astype(F32)).astype(BF16)[None] for k, g in zip(keep, got))
    return (input_grad, logit_grad[0], *tall_grads, down_grad[None])


def solution(mesh):
    n_dp = mesh.shape["dp"]
    fine = Mesh(
        mesh.devices.reshape(n_dp // 2, 2, mesh.shape["ctx"], mesh.shape["tp"]),
        ("z", "core", "ctx", "tp"),
    )
    dp = ("z", "core")
    token = dp + ("ctx",)
    in_specs = (
        P(token, "tp"),
        P(token, "tp"),
        P(token),
        P(token, None),
        P(("ctx", "tp"), None, dp),
        P(("ctx", "tp"), None, dp),
        P(("ctx", "tp"), dp, None),
    )
    out_specs = (
        P(token, "tp"),
        P(token),
        P(("ctx", "tp"), None, dp),
        P(("ctx", "tp"), None, dp),
        P(("ctx", "tp"), dp, None),
    )
    return jax.shard_map(body, mesh=fine, in_specs=in_specs, out_specs=out_specs, check_vma=False)
```

time: 278 us -> 253 us (0.910)
  waiting for transfers between devices: 154 us -> 120 us
  Pallas kernels: 45.2 us -> 58.4 us
  other arithmetic: 10.2 us -> 6.25 us
    ppermute x7 -> x15, waiting for transfers between devices: 150 us -> 109 us  [flip(): return lax.ppermute(value, axis, [(i, i ^ 1) for i in range(count)])]
    pallas_call x5 -> x11, Pallas kernels: 45.2 us -> 58.4 us  [the longest x2 15.5 us: tall_part(): call(tall_kernel, 'tall_part', [struct((width, unit), dtype)] * 2, grid=(...]
    unnamed x12 -> x42, local copies, waits for them, and re-layouts: 2.31 us -> 11.1 us
    optimization_barrier x0 -> x1, waiting for transfers between devices: none -> 6.44 us  [after(): return lax.optimization_barrier((value, first))[0]]
    reshape x4 -> x0, local copies, waits for them, and re-layouts: 3.12 us -> none  [the longest x1 1.5 us: body(): mine = recv.reshape(n_ctx, n_tp, HALF, 2, part_width).transpose(0, 2, 3,...]
    convert_element_type x4 -> x0, other arithmetic: 3.03 us -> none  [the longest x1 1.1 us: body(): scaled_dy = (grad_out.astype(F32) * weight[:, None]).astype(BF16)]
    broadcast_in_dim x3 -> x2, other arithmetic: 5.25 us -> 6.25 us  [body(): (k + g.astype(F32)).astype(BF16)[None]]
    ppermute x7 -> x15, starting transfers between devices: 7.3 us -> 8.09 us  [flip(): return lax.ppermute(value, axis, [(i, i ^ 1) for i in range(count)])]
  transfers between devices with their start and end apart: 10 -> 18, of which waited for: 8 -> 10; matrix products, arithmetic and copies ran while one was open for 3% -> 2% of each run, Pallas kernels for 4% -> 20%
where the time goes in v2:
time: 253 us; the launch traced here: 251 us
  waiting for transfers between devices  120 us (47%)
  Pallas kernels  58.4 us (23%)
  blocking collectives  25.9 us (10%)
  starting transfers between devices  15 us (6%)
  between operations  14.2 us (6%)
  local copies, waits for them, and re-layouts  11.1 us (4%)
  other arithmetic  6.25 us (2%)
    ppermute x15, waiting for transfers between devices, flip(): return lax.ppermute(value, axis, [(i, i ^ 1) for i in range(count)])  109 us
    all_to_all x1, blocking collectives, body(): lax.all_to_all(send, ('ctx', 'tp'), split_axis=0, concat_axis=0, tiled=True)  25.9 us
    pallas_call x2, Pallas kernels, tall_part(): call(tall_kernel, 'tall_part', [struct((width, unit), dtype)] * 2, grid=(...  15.5 us
    pallas_call x2, Pallas kernels, flat_part(): call(flat_kernel, 'flat_part', struct((unit, width), BF16), grid=(steps,)...  12.7 us
    unnamed x42, local copies, waits for them, and re-layouts  11.1 us
    pallas_call x1, Pallas kernels, gate_up_part(): call(gate_up_kernel, 'gate_up_part', [struct((rows, 2 * unit), BF16)] * 2...  9.42 us
    pallas_call x1, Pallas kernels, input_part(): call(input_kernel, 'input_part', struct((rows, width + LANES), BF16), gri...  9.12 us
    ppermute x15, starting transfers between devices, flip(): return lax.ppermute(value, axis, [(i, i ^ 1) for i in range(count)])  8.09 us
  transfers between devices with their start and end apart: 18, of which 10 were waited for; matrix products, arithmetic and copies ran while one was open for 2% of the time, Pallas kernels for 20%

profile of v2, /device:TPU:2, one launch (start us, length us, event | category | flops | bytes accessed | tf_op | source)
XLA Modules:
  0.0 250.5 jit_solution(477619702742179325)
XLA Ops:
  7.2 0.0 all-gather.2.cloned.1.call-start
  7.2 1.0 copy-done.1
  8.2 1.0 copy-done.2
  9.2 0.7 copy-done.3
  9.8 0.7 copy-done.5
  10.5 0.6 spread.1
  11.1 25.9 %all_to_all.10.refs_0_ = bf16[16,10,2560]{2,1,0:T(8,128)(2,1)S(1)} all-to-all(bf16[16,10,2560]{2,1,0:T(8,128)(2,1)S(1)} %get-tuple-element.49), channel_id=1, replica_groups=mesh['z'=8,'core'=2,'ctx'=4,'tp'=4] {'ctx','tp'}, dimensions={0} | all-to-all | bytes 1638400 | tf_op jit(solution)/shard_map/all_to_all | solution.py:347
  37.0 1.1 arrange.1
  38.1 0.0 all-gather.2.cloned.1.call-update
  38.1 0.0 reduce-scatter.4.cloned.1.call-start
  38.2 0.4 copy-done.6
  38.6 0.0 collective-permute-start.2
  38.6 1.5 collective-permute-start
  40.1 0.6 collective-permute-start.1
  40.6 1.5 collective-permute-start.6
  42.1 0.0 collective-permute-start.3
  42.1 0.0 collective-permute-done.2.refs_3_.refs_4_
  42.1 0.5 collective-permute-start.7
  42.6 27.6 %collective-permute-done.refs_2_ = bf16[5120,128]{1,0:T(8,128)(2,1)S(1)} collective-permute-done((bf16[5120,128]{1,0:T(8,128)(2,1)S(1)}, bf16[5120,128]{1,0:T(8,128)(2,1)S(1)}, u32[]{:S(2)}, u32[]{:S(2)}) %collective-permute-start) | collective-permute-done | bytes 1310752 | tf_op jit(solution)/shard_map/ppermute | solution.py:334
  70.2 0.0 collective-permute-start.4
  70.2 28.1 %collective-permute-done.1.refs_6_.refs_3_ = bf16[5120,128]{1,0:T(8,128)(2,1)S(1)} collective-permute-done((bf16[5120,128]{1,0:T(8,128)(2,1)S(1)}, bf16[5120,128]{1,0:T(8,128)(2,1)S(1)}, u32[]{:S(2)}, u32[]{:S(2)}) %collective-permute-start.1) | collective-permute-done | bytes 1310752 | tf_op jit(solution)/shard_map/ppermute | solution.py:334
  98.3 0.0 collective-permute-start.5
  98.3 27.7 %collective-permute-done.6.refs_2_ = bf16[128,5120]{1,0:T(8,128)(2,1)S(1)} collective-permute-done((bf16[128,5120]{1,0:T(8,128)(2,1)}, bf16[128,5120]{1,0:T(8,128)(2,1)S(1)}, u32[]{:S(2)}, u32[]{:S(2)}) %collective-permute-start.6) | collective-permute-done | bytes 1310752 | tf_op jit(solution)/shard_map/ppermute | solution.py:334
  126.0 0.0 collective-permute-start.8
  126.0 0.0 collective-permute-done.3.refs_7_.refs_5_
  126.0 0.0 collective-permute-done.7.refs_3_
  126.0 0.0 copy-start.16
  126.0 0.0 collective-permute-done.4.refs_4_.refs_6_
  126.1 0.0 collective-permute-done.5.refs_8_.refs_7_
  126.1 1.0 copy-done.15
  127.0 0.5 copy-done.11
  127.5 0.4 copy-done.16
  127.9 1.1 copy-done.13
  129.0 0.1 collective-permute-done.8.refs_4_
  129.1 0.1 collective-permute-start.9
  129.3 9.4 %gate_up_part.1 = (bf16[320,256]{1,0:T(8,128)(2,1)}, bf16[320,256]{1,0:T(8,128)(2,1)}, f32[320,512]{1,0:T(8,128)}, f32[320,512]{1,0:T(8,128)}) custom-call(bf16[320,10240]{1,0:T(8,128)(2,1)} %all-gather.2.cloned.1.call-done.refs_0_.y0.x0, bf16[5120,128]{1,0:T(8,128)(2,1)} %bitcast.15, bf16[5120,128]{1,0:T(8,128)(2,1)} %copy-done.9, ...), custom_call_target="tpu_custom_call" | custom-call | tf_op jit(solution)/shard_map/gate_up_part/pallas_call | solution.py:179
  138.7 0.4 collective-permute-start.10
  139.1 1.2 collective-permute-done.10.s1
  140.3 0.7 copy-done.19
  141.0 6.2 %flat_part.2 = bf16[128,5120]{1,0:T(8,128)(2,1)} custom-call(bf16[320,10240]{1,0:T(8,128)(2,1)} %all-gather.2.cloned.1.call-done.refs_0_.y0.x0, bf16[320,10240]{1,0:T(8,128)(2,1)} %collective-permute-done.9.y1.x1, bf16[320,256]{1,0:T(8,128)(2,1)} %get-tuple-element.81.s0, bf16[320,256]{1,0:T(8,128)(2,1)} %copy-done.19), custom_call_target="tpu_custom_call" | custom-call | tf_op jit(solution)/shard_map/flat_part/pallas_call | solution.py:321
  147.1 1.5 collective-permute-start.12
  148.6 7.9 %back_part.1 = (bf16[320,512]{1,0:T(8,128)(2,1)}, bf16[320,512]{1,0:T(8,128)(2,1)}, bf16[320,128]{1,0:T(8,128)(2,1)}) custom-call(bf16[320,10240]{1,0:T(8,128)(2,1)} %all-gather.2.cloned.1.call-done.refs_0_.y0.x0, bf16[128,5120]{1,0:T(8,128)(2,1)} %bitcast.25, bf16[128,5120]{1,0:T(8,128)(2,1)} %copy-done.15, bf16[128,5120]{1,0:T(8,128)(2,1)} %copy-done.16, ...), custom_call_target="tpu_custom_call" | custom-call | tf_op jit(solution)/shard_map/back_part/pallas_call | solution.py:228
  156.5 0.1 collective-permute-start.11
  156.6 9.1 %input_part.1 = bf16[320,5248]{1,0:T(8,128)(2,1)} custom-call(bf16[320,512]{1,0:T(8,128)(2,1)} %get-tuple-element.84.here_ref.d0, bf16[320,512]{1,0:T(8,128)(2,1)} %get-tuple-element.72.there_ref, bf16[320,128]{1,0:T(8,128)(2,1)} %get-tuple-element.73.r_ref, bf16[5120,128]{1,0:T(8,128)(2,1)} %bitcast.16, bf16[5120,128]{1,0:T(8,128)(2,1)} %bitcast.20, ...), custom_call_target="tpu_custom_call" | custom-call | tf_op jit(solution)/shard_map/input_part/pallas_call | solution.py:266
  165.7 0.0 reduce-scatter.4.cloned.1.call-update
  165.8 0.7 copy-done.18
  166.5 7.1 %tall_part.2 = (bf16[5120,128]{1,0:T(8,128)(2,1)}, bf16[5120,128]{1,0:T(8,128)(2,1)}) custom-call(bf16[320,10240]{1,0:T(8,128)(2,1)} %all-gather.2.cloned.1.call-done.refs_0_.y0.x0, bf16[320,10240]{1,0:T(8,128)(2,1)} %collective-permute-done.9.y1.x1, bf16[320,512]{1,0:T(8,128)(2,1)} %get-tuple-element.84.here_ref.d0, bf16[320,512]{1,0:T(8,128)(2,1)} %copy-done.18), custom_call_target="tpu_custom_call" | custom-call | tf_op jit(solution)/shard_map/tall_part/pallas_call | solution.py:291
  173.7 0.6 collective-permute-start.13
  174.2 1.5 collective-permute-start.14
  175.7 3.3 %collective-permute-done.12.rest_0_ = bf16[128,5120]{1,0:T(8,128)(2,1)S(1)} collective-permute-done((bf16[128,5120]{1,0:T(8,128)(2,1)}, bf16[128,5120]{1,0:T(8,128)(2,1)S(1)}, u32[]{:S(2)}, u32[]{:S(2)}) %collective-permute-start.12) | collective-permute-done | bytes 1310752 | tf_op jit(solution)/shard_map/ppermute | solution.py:334
  179.0 1.1 copy-done.20
  180.0 6.6 %flat_part.3 = bf16[128,5120]{1,0:T(8,128)(2,1)} custom-call(bf16[320,10240]{1,0:T(8,128)(2,1)} %all-gather.2.cloned.1.call-done.refs_0_.y0.x0, bf16[320,10240]{1,0:T(8,128)(2,1)} %collective-permute-done.9.y1.x1, bf16[320,256]{1,0:T(8,128)(2,1)} %get-tuple-element.81.s0, bf16[320,256]{1,0:T(8,128)(2,1)} %copy-done.19, bf16[128,5120]{1,0:T(8,128)(2,1)} %copy-done.20), custom_call_target="tpu_custom_call" | custom-call | flops 70000001024 | tf_op jit(solution)/shard_map/flat_part/pallas_call | solution.py:321
  186.6 8.3 %tall_part.3 = (f32[5120,128]{1,0:T(8,128)}, f32[5120,128]{1,0:T(8,128)}) custom-call(bf16[320,10240]{1,0:T(8,128)(2,1)} %all-gather.2.cloned.1.call-done.refs_0_.y0.x0, bf16[320,10240]{1,0:T(8,128)(2,1)} %collective-permute-done.9.y1.x1, bf16[320,512]{1,0:T(8,128)(2,1)} %get-tuple-element.84.here_ref.d0, bf16[320,512]{1,0:T(8,128)(2,1)} %copy-done.18), custom_call_target="tpu_custom_call" | custom-call | flops 70000001024 | tf_op jit(solution)/shard_map/tall_part/pallas_call | solution.py:291
  194.9 12.1 %collective-permute-done.13 = bf16[5120,128]{1,0:T(8,128)(2,1)S(1)} collective-permute-done((bf16[5120,128]{1,0:T(8,128)(2,1)}, bf16[5120,128]{1,0:T(8,128)(2,1)S(1)}, u32[]{:S(2)}, u32[]{:S(2)}) %collective-permute-start.13) | collective-permute-done | bytes 1310752 | tf_op jit(solution)/shard_map/ppermute | solution.py:334
  207.0 1.1 copy-done.17
  208.1 3.6 %fusion = bf16[1,5120,128]{2,1,0:T(8,128)(2,1)} fusion(f32[5120,128]{1,0:T(8,128)} %get-tuple-element.86, bf16[5120,128]{1,0:T(8,128)(2,1)} %copy-done.17), kind=kLoop, calls=%fused_computation.2 | loop fusion | flops 1966080 | bytes 5242880 | tf_op jit(solution)/shard_map/broadcast_in_dim | solution.py:378
  211.7 6.4 %reduce-scatter.4.cloned.1.call-done.refs_0_ = bf16[40,5248]{1,0:T(8,128)(2,1)} async-done(((bf16[320,5248]{1,0:T(8,128)(2,1)}), bf16[40,5248]{1,0:T(8,128)(2,1)}) %reduce-scatter.4.cloned.1.call-update) | async-done | bytes 419856 | tf_op jit(solution)/shard_map/optimization_barrier | solution.py:338
  218.1 1.0 copy-done
  219.1 0.9 ship.1
  220.1 6.8 %all-to-all-start.1 = ((bf16[16,10,1408]{2,1,0:T(8,128)(2,1)}), bf16[16,10,1408]{2,1,0:T(8,128)(2,1)S(1)}, u32[]{:S(2)}, u32[]{:S(2)}) async-start(bf16[16,10,1408]{2,1,0:T(8,128)(2,1)} %ship.1), calls=%async_computation.1 | async-start | bytes 1441792 | tf_op jit(solution)/shard_map/all_to_all | solution.py:376
  226.8 8.4 %collective-permute-done.14 = bf16[5120,128]{1,0:T(8,128)(2,1)} collective-permute-done((bf16[5120,128]{1,0:T(8,128)(2,1)}, bf16[5120,128]{1,0:T(8,128)(2,1)}, u32[]{:S(2)}, u32[]{:S(2)}) %collective-permute-start.14) | collective-permute-done | bytes 1310752 | tf_op jit(solution)/shard_map/ppermute | solution.py:334
  235.2 2.7 %fusion.1 = bf16[1,5120,128]{2,1,0:T(8,128)(2,1)} fusion(f32[5120,128]{1,0:T(8,128)S(1)} %copy-done.14, bf16[5120,128]{1,0:T(8,128)(2,1)} %collective-permute-done.14), kind=kLoop, calls=%fused_computation.3 | loop fusion | flops 1966080 | bytes 5242880 | tf_op jit(solution)/shard_map/broadcast_in_dim | solution.py:378
  237.9 4.7 %all-to-all-done.1.land_ref = bf16[16,10,1408]{2,1,0:T(8,128)(2,1)S(1)} async-done(((bf16[16,10,1408]{2,1,0:T(8,128)(2,1)}), bf16[16,10,1408]{2,1,0:T(8,128)(2,1)S(1)}, u32[]{:S(2)}, u32[]{:S(2)}) %all-to-all-start.1) | async-done | bytes 450592 | tf_op jit(solution)/shard_map/all_to_all | solution.py:376
  242.7 1.0 take_home.1
  (30 shorter events, 0.1 us)
Async XLA Ops:
  7.2 122.0 %all-gather.2.cloned.1.call-start = ((), (), s32[]{:S(2)}) async-start(), calls=%async_computation.3 | async-start | bytes 7372800 | tf_op jit(solution)/shard_map/all_gather | solution.py:355
  7.2 1.0 copy-start.1
  8.2 1.0 copy-start.2
  9.2 0.7 copy-start.3
  9.8 0.7 copy-start.5
  37.0 1.6 copy-start.6
  37.0 3.1 %copy-start.7 = (bf16[1,5120,128]{2,1,0:T(8,128)(2,1)S(1)}, bf16[1,5120,128]{2,1,0:T(8,128)(2,1)}, u32[]{:S(2)}) copy-start(bf16[1,5120,128]{2,1,0:T(8,128)(2,1)} %param.12) | copy-start | bytes 3932164
  38.1 180.0 %reduce-scatter.4.cloned.1.call-start = ((), (), s32[]{:S(2)}) async-start(), calls=%async_computation.4 | async-start | bytes 3778560
  38.6 3.5 %collective-permute-start.2 = (bf16[5120,128]{1,0:T(8,128)(2,1)S(1)}, bf16[5120,128]{1,0:T(8,128)(2,1)S(1)}, u32[]{:S(2)}, u32[]{:S(2)}) collective-permute-start(bf16[5120,128]{1,0:T(8,128)(2,1)S(1)} %bitcast.17), channel_id=1, source_target_pairs={{0,16},{16,0},{1,17},{17,1},{2,18},{18,2},{3,19},{19,3},{4,20},{20... | collective-permute-start | bytes 3932168 | tf_op jit(solution)/shard_map/ppermute | solution.py:334
  38.6 31.6 %collective-permute-start = (bf16[5120,128]{1,0:T(8,128)(2,1)S(1)}, bf16[5120,128]{1,0:T(8,128)(2,1)S(1)}, u32[]{:S(2)}, u32[]{:S(2)}) collective-permute-start(bf16[5120,128]{1,0:T(8,128)(2,1)S(1)} %bitcast.18), channel_id=1, source_target_pairs={{0,1},{1,0},{2,3},{3,2},{4,5},{5,4},{6,7},{7,6},{8,9},{9,8},{10,11... | collective-permute-start | bytes 3932168 | tf_op jit(solution)/shard_map/ppermute | solution.py:334
  40.1 58.2 %collective-permute-start.1 = (bf16[5120,128]{1,0:T(8,128)(2,1)S(1)}, bf16[5120,128]{1,0:T(8,128)(2,1)S(1)}, u32[]{:S(2)}, u32[]{:S(2)}) collective-permute-start(bf16[5120,128]{1,0:T(8,128)(2,1)S(1)} %bitcast.21), channel_id=1, source_target_pairs={{0,1},{1,0},{2,3},{3,2},{4,5},{5,4},{6,7},{7,6},{8,9},{9,8},{10,11... | collective-permute-start | bytes 3932168 | tf_op jit(solution)/shard_map/ppermute | solution.py:334
  40.6 85.3 %collective-permute-start.6 = (bf16[128,5120]{1,0:T(8,128)(2,1)}, bf16[128,5120]{1,0:T(8,128)(2,1)S(1)}, u32[]{:S(2)}, u32[]{:S(2)}) collective-permute-start(bf16[128,5120]{1,0:T(8,128)(2,1)} %bitcast.23), channel_id=1, source_target_pairs={{0,1},{1,0},{2,3},{3,2},{4,5},{5,4},{6,7},{7,6},{8,9},{9,8},{10,11... | collective-permute-start | bytes 3932168 | tf_op jit(solution)/shard_map/ppermute | solution.py:334
  42.1 83.9 %collective-permute-start.3 = (bf16[5120,128]{1,0:T(8,128)(2,1)S(1)}, bf16[5120,128]{1,0:T(8,128)(2,1)S(1)}, u32[]{:S(2)}, u32[]{:S(2)}) collective-permute-start(bf16[5120,128]{1,0:T(8,128)(2,1)S(1)} %bitcast.22), channel_id=1, source_target_pairs={{0,16},{16,0},{1,17},{17,1},{2,18},{18,2},{3,19},{19,3},{4,20},{20... | collective-permute-start | bytes 3932168 | tf_op jit(solution)/shard_map/ppermute | solution.py:334
  42.1 83.9 %copy-start.8 = (bf16[5120,128]{1,0:T(8,128)(2,1)}, bf16[5120,128]{1,0:T(8,128)(2,1)S(1)}, u32[]{:S(2)}) copy-start(bf16[5120,128]{1,0:T(8,128)(2,1)S(1)} %collective-permute-done.2.refs_3_.refs_4_) | copy-start | bytes 3932164
  42.1 83.9 %collective-permute-start.7 = (bf16[128,5120]{1,0:T(8,128)(2,1)}, bf16[128,5120]{1,0:T(8,128)(2,1)S(1)}, u32[]{:S(2)}, u32[]{:S(2)}) collective-permute-start(bf16[128,5120]{1,0:T(8,128)(2,1)} %bitcast.24), channel_id=1, source_target_pairs={{0,16},{16,0},{1,17},{17,1},{2,18},{18,2},{3,19},{19,3},{4,20},{20... | collective-permute-start | bytes 3932168 | tf_op jit(solution)/shard_map/ppermute | solution.py:334
  70.2 55.8 %copy-start.9 = (bf16[5120,128]{1,0:T(8,128)(2,1)}, bf16[5120,128]{1,0:T(8,128)(2,1)S(1)}, u32[]{:S(2)}) copy-start(bf16[5120,128]{1,0:T(8,128)(2,1)S(1)} %collective-permute-done.refs_2_) | copy-start | bytes 3932164
  70.2 55.9 %collective-permute-start.4 = (bf16[5120,128]{1,0:T(8,128)(2,1)S(1)}, bf16[5120,128]{1,0:T(8,128)(2,1)S(1)}, u32[]{:S(2)}, u32[]{:S(2)}) collective-permute-start(bf16[5120,128]{1,0:T(8,128)(2,1)S(1)} %collective-permute-done.refs_2_), channel_id=1, source_target_pairs={{0,16},{16,0},{1,17},{17,1},{2,18},{18,2},{3,19},{19,3},{4,20},{20... | collective-permute-start | bytes 3932168 | tf_op jit(solution)/shard_map/ppermute | solution.py:334
  98.3 27.8 %copy-start.10 = (bf16[5120,128]{1,0:T(8,128)(2,1)}, bf16[5120,128]{1,0:T(8,128)(2,1)S(1)}, u32[]{:S(2)}) copy-start(bf16[5120,128]{1,0:T(8,128)(2,1)S(1)} %collective-permute-done.1.refs_6_.refs_3_) | copy-start | bytes 3932164
  98.3 27.8 %collective-permute-start.5 = (bf16[5120,128]{1,0:T(8,128)(2,1)S(1)}, bf16[5120,128]{1,0:T(8,128)(2,1)S(1)}, u32[]{:S(2)}, u32[]{:S(2)}) collective-permute-start(bf16[5120,128]{1,0:T(8,128)(2,1)S(1)} %collective-permute-done.1.refs_6_.refs_3_), channel_id=1, source_target_pairs={{0,16},{16,0},{1,17},{17,1},{2,18},{18,2},{3,19},{19,3},{4,20},{20... | collective-permute-start | bytes 3932168 | tf_op jit(solution)/shard_map/ppermute | solution.py:334
  126.0 1.1 copy-start.15
  126.0 3.2 %collective-permute-start.8 = (bf16[128,5120]{1,0:T(8,128)(2,1)S(1)}, bf16[128,5120]{1,0:T(8,128)(2,1)}, u32[]{:S(2)}, u32[]{:S(2)}) collective-permute-start(bf16[128,5120]{1,0:T(8,128)(2,1)S(1)} %collective-permute-done.6.refs_2_), channel_id=1, source_target_pairs={{0,16},{16,0},{1,17},{17,1},{2,18},{18,2},{3,19},{19,3},{4,20},{20... | collective-permute-start | bytes 3932168 | tf_op jit(solution)/shard_map/ppermute | solution.py:334
  126.0 1.5 copy-start.11
  126.0 1.9 copy-start.16
  126.0 3.2 %copy-start.12 = (bf16[5120,128]{1,0:T(8,128)(2,1)}, bf16[5120,128]{1,0:T(8,128)(2,1)S(1)}, u32[]{:S(2)}) copy-start(bf16[5120,128]{1,0:T(8,128)(2,1)S(1)} %collective-permute-done.4.refs_4_.refs_6_) | copy-start | bytes 3932164
  127.9 1.1 copy-start.13
  129.1 11.2 %collective-permute-start.9 = (bf16[320,10240]{1,0:T(8,128)(2,1)}, bf16[320,10240]{1,0:T(8,128)(2,1)}, u32[]{:S(2)}, u32[]{:S(2)}) collective-permute-start(bf16[320,10240]{1,0:T(8,128)(2,1)} %all-gather.2.cloned.1.call-done.refs_0_.y0.x0), channel_id=1, source_target_pairs={{0,16},{16,0},{1,17},{17,1},{2,18},{18,2},{3,19},{19,3},{4,20},{20... | collective-permute-start | bytes 19660808 | tf_op jit(solution)/shard_map/ppermute | solution.py:334
  138.7 1.6 collective-permute-start.10
  140.3 0.7 copy-start.19
  147.1 31.8 %collective-permute-start.12 = (bf16[128,5120]{1,0:T(8,128)(2,1)}, bf16[128,5120]{1,0:T(8,128)(2,1)S(1)}, u32[]{:S(2)}, u32[]{:S(2)}) collective-permute-start(bf16[128,5120]{1,0:T(8,128)(2,1)} %flat_part.2), channel_id=1, source_target_pairs={{0,1},{1,0},{2,3},{3,2},{4,5},{5,4},{6,7},{7,6},{8,9},{9,8},{10,11... | collective-permute-start | bytes 3932168 | tf_op jit(solution)/shard_map/ppermute | solution.py:334
  156.5 9.2 %collective-permute-start.11 = (bf16[320,512]{1,0:T(8,128)(2,1)}, bf16[320,512]{1,0:T(8,128)(2,1)S(1)}, u32[]{:S(2)}, u32[]{:S(2)}) collective-permute-start(bf16[320,512]{1,0:T(8,128)(2,1)} %get-tuple-element.72.there_ref), channel_id=1, source_target_pairs={{0,16},{16,0},{1,17},{17,1},{2,18},{18,2},{3,19},{19,3},{4,20},{20... | collective-permute-start | bytes 983048 | tf_op jit(solution)/shard_map/ppermute | solution.py:334
  165.8 0.7 copy-start.18
  173.7 33.4 %collective-permute-start.13 = (bf16[5120,128]{1,0:T(8,128)(2,1)}, bf16[5120,128]{1,0:T(8,128)(2,1)S(1)}, u32[]{:S(2)}, u32[]{:S(2)}) collective-permute-start(bf16[5120,128]{1,0:T(8,128)(2,1)} %get-tuple-element.76), channel_id=1, source_target_pairs={{0,1},{1,0},{2,3},{3,2},{4,5},{5,4},{6,7},{7,6},{8,9},{9,8},{10,11... | collective-permute-start | bytes 3932168 | tf_op jit(solution)/shard_map/ppermute | solution.py:334
  174.2 61.0 %collective-permute-start.14 = (bf16[5120,128]{1,0:T(8,128)(2,1)}, bf16[5120,128]{1,0:T(8,128)(2,1)}, u32[]{:S(2)}, u32[]{:S(2)}) collective-permute-start(bf16[5120,128]{1,0:T(8,128)(2,1)} %get-tuple-element.92), channel_id=1, source_target_pairs={{0,1},{1,0},{2,3},{3,2},{4,5},{5,4},{6,7},{7,6},{8,9},{9,8},{10,11... | collective-permute-start | bytes 3932168 | tf_op jit(solution)/shard_map/ppermute | solution.py:334
  179.0 1.1 copy-start.20
  207.0 1.1 copy-start.17
  208.1 27.1 %copy-start.14 = (f32[5120,128]{1,0:T(8,128)S(1)}, f32[5120,128]{1,0:T(8,128)}, u32[]{:S(2)}) copy-start(f32[5120,128]{1,0:T(8,128)} %get-tuple-element.91) | copy-start | bytes 7864324
  218.1 1.0 copy-start
  220.1 22.6 %all-to-all-start.1 = ((bf16[16,10,1408]{2,1,0:T(8,128)(2,1)}), bf16[16,10,1408]{2,1,0:T(8,128)(2,1)S(1)}, u32[]{:S(2)}, u32[]{:S(2)}) async-start(bf16[16,10,1408]{2,1,0:T(8,128)(2,1)} %ship.1), calls=%async_computation.1 | async-start | bytes 1441792 | tf_op jit(solution)/shard_map/all_to_all | solution.py:376
  235.2 7.4 %copy-start.4 = (f32[128]{0:T(128)S(1)}, f32[128]{0:T(128)}, u32[]{:S(2)}) copy-start(f32[128]{0:T(128)} %param.9) | copy-start | bytes 1540
Sparse Core Ops, SparseCore 0:
  38.3 76.8 all-gather.1
  165.9 52.1 reduce-scatter.3

commit v3 on v2

--- a/solution.py
+++ b/solution.py
@@ -6,10 +6,13 @@
 from jax.sharding import Mesh, PartitionSpec as P
 
 HALF = 10
+MAIN = 8
+REST = HALF - MAIN
 PAD = 16
 LANES = 128
-BLOCK = 1024
+BLOCK = 2560
 LONG = 70_000_000_000
+SHORT = 23_000_000_000
 INNER = (((1,), (1,)), ((), ()))
 OUTER = (((0,), (0,)), ((), ()))
 F32 = jnp.float32
@@ -36,7 +39,7 @@
 
 
 def spread_kernel(x_ref, dy_ref, logit_ref, route_ref, send_ref, place_ref, n_dev):
-    rows = x_ref.shape[0]
+    rows, part = x_ref.shape
     route = route_ref[...]
     expert = lax.broadcasted_iota(jnp.int32, (n_dev // 2, rows), 0)
     hit = (route == expert).astype(F32)
@@ -48,40 +51,69 @@
     member = (rank >= HALF).astype(jnp.int32)
     place = (2 * route + member) * PAD + rank - HALF * member
     place_ref[...] = place
-    slot = lax.broadcasted_iota(jnp.int32, (n_dev * PAD, rows), 0)
-    pick = (slot == place).astype(F32)
     weight = jax.nn.sigmoid(logit_ref[...]).astype(BF16).astype(F32)
-    part = x_ref.shape[1]
-    for k, (chosen, value) in enumerate(((pick, x_ref[...]), (pick * weight, dy_ref[...]))):
-        out = jnp.dot(chosen.astype(BF16), value, preferred_element_type=F32).astype(BF16)
+    slot = lax.broadcasted_iota(jnp.int32, (n_dev * MAIN, rows), 0)
+    target, r = slot // MAIN, slot % MAIN
+    pieces = MAIN // REST
+    main = (target * PAD + r == place).astype(F32)
+    rest = (target * PAD + MAIN + r // pieces == place).astype(F32)
+    which = (slot % pieces)[:, :1]
+    cut = 2 * part // pieces
+    extra = jnp.zeros((n_dev * MAIN, cut), F32)
+    for k, (scale, value) in enumerate(((1.0, x_ref[...]), (weight, dy_ref[...]))):
+        out = jnp.dot((main * scale).astype(BF16), value, preferred_element_type=F32)
+        out = out.astype(BF16)
         for t in range(n_dev):
-            send_ref[t, :, k * part : (k + 1) * part] = out[t * PAD : t * PAD + HALF]
+            send_ref[t, :, k * part : (k + 1) * part] = out[t * MAIN : (t + 1) * MAIN]
+        tail = jnp.dot((rest * scale).astype(BF16), value, preferred_element_type=F32)
+        for h in range(part // cut):
+            chosen = which == k * (part // cut) + h
+            extra = jnp.where(chosen, tail[:, h * cut : (h + 1) * cut], extra)
+    extra = extra.astype(BF16)
+    for t in range(n_dev):
+        send_ref[t, :, 2 * part :] = extra[t * MAIN : (t + 1) * MAIN]
 
 
 def spread(x, dy, logit, route, n_dev):
     rows, part = x.shape
+    wide = 2 * part * HALF // MAIN
     return call(
         lambda *refs: spread_kernel(*refs, n_dev=n_dev),
         "spread",
-        [struct((n_dev, HALF, 2 * part), BF16), struct((1, rows), jnp.int32)],
-        vmem=16,
+        [struct((n_dev, MAIN, wide), BF16), struct((1, rows), jnp.int32)],
     )(x, dy, logit, route)
 
 
 def arrange_kernel(recv_ref, out_ref, n_ctx, n_tp):
-    part = recv_ref.shape[2] // 2
+    n_dev = n_ctx * n_tp
+    part = out_ref.shape[1] // (2 * n_tp)
+    pieces = MAIN // REST
+    cut = 2 * part // pieces
+    extra = jnp.concatenate([recv_ref[t, :, 2 * part :] for t in range(n_dev)], 0)
+    size = n_dev * MAIN
+    row = lax.broadcasted_iota(jnp.int32, (size, size), 0)
+    col = lax.broadcasted_iota(jnp.int32, (size, size), 1)
+    group = n_ctx * REST
+    t, p = row // (pieces * group), row // group % pieces
+    c, i = row // REST % n_ctx, row % REST
+    order = (col == (c * n_tp + t) * MAIN + i * pieces + p).astype(BF16)
+    extra = jnp.dot(order, extra, preferred_element_type=F32)
     for k in range(2):
         for t in range(n_tp):
             rows = [
                 recv_ref[c * n_tp + t, :, k * part : (k + 1) * part].astype(F32)
                 for c in range(n_ctx)
             ]
+            tail = []
+            for h in range(part // cut):
+                at = (t * pieces + k * (part // cut) + h) * group
+                tail.append(extra[at : at + group])
+            rows.append(jnp.concatenate(tail, 1))
             start = (k * n_tp + t) * part
             out_ref[:, start : start + part] = jnp.concatenate(rows, 0).astype(BF16)
 
 
-def arrange(recv, n_ctx, n_tp):
-    part = recv.shape[2] // 2
+def arrange(recv, part, n_ctx, n_tp):
     return call(
         lambda *refs: arrange_kernel(*refs, n_ctx=n_ctx, n_tp=n_tp),
         "arrange",
@@ -97,9 +129,12 @@
     for t in range(n_tp):
         value = sum_ref[:, t * part : (t + 1) * part].astype(F32)
         for c in range(n_ctx):
-            rows = slice(c * HALF, (c + 1) * HALF)
-            out_ref[c * n_tp + t, :, :part] = value[rows].astype(BF16)
-            out_ref[c * n_tp + t, :, part:] = router[rows].astype(BF16)
+            main = slice(c * MAIN, (c + 1) * MAIN)
+            rest = slice(n_ctx * MAIN + c * REST, n_ctx * MAIN + (c + 1) * REST)
+            both = jnp.concatenate([value[main], value[rest]], 0)
+            out_ref[c * n_tp + t, :, :part] = both.astype(BF16)
+            both = jnp.concatenate([router[main], router[rest]], 0)
+            out_ref[c * n_tp + t, :, part:] = both.astype(BF16)
 
 
 def ship(summed, n_ctx, n_tp):
@@ -187,8 +222,8 @@
 
 
 def back_kernel(*refs):
-    dy_ref, downs = refs[0], refs[1:5]
-    gate_ref, up_ref, here_ref, there_ref, r_ref, back_a = refs[5:]
+    dy_ref, downs = refs[0], refs[1:-6]
+    gate_ref, up_ref, here_ref, there_ref, r_ref, back_a = refs[-6:]
     step = pl.program_id(0)
     back_p = lax.dot_general(dy_ref[...], join(downs, 0), INNER, preferred_element_type=F32)
 
@@ -223,7 +258,7 @@
 def back_part(both, downs, gate, up):
     rows, wide = both.shape
     width = wide // 2
-    unit = downs[0].shape[0]
+    unit = gate.shape[1] // 4
     steps = width // BLOCK
     return call(
         back_kernel,
@@ -231,10 +266,11 @@
         [struct((rows, 4 * unit), BF16)] * 2 + [struct((rows, LANES), BF16)],
         grid=(steps,),
         in_specs=[pl.BlockSpec((rows, BLOCK), lambda i: (0, i + steps))]
-        + [pl.BlockSpec((unit, BLOCK), lambda i: (0, i))] * 4
+        + [pl.BlockSpec((w.shape[0], BLOCK), lambda i: (0, i)) for w in downs]
         + [whole((rows, 4 * unit))] * 2,
         out_specs=[whole((rows, 4 * unit))] * 2 + [whole((rows, LANES))],
         scratch_shapes=[pltpu.VMEM((rows, 4 * unit), F32)],
+        flops=LONG,
     )(both, *downs, gate, up)
 
 
@@ -345,23 +381,24 @@
     route = expert_index.reshape(1, -1)
     send, place = spread(tokens_in, grad_out, logit, route, n_ctx * n_tp)
     recv = lax.all_to_all(send, ("ctx", "tp"), split_axis=0, concat_axis=0, tiled=True)
-    mine = arrange(recv, n_ctx, n_tp)
+    mine = arrange(recv, tokens_in.shape[1], n_ctx, n_tp)
     own = (gate_half[0], up_half[0], down_half[0])
     other = tuple(flip(w, "tp") for w in after(own, recv))
     across = lambda group: tuple(flip(w, "core") for w in group)
-    groups = (own, other, across(own), across(other))
-    sets = tuple(g[:2] for g in groups)
-    downs = tuple(g[2] for g in groups)
+    own_there = across(own)
+    sets = (own[:2], other[:2], own_there[:2], across(other[:2]))
     here = lax.all_gather(mine, "z", axis=0, tiled=True)
-    here, sets, downs = lax.optimization_barrier((here, sets, downs))
+    here, sets = lax.optimization_barrier((here, sets))
     beside = flip(here, "core")
     both = (here, beside)
     s_here, s_there, gate, up = gate_up_part(here, sets)
+    down = after(other[2], s_here)
+    downs = (own[2], down, own_there[2], flip(down, "core"))
     s = (s_here, flip(s_there, "core"))
-    give_down = flat_part(both, s, 1)
+    d_here, d_there, router = back_part(here, downs, gate, up)
+    give_down = flat_part(both, after(s, router), 1)
     got_down = flip(give_down, "tp")
-    d_here, d_there, router = back_part(after(here, give_down), downs, gate, up)
-    part = input_part(d_here, d_there, router, sets)
+    part = input_part(after(d_here, give_down), d_there, router, sets)
     summed = lax.optimization_barrier(
         lax.psum_scatter(part, "z", scatter_dimension=0, tiled=True)
     )
@@ -369,8 +406,8 @@
     give = tall_part(both, d, 1, BF16)
     got = (flip(give[0], "tp"), flip(give[1], "tp"))
     s, d, got_down = lax.optimization_barrier((s, after(d, give[0]), got_down))
-    down_grad = flat_part(both, s, 0, got_down, LONG)
-    keep = tall_part(both, after(d, down_grad), 0, F32, LONG)
+    down_grad = flat_part(both, s, 0, got_down, SHORT)
+    keep = tall_part(both, after(d, down_grad), 0, F32, SHORT)
     summed = after(summed, keep[0])
     shipped = ship(summed, n_ctx, n_tp)
     landed = lax.all_to_all(shipped, ("ctx", "tp"), split_axis=0, concat_axis=0, tiled=True)

time: 253 us -> 244 us (0.964)
  waiting for transfers between devices: 120 us -> 129 us
  Pallas kernels: 58.4 us -> 49.7 us
  blocking collectives: 25.9 us -> 20.9 us
    all_gather x1, waiting for transfers between devices: 0.01 us -> 15 us  [body(): here = lax.all_gather(mine, 'z', axis=0, tiled=True)]
    optimization_barrier x1, waiting for transfers between devices: 6.44 us -> 0.01 us  [after(): return lax.optimization_barrier((value, first))[0]]
    all_to_all x1, blocking collectives: 25.9 us -> 20.9 us  [body(): lax.all_to_all(send, ('ctx', 'tp'), split_axis=0, concat_axis=0, tiled=True)]
    pallas_call x2, Pallas kernels: 15.5 us -> 11.6 us  [tall_part(): call(tall_kernel, 'tall_part', [struct((width, unit), dtype)] * 2, grid=(...]
    pallas_call x2, Pallas kernels: 12.7 us -> 9.43 us  [flat_part(): call(flat_kernel, 'flat_part', struct((unit, width), BF16), grid=(steps,)...]
    unnamed x42 -> x36, local copies, waits for them, and re-layouts: 11.1 us -> 9 us
  transfers between devices with their start and end apart: 18 -> 18, of which waited for: 10 -> 11; matrix products, arithmetic and copies ran while one was open for 2% -> 3% of each run, Pallas kernels for 20% -> 17%
where the time goes in v3:
time: 244 us; the launch traced here: 242 us
  waiting for transfers between devices  129 us (53%)
  Pallas kernels  49.7 us (20%)
  blocking collectives  20.9 us (9%)
  between operations  14.1 us (6%)
  starting transfers between devices  13.2 us (5%)
  local copies, waits for them, and re-layouts  9 us (4%)
  other arithmetic  6.29 us (3%)
    ppermute x15, waiting for transfers between devices, flip(): return lax.ppermute(value, axis, [(i, i ^ 1) for i in range(count)])  110 us
    all_to_all x1, blocking collectives, body(): lax.all_to_all(send, ('ctx', 'tp'), split_axis=0, concat_axis=0, tiled=True)  20.9 us
    all_gather x1, waiting for transfers between devices, body(): here = lax.all_gather(mine, 'z', axis=0, tiled=True)  15 us
    pallas_call x2, Pallas kernels, tall_part(): call(tall_kernel, 'tall_part', [struct((width, unit), dtype)] * 2, grid=(...  11.6 us
    pallas_call x2, Pallas kernels, flat_part(): call(flat_kernel, 'flat_part', struct((unit, width), BF16), grid=(steps,)...  9.43 us
    unnamed x36, local copies, waits for them, and re-layouts  9 us
    pallas_call x1, Pallas kernels, input_part(): call(input_kernel, 'input_part', struct((rows, width + LANES), BF16), gri...  8.32 us
    ppermute x15, starting transfers between devices, flip(): return lax.ppermute(value, axis, [(i, i ^ 1) for i in range(count)])  8.23 us
  transfers between devices with their start and end apart: 18, of which 11 were waited for; matrix products, arithmetic and copies ran while one was open for 3% of the time, Pallas kernels for 17%

profile of v3, /device:TPU:2, one launch (start us, length us, event | category | flops | bytes accessed | tf_op | source)
XLA Modules:
  0.0 241.8 jit_solution(2834891623638576850)
XLA Ops:
  7.2 0.0 all-gather.2.cloned.1.call-start
  7.2 2.6 %spread.1 = (bf16[16,8,3200]{2,1,0:T(8,128)(2,1)}, s32[1,128]{1,0:T(1,128)}) custom-call(bf16[128,1280]{1,0:T(8,128)(2,1)} %refs_0_.1, bf16[128,1280]{1,0:T(8,128)(2,1)} %refs_1_.1, f32[1,128]{1,0:T(1,128)} %bitcast.12, s32[1,128]{1,0:T(1,128)} %bitcast.22), custom_call_target="tpu_custom_call" | custom-call | tf_op jit(solution)/shard_map/spread/pallas_call | solution.py:80
  9.8 20.9 %all_to_all.10.refs_0_ = bf16[16,8,3200]{2,1,0:T(8,128)(2,1)S(1)} all-to-all(bf16[16,8,3200]{2,1,0:T(8,128)(2,1)} %get-tuple-element.48), channel_id=1, replica_groups=mesh['z'=8,'core'=2,'ctx'=4,'tp'=4] {'ctx','tp'}, dimensions={0} | all-to-all | bytes 1638400 | tf_op jit(solution)/shard_map/all_to_all | solution.py:383
  30.8 1.1 arrange.1
  31.9 0.0 all-gather.2.cloned.1.call-update
  31.9 0.0 reduce-scatter.4.cloned.1.call-start
  31.9 0.4 copy-done.3
  32.4 1.5 collective-permute-start
  33.8 0.6 collective-permute-start.1
  34.4 0.0 collective-permute-start.2
  34.4 0.5 collective-permute-start.3
  34.9 29.2 %collective-permute-done.refs_2_ = bf16[5120,128]{1,0:T(8,128)(2,1)S(1)} collective-permute-done((bf16[5120,128]{1,0:T(8,128)(2,1)S(1)}, bf16[5120,128]{1,0:T(8,128)(2,1)S(1)}, u32[]{:S(2)}, u32[]{:S(2)}) %collective-permute-start) | collective-permute-done | bytes 1310752 | tf_op jit(solution)/shard_map/ppermute | solution.py:370
  64.1 0.0 collective-permute-start.4
  64.1 25.7 %collective-permute-done.1.refs_6_.refs_3_ = bf16[5120,128]{1,0:T(8,128)(2,1)S(1)} collective-permute-done((bf16[5120,128]{1,0:T(8,128)(2,1)S(1)}, bf16[5120,128]{1,0:T(8,128)(2,1)S(1)}, u32[]{:S(2)}, u32[]{:S(2)}) %collective-permute-start.1) | collective-permute-done | bytes 1310752 | tf_op jit(solution)/shard_map/ppermute | solution.py:370
  89.8 0.0 collective-permute-start.5
  89.8 1.5 collective-permute-start.6
  91.3 0.0 collective-permute-done.2.refs_3_.refs_4_
  91.3 0.2 collective-permute-start.7
  91.5 0.0 collective-permute-done.3.refs_7_.refs_5_
  91.5 0.0 copy-done.5
  91.5 0.0 collective-permute-done.4.refs_4_.refs_6_
  91.5 0.8 copy-done.7
  92.4 0.4 copy-done.8
  92.8 1.1 copy-done.9
  93.9 0.0 collective-permute-done.5.refs_8_.refs_7_
  93.9 15.0 %all-gather.2.cloned.1.call-done.refs_0_.y0.x0 = bf16[320,10240]{1,0:T(8,128)(2,1)} async-done(((bf16[40,10240]{1,0:T(8,128)(2,1)}), bf16[320,10240]{1,0:T(8,128)(2,1)}) %all-gather.2.cloned.1.call-update) | async-done | bytes 6553616 | tf_op jit(solution)/shard_map/all_gather | solution.py:390
  108.9 8.2 %gate_up_part.1 = (bf16[320,256]{1,0:T(8,128)(2,1)}, bf16[320,256]{1,0:T(8,128)(2,1)}, f32[320,512]{1,0:T(8,128)}, f32[320,512]{1,0:T(8,128)}) custom-call(bf16[320,10240]{1,0:T(8,128)(2,1)} %all-gather.2.cloned.1.call-done.refs_0_.y0.x0, bf16[5120,128]{1,0:T(8,128)(2,1)} %bitcast.14, bf16[5120,128]{1,0:T(8,128)(2,1)} %copy-done.5, ...), custom_call_target="tpu_custom_call" | custom-call | tf_op jit(solution)/shard_map/gate_up_part/pallas_call | solution.py:214
  117.0 4.3 %collective-permute-done.6.refs_2_ = bf16[128,5120]{1,0:T(8,128)(2,1)} collective-permute-done((bf16[128,5120]{1,0:T(8,128)(2,1)}, bf16[128,5120]{1,0:T(8,128)(2,1)}, u32[]{:S(2)}, u32[]{:S(2)}) %collective-permute-start.6) | collective-permute-done | bytes 1310752 | tf_op jit(solution)/shard_map/ppermute | solution.py:370
  121.3 0.0 collective-permute-start.8
  121.3 0.5 collective-permute-start.9
  121.8 0.0 collective-permute-start.10
  121.8 0.0 collective-permute-done.7.refs_3_
  121.9 4.6 %collective-permute-done.8.refs_4_ = bf16[128,5120]{1,0:T(8,128)(2,1)S(1)} collective-permute-done((bf16[128,5120]{1,0:T(8,128)(2,1)}, bf16[128,5120]{1,0:T(8,128)(2,1)S(1)}, u32[]{:S(2)}, u32[]{:S(2)}) %collective-permute-start.8) | collective-permute-done | bytes 1310752 | tf_op jit(solution)/shard_map/ppermute | solution.py:370
  126.4 0.0 copy-done.15
  126.4 1.1 copy-done.17
  127.5 6.5 %back_part.1 = (bf16[320,512]{1,0:T(8,128)(2,1)}, bf16[320,512]{1,0:T(8,128)(2,1)}, bf16[320,128]{1,0:T(8,128)(2,1)}) custom-call(bf16[320,10240]{1,0:T(8,128)(2,1)} %all-gather.2.cloned.1.call-done.refs_0_.y0.x0, bf16[128,5120]{1,0:T(8,128)(2,1)} %bitcast.25, bf16[128,5120]{1,0:T(8,128)(2,1)} %collective-permute-done.6.refs_2_, ...), custom_call_target="tpu_custom_call" | custom-call | flops 70000001024 | tf_op jit(solution)/shard_map/back_part/pallas_call | solution.py:263
  134.0 0.0 collective-permute-done.10.s1
  134.0 0.3 collective-permute-done.9.y1.x1
  134.3 0.3 copy-done.14
  134.6 4.5 %flat_part.2 = bf16[128,5120]{1,0:T(8,128)(2,1)} custom-call(bf16[320,10240]{1,0:T(8,128)(2,1)} %all-gather.2.cloned.1.call-done.refs_0_.y0.x0, bf16[320,10240]{1,0:T(8,128)(2,1)} %collective-permute-done.9.y1.x1, bf16[320,256]{1,0:T(8,128)(2,1)} %get-tuple-element.79.s0, bf16[320,256]{1,0:T(8,128)(2,1)} %copy-done.14), custom_call_target="tpu_custom_call" | custom-call | tf_op jit(solution)/shard_map/flat_part/pallas_call | solution.py:357
  139.1 1.5 collective-permute-start.12
  140.6 8.3 %input_part.1 = bf16[320,5248]{1,0:T(8,128)(2,1)} custom-call(bf16[320,512]{1,0:T(8,128)(2,1)} %get-tuple-element.82.here_ref.d0, bf16[320,512]{1,0:T(8,128)(2,1)} %get-tuple-element.71.there_ref, bf16[320,128]{1,0:T(8,128)(2,1)} %get-tuple-element.67.r_ref, bf16[5120,128]{1,0:T(8,128)(2,1)} %bitcast.15, bf16[5120,128]{1,0:T(8,128)(2,1)} %bitcast.19, ...), custom_call_target="tpu_custom_call" | custom-call | tf_op jit(solution)/shard_map/input_part/pallas_call | solution.py:302
  148.9 0.0 reduce-scatter.4.cloned.1.call-update
  149.0 0.9 copy-done.12
  149.9 0.0 collective-permute-start.11
  149.9 1.6 collective-permute-done.11.d1
  151.5 0.7 copy-done.13
  152.3 5.5 %tall_part.2 = (bf16[5120,128]{1,0:T(8,128)(2,1)}, bf16[5120,128]{1,0:T(8,128)(2,1)}) custom-call(bf16[320,10240]{1,0:T(8,128)(2,1)} %all-gather.2.cloned.1.call-done.refs_0_.y0.x0, bf16[320,10240]{1,0:T(8,128)(2,1)} %collective-permute-done.9.y1.x1, bf16[320,512]{1,0:T(8,128)(2,1)} %get-tuple-element.82.here_ref.d0, bf16[320,512]{1,0:T(8,128)(2,1)} %copy-done.13), custom_call_target="tpu_custom_call" | custom-call | tf_op jit(solution)/shard_map/tall_part/pallas_call | solution.py:327
  157.8 0.6 collective-permute-start.13
  158.3 1.5 collective-permute-start.14
  159.8 11.2 %collective-permute-done.12.rest_0_ = bf16[128,5120]{1,0:T(8,128)(2,1)S(1)} collective-permute-done((bf16[128,5120]{1,0:T(8,128)(2,1)}, bf16[128,5120]{1,0:T(8,128)(2,1)S(1)}, u32[]{:S(2)}, u32[]{:S(2)}) %collective-permute-start.12) | collective-permute-done | bytes 1310752 | tf_op jit(solution)/shard_map/ppermute | solution.py:370
  171.0 1.1 copy-done.16
  172.0 4.9 %flat_part.3 = bf16[128,5120]{1,0:T(8,128)(2,1)} custom-call(bf16[320,10240]{1,0:T(8,128)(2,1)} %all-gather.2.cloned.1.call-done.refs_0_.y0.x0, bf16[320,10240]{1,0:T(8,128)(2,1)} %collective-permute-done.9.y1.x1, bf16[320,256]{1,0:T(8,128)(2,1)} %get-tuple-element.79.s0, bf16[320,256]{1,0:T(8,128)(2,1)} %copy-done.14, bf16[128,5120]{1,0:T(8,128)(2,1)} %copy-done.16), custom_call_target="tpu_custom_call" | custom-call | flops 23000000512 | tf_op jit(solution)/shard_map/flat_part/pallas_call | solution.py:357
  177.0 6.1 %tall_part.3 = (f32[5120,128]{1,0:T(8,128)}, f32[5120,128]{1,0:T(8,128)}) custom-call(bf16[320,10240]{1,0:T(8,128)(2,1)} %all-gather.2.cloned.1.call-done.refs_0_.y0.x0, bf16[320,10240]{1,0:T(8,128)(2,1)} %collective-permute-done.9.y1.x1, bf16[320,512]{1,0:T(8,128)(2,1)} %get-tuple-element.82.here_ref.d0, bf16[320,512]{1,0:T(8,128)(2,1)} %copy-done.13), custom_call_target="tpu_custom_call" | custom-call | flops 23000000512 | tf_op jit(solution)/shard_map/tall_part/pallas_call | solution.py:327
  183.1 16.0 %collective-permute-done.13 = bf16[5120,128]{1,0:T(8,128)(2,1)S(1)} collective-permute-done((bf16[5120,128]{1,0:T(8,128)(2,1)}, bf16[5120,128]{1,0:T(8,128)(2,1)S(1)}, u32[]{:S(2)}, u32[]{:S(2)}) %collective-permute-start.13) | collective-permute-done | bytes 1310752 | tf_op jit(solution)/shard_map/ppermute | solution.py:370
  199.1 1.1 copy-done.11
  200.1 3.6 %fusion = bf16[1,5120,128]{2,1,0:T(8,128)(2,1)} fusion(f32[5120,128]{1,0:T(8,128)} %get-tuple-element.84, bf16[5120,128]{1,0:T(8,128)(2,1)} %copy-done.11), kind=kLoop, calls=%fused_computation.2 | loop fusion | flops 1966080 | bytes 5242880 | tf_op jit(solution)/shard_map/broadcast_in_dim | solution.py:415
  203.8 1.0 copy-done
  204.8 0.9 ship.1
  205.7 4.9 %all-to-all-start.1 = ((bf16[16,10,1408]{2,1,0:T(8,128)(2,1)}), bf16[16,10,1408]{2,1,0:T(8,128)(2,1)S(1)}, u32[]{:S(2)}, u32[]{:S(2)}) async-start(bf16[16,10,1408]{2,1,0:T(8,128)(2,1)} %ship.1), calls=%async_computation.1 | async-start | bytes 1441792 | tf_op jit(solution)/shard_map/all_to_all | solution.py:413
  210.6 16.7 %collective-permute-done.14 = bf16[5120,128]{1,0:T(8,128)(2,1)} collective-permute-done((bf16[5120,128]{1,0:T(8,128)(2,1)}, bf16[5120,128]{1,0:T(8,128)(2,1)}, u32[]{:S(2)}, u32[]{:S(2)}) %collective-permute-start.14) | collective-permute-done | bytes 1310752 | tf_op jit(solution)/shard_map/ppermute | solution.py:370
  227.3 2.7 %fusion.1 = bf16[1,5120,128]{2,1,0:T(8,128)(2,1)} fusion(f32[5120,128]{1,0:T(8,128)S(1)} %copy-done.10, bf16[5120,128]{1,0:T(8,128)(2,1)} %collective-permute-done.14), kind=kLoop, calls=%fused_computation.3 | loop fusion | flops 1966080 | bytes 5242880 | tf_op jit(solution)/shard_map/broadcast_in_dim | solution.py:415
  229.9 4.0 %all-to-all-done.1.land_ref = bf16[16,10,1408]{2,1,0:T(8,128)(2,1)S(1)} async-done(((bf16[16,10,1408]{2,1,0:T(8,128)(2,1)}), bf16[16,10,1408]{2,1,0:T(8,128)(2,1)S(1)}, u32[]{:S(2)}, u32[]{:S(2)}) %all-to-all-start.1) | async-done | bytes 450592 | tf_op jit(solution)/shard_map/all_to_all | solution.py:413
  234.0 1.0 take_home.1
  (24 shorter events, 0.0 us)
Async XLA Ops:
  7.2 101.7 %all-gather.2.cloned.1.call-start = ((), (), s32[]{:S(2)}) async-start(), calls=%async_computation.3 | async-start | bytes 7372800 | tf_op jit(solution)/shard_map/all_gather | solution.py:390
  9.8 24.0 %copy-start.4 = (bf16[1,5120,128]{2,1,0:T(8,128)(2,1)S(1)}, bf16[1,5120,128]{2,1,0:T(8,128)(2,1)}, u32[]{:S(2)}) copy-start(bf16[1,5120,128]{2,1,0:T(8,128)(2,1)} %param.12) | copy-start | bytes 3932164
  30.8 1.6 copy-start.3
  31.9 171.9 %reduce-scatter.4.cloned.1.call-start = ((), (), s32[]{:S(2)}) async-start(), calls=%async_computation.4 | async-start | bytes 3778560
  32.4 31.7 %collective-permute-start = (bf16[5120,128]{1,0:T(8,128)(2,1)S(1)}, bf16[5120,128]{1,0:T(8,128)(2,1)S(1)}, u32[]{:S(2)}, u32[]{:S(2)}) collective-permute-start(bf16[5120,128]{1,0:T(8,128)(2,1)S(1)} %bitcast.16), channel_id=1, source_target_pairs={{0,1},{1,0},{2,3},{3,2},{4,5},{5,4},{6,7},{7,6},{8,9},{9,8},{10,11... | collective-permute-start | bytes 3932168 | tf_op jit(solution)/shard_map/ppermute | solution.py:370
  33.8 56.0 %collective-permute-start.1 = (bf16[5120,128]{1,0:T(8,128)(2,1)S(1)}, bf16[5120,128]{1,0:T(8,128)(2,1)S(1)}, u32[]{:S(2)}, u32[]{:S(2)}) collective-permute-start(bf16[5120,128]{1,0:T(8,128)(2,1)S(1)} %bitcast.20), channel_id=1, source_target_pairs={{0,1},{1,0},{2,3},{3,2},{4,5},{5,4},{6,7},{7,6},{8,9},{9,8},{10,11... | collective-permute-start | bytes 3932168 | tf_op jit(solution)/shard_map/ppermute | solution.py:370
  34.4 56.9 %collective-permute-start.2 = (bf16[5120,128]{1,0:T(8,128)(2,1)S(1)}, bf16[5120,128]{1,0:T(8,128)(2,1)S(1)}, u32[]{:S(2)}, u32[]{:S(2)}) collective-permute-start(bf16[5120,128]{1,0:T(8,128)(2,1)S(1)} %bitcast.17), channel_id=1, source_target_pairs={{0,16},{16,0},{1,17},{17,1},{2,18},{18,2},{3,19},{19,3},{4,20},{20... | collective-permute-start | bytes 3932168 | tf_op jit(solution)/shard_map/ppermute | solution.py:370
  34.4 57.1 %collective-permute-start.3 = (bf16[5120,128]{1,0:T(8,128)(2,1)S(1)}, bf16[5120,128]{1,0:T(8,128)(2,1)S(1)}, u32[]{:S(2)}, u32[]{:S(2)}) collective-permute-start(bf16[5120,128]{1,0:T(8,128)(2,1)S(1)} %bitcast.21), channel_id=1, source_target_pairs={{0,16},{16,0},{1,17},{17,1},{2,18},{18,2},{3,19},{19,3},{4,20},{20... | collective-permute-start | bytes 3932168 | tf_op jit(solution)/shard_map/ppermute | solution.py:370
  64.1 27.4 %copy-start.5 = (bf16[5120,128]{1,0:T(8,128)(2,1)}, bf16[5120,128]{1,0:T(8,128)(2,1)S(1)}, u32[]{:S(2)}) copy-start(bf16[5120,128]{1,0:T(8,128)(2,1)S(1)} %collective-permute-done.refs_2_) | copy-start | bytes 3932164
  64.1 27.4 %collective-permute-start.4 = (bf16[5120,128]{1,0:T(8,128)(2,1)S(1)}, bf16[5120,128]{1,0:T(8,128)(2,1)S(1)}, u32[]{:S(2)}, u32[]{:S(2)}) collective-permute-start(bf16[5120,128]{1,0:T(8,128)(2,1)S(1)} %collective-permute-done.refs_2_), channel_id=1, source_target_pairs={{0,16},{16,0},{1,17},{17,1},{2,18},{18,2},{3,19},{19,3},{4,20},{20... | collective-permute-start | bytes 3932168 | tf_op jit(solution)/shard_map/ppermute | solution.py:370
  89.8 1.7 copy-start.6
  89.8 4.1 %collective-permute-start.5 = (bf16[5120,128]{1,0:T(8,128)(2,1)S(1)}, bf16[5120,128]{1,0:T(8,128)(2,1)}, u32[]{:S(2)}, u32[]{:S(2)}) collective-permute-start(bf16[5120,128]{1,0:T(8,128)(2,1)S(1)} %collective-permute-done.1.refs_6_.refs_3_), channel_id=1, source_target_pairs={{0,16},{16,0},{1,17},{17,1},{2,18},{18,2},{3,19},{19,3},{4,20},{20... | collective-permute-start | bytes 3932168 | tf_op jit(solution)/shard_map/ppermute | solution.py:370
  89.8 31.5 %collective-permute-start.6 = (bf16[128,5120]{1,0:T(8,128)(2,1)}, bf16[128,5120]{1,0:T(8,128)(2,1)}, u32[]{:S(2)}, u32[]{:S(2)}) collective-permute-start(bf16[128,5120]{1,0:T(8,128)(2,1)} %bitcast.23), channel_id=1, source_target_pairs={{0,1},{1,0},{2,3},{3,2},{4,5},{5,4},{6,7},{7,6},{8,9},{9,8},{10,11... | collective-permute-start | bytes 3932168 | tf_op jit(solution)/shard_map/ppermute | solution.py:370
  91.3 1.1 copy-start.7
  91.3 30.6 %collective-permute-start.7 = (bf16[128,5120]{1,0:T(8,128)(2,1)}, bf16[128,5120]{1,0:T(8,128)(2,1)S(1)}, u32[]{:S(2)}, u32[]{:S(2)}) collective-permute-start(bf16[128,5120]{1,0:T(8,128)(2,1)} %bitcast.24), channel_id=1, source_target_pairs={{0,16},{16,0},{1,17},{17,1},{2,18},{18,2},{3,19},{19,3},{4,20},{20... | collective-permute-start | bytes 3932168 | tf_op jit(solution)/shard_map/ppermute | solution.py:370
  91.5 1.3 copy-start.8
  92.8 1.1 copy-start.9
  121.3 5.1 %collective-permute-start.8 = (bf16[128,5120]{1,0:T(8,128)(2,1)}, bf16[128,5120]{1,0:T(8,128)(2,1)S(1)}, u32[]{:S(2)}, u32[]{:S(2)}) collective-permute-start(bf16[128,5120]{1,0:T(8,128)(2,1)} %collective-permute-done.6.refs_2_), channel_id=1, source_target_pairs={{0,16},{16,0},{1,17},{17,1},{2,18},{18,2},{3,19},{19,3},{4,20},{20... | collective-permute-start | bytes 3932168 | tf_op jit(solution)/shard_map/ppermute | solution.py:370
  121.3 13.0 %collective-permute-start.9 = (bf16[320,10240]{1,0:T(8,128)(2,1)}, bf16[320,10240]{1,0:T(8,128)(2,1)}, u32[]{:S(2)}, u32[]{:S(2)}) collective-permute-start(bf16[320,10240]{1,0:T(8,128)(2,1)} %all-gather.2.cloned.1.call-done.refs_0_.y0.x0), channel_id=1, source_target_pairs={{0,16},{16,0},{1,17},{17,1},{2,18},{18,2},{3,19},{19,3},{4,20},{20... | collective-permute-start | bytes 19660808 | tf_op jit(solution)/shard_map/ppermute | solution.py:370
  121.8 12.1 %collective-permute-start.10 = (bf16[320,256]{1,0:T(8,128)(2,1)}, bf16[320,256]{1,0:T(8,128)(2,1)S(1)}, u32[]{:S(2)}, u32[]{:S(2)}) collective-permute-start(bf16[320,256]{1,0:T(8,128)(2,1)} %get-tuple-element.66), channel_id=1, source_target_pairs={{0,16},{16,0},{1,17},{17,1},{2,18},{18,2},{3,19},{19,3},{4,20},{20... | collective-permute-start | bytes 491528 | tf_op jit(solution)/shard_map/ppermute | solution.py:370
  121.8 4.6 %copy-start.15 = (bf16[128,5120]{1,0:T(8,128)(2,1)}, bf16[128,5120]{1,0:T(8,128)(2,1)S(1)}, u32[]{:S(2)}) copy-start(bf16[128,5120]{1,0:T(8,128)(2,1)S(1)} %collective-permute-done.7.refs_3_) | copy-start | bytes 3932164
  126.4 1.1 copy-start.17
  134.0 0.7 copy-start.14
  139.1 31.8 %collective-permute-start.12 = (bf16[128,5120]{1,0:T(8,128)(2,1)}, bf16[128,5120]{1,0:T(8,128)(2,1)S(1)}, u32[]{:S(2)}, u32[]{:S(2)}) collective-permute-start(bf16[128,5120]{1,0:T(8,128)(2,1)} %flat_part.2), channel_id=1, source_target_pairs={{0,1},{1,0},{2,3},{3,2},{4,5},{5,4},{6,7},{7,6},{8,9},{9,8},{10,11... | collective-permute-start | bytes 3932168 | tf_op jit(solution)/shard_map/ppermute | solution.py:370
  148.9 1.0 copy-start.12
  149.9 1.6 collective-permute-start.11
  151.5 0.7 copy-start.13
  157.8 41.3 %collective-permute-start.13 = (bf16[5120,128]{1,0:T(8,128)(2,1)}, bf16[5120,128]{1,0:T(8,128)(2,1)S(1)}, u32[]{:S(2)}, u32[]{:S(2)}) collective-permute-start(bf16[5120,128]{1,0:T(8,128)(2,1)} %get-tuple-element.74), channel_id=1, source_target_pairs={{0,1},{1,0},{2,3},{3,2},{4,5},{5,4},{6,7},{7,6},{8,9},{9,8},{10,11... | collective-permute-start | bytes 3932168 | tf_op jit(solution)/shard_map/ppermute | solution.py:370
  158.3 68.9 %collective-permute-start.14 = (bf16[5120,128]{1,0:T(8,128)(2,1)}, bf16[5120,128]{1,0:T(8,128)(2,1)}, u32[]{:S(2)}, u32[]{:S(2)}) collective-permute-start(bf16[5120,128]{1,0:T(8,128)(2,1)} %get-tuple-element.90), channel_id=1, source_target_pairs={{0,1},{1,0},{2,3},{3,2},{4,5},{5,4},{6,7},{7,6},{8,9},{9,8},{10,11... | collective-permute-start | bytes 3932168 | tf_op jit(solution)/shard_map/ppermute | solution.py:370
  171.0 1.1 copy-start.16
  199.1 1.1 copy-start.11
  200.1 27.1 %copy-start.10 = (f32[5120,128]{1,0:T(8,128)S(1)}, f32[5120,128]{1,0:T(8,128)}, u32[]{:S(2)}) copy-start(f32[5120,128]{1,0:T(8,128)} %get-tuple-element.89) | copy-start | bytes 7864324
  203.8 1.0 copy-start
  205.7 28.3 %all-to-all-start.1 = ((bf16[16,10,1408]{2,1,0:T(8,128)(2,1)}), bf16[16,10,1408]{2,1,0:T(8,128)(2,1)S(1)}, u32[]{:S(2)}, u32[]{:S(2)}) async-start(bf16[16,10,1408]{2,1,0:T(8,128)(2,1)} %ship.1), calls=%async_computation.1 | async-start | bytes 1441792 | tf_op jit(solution)/shard_map/all_to_all | solution.py:413
  227.3 6.7 %copy-start.1 = (f32[128]{0:T(128)S(1)}, f32[128]{0:T(128)}, u32[]{:S(2)}) copy-start(f32[128]{0:T(128)} %param.9) | copy-start | bytes 1540
  227.3 6.7 %copy-start.2 = (s32[1,128]{1,0:T(1,128)S(1)}, s32[1,128]{1,0:T(1,128)}, u32[]{:S(2)}) copy-start(s32[1,128]{1,0:T(1,128)} %get-tuple-element.86.place_ref) | copy-start | bytes 1540
Sparse Core Ops, SparseCore 0:
  32.0 76.8 all-gather.1
  149.1 52.0 reduce-scatter.3

commit v4 on v3

--- a/solution.py
+++ b/solution.py
@@ -11,8 +11,7 @@
 PAD = 16
 LANES = 128
 BLOCK = 2560
-LONG = 70_000_000_000
-SHORT = 23_000_000_000
+SHORT = 34_590_000_000
 INNER = (((1,), (1,)), ((), ()))
 OUTER = (((0,), (0,)), ((), ()))
 F32 = jnp.float32
@@ -270,7 +269,7 @@
         + [whole((rows, 4 * unit))] * 2,
         out_specs=[whole((rows, 4 * unit))] * 2 + [whole((rows, LANES))],
         scratch_shapes=[pltpu.VMEM((rows, 4 * unit), F32)],
-        flops=LONG,
+
     )(both, *downs, gate, up)
 
 
@@ -383,22 +382,25 @@
     recv = lax.all_to_all(send, ("ctx", "tp"), split_axis=0, concat_axis=0, tiled=True)
     mine = arrange(recv, tokens_in.shape[1], n_ctx, n_tp)
     own = (gate_half[0], up_half[0], down_half[0])
-    other = tuple(flip(w, "tp") for w in after(own, recv))
+    cut = own[2].shape[0] // 2
+    gate, up, down = after(own, recv)
+    other = (flip(gate, "tp"), flip(up, "tp"))
+    most, late = flip(down[:cut], "tp"), flip(down[cut:], "tp")
     across = lambda group: tuple(flip(w, "core") for w in group)
     own_there = across(own)
-    sets = (own[:2], other[:2], own_there[:2], across(other[:2]))
+    sets = (own[:2], other, own_there[:2], across(other))
     here = lax.all_gather(mine, "z", axis=0, tiled=True)
-    here, sets = lax.optimization_barrier((here, sets))
+    here, sets, most = lax.optimization_barrier((here, sets, most))
     beside = flip(here, "core")
     both = (here, beside)
     s_here, s_there, gate, up = gate_up_part(here, sets)
-    down = after(other[2], s_here)
-    downs = (own[2], down, own_there[2], flip(down, "core"))
     s = (s_here, flip(s_there, "core"))
-    d_here, d_there, router = back_part(here, downs, gate, up)
-    give_down = flat_part(both, after(s, router), 1)
+    give_down = flat_part(both, s, 1)
     got_down = flip(give_down, "tp")
-    part = input_part(after(d_here, give_down), d_there, router, sets)
+    down = after((most, late), give_down)
+    downs = (own[2], *down, own_there[2], *across(down))
+    d_here, d_there, router = back_part(after(here, give_down), downs, gate, up)
+    part = input_part(d_here, d_there, router, sets)
     summed = lax.optimization_barrier(
         lax.psum_scatter(part, "z", scatter_dimension=0, tiled=True)
     )

time: 244 us -> 235 us (0.963)
  waiting for transfers between devices: 129 us -> 117 us
  starting transfers between devices: 13.2 us -> 17.4 us
    all_gather x1, waiting for transfers between devices: 15 us -> 0.01 us  [body(): here = lax.all_gather(mine, 'z', axis=0, tiled=True)]
    optimization_barrier x1, waiting for transfers between devices: 0.01 us -> 9.6 us  [after(): return lax.optimization_barrier((value, first))[0]]
    ppermute x15 -> x17, waiting for transfers between devices: 110 us -> 102 us  [flip(): return lax.ppermute(value, axis, [(i, i ^ 1) for i in range(count)])]
    unnamed x36 -> x34, local copies, waits for them, and re-layouts: 9 us -> 4.88 us
    slice x0 -> x1, local copies, waits for them, and re-layouts: none -> 2.72 us  [body(): most, late = (flip(down[:cut], 'tp'), flip(down[cut:], 'tp'))]
    ppermute x15 -> x17, starting transfers between devices: 8.23 us -> 10.1 us  [flip(): return lax.ppermute(value, axis, [(i, i ^ 1) for i in range(count)])]
  transfers between devices with their start and end apart: 18 -> 20, of which waited for: 11 -> 11; matrix products, arithmetic and copies ran while one was open for 3% -> 4% of each run, Pallas kernels for 17% -> 19%
where the time goes in v4:
time: 235 us; the launch traced here: 233 us
  waiting for transfers between devices  117 us (50%)
  Pallas kernels  49.8 us (21%)
  blocking collectives  20.9 us (9%)
  starting transfers between devices  17.4 us (7%)
  between operations  14.1 us (6%)
  local copies, waits for them, and re-layouts  7.6 us (3%)
  other arithmetic  6.21 us (3%)
    ppermute x17, waiting for transfers between devices, flip(): return lax.ppermute(value, axis, [(i, i ^ 1) for i in range(count)])  102 us
    all_to_all x1, blocking collectives, body(): lax.all_to_all(send, ('ctx', 'tp'), split_axis=0, concat_axis=0, tiled=True)  20.9 us
    pallas_call x2, Pallas kernels, tall_part(): call(tall_kernel, 'tall_part', [struct((width, unit), dtype)] * 2, grid=(...  11.5 us
    ppermute x17, starting transfers between devices, flip(): return lax.ppermute(value, axis, [(i, i ^ 1) for i in range(count)])  10.1 us
    optimization_barrier x1, waiting for transfers between devices, after(): return lax.optimization_barrier((value, first))[0]  9.6 us
    pallas_call x2, Pallas kernels, flat_part(): call(flat_kernel, 'flat_part', struct((unit, width), BF16), grid=(steps,)...  9.48 us
    pallas_call x1, Pallas kernels, input_part(): call(input_kernel, 'input_part', struct((rows, width + LANES), BF16), gri...  8.37 us
    pallas_call x1, Pallas kernels, gate_up_part(): call(gate_up_kernel, 'gate_up_part', [struct((rows, 2 * unit), BF16)] * 2...  8.21 us
  transfers between devices with their start and end apart: 20, of which 11 were waited for; matrix products, arithmetic and copies ran while one was open for 4% of the time, Pallas kernels for 19%

profile of v4, /device:TPU:2, one launch (start us, length us, event | category | flops | bytes accessed | tf_op | source)
XLA Modules:
  0.0 232.8 jit_solution(2584796919847854930)
XLA Ops:
  7.2 0.0 all-gather.2.cloned.1.call-start
  7.2 2.6 %spread.1 = (bf16[16,8,3200]{2,1,0:T(8,128)(2,1)}, s32[1,128]{1,0:T(1,128)}) custom-call(bf16[128,1280]{1,0:T(8,128)(2,1)} %refs_0_.1, bf16[128,1280]{1,0:T(8,128)(2,1)} %refs_1_.1, f32[1,128]{1,0:T(1,128)} %bitcast.12, s32[1,128]{1,0:T(1,128)} %bitcast.25), custom_call_target="tpu_custom_call" | custom-call | tf_op jit(solution)/shard_map/spread/pallas_call | solution.py:79
  9.8 20.9 %all_to_all.10.refs_0_ = bf16[16,8,3200]{2,1,0:T(8,128)(2,1)S(1)} all-to-all(bf16[16,8,3200]{2,1,0:T(8,128)(2,1)} %get-tuple-element.48), channel_id=1, replica_groups=mesh['z'=8,'core'=2,'ctx'=4,'tp'=4] {'ctx','tp'}, dimensions={0} | all-to-all | bytes 1638400 | tf_op jit(solution)/shard_map/all_to_all | solution.py:382
  30.8 1.1 arrange.1
  31.9 0.0 all-gather.2.cloned.1.call-update
  31.9 0.0 reduce-scatter.4.cloned.1.call-start
  31.9 0.4 copy-done.3
  32.4 1.5 collective-permute-start
  33.8 0.6 collective-permute-start.1
  34.4 0.0 collective-permute-start.2
  34.4 0.5 collective-permute-start.3
  34.9 29.2 %collective-permute-done.refs_2_ = bf16[5120,128]{1,0:T(8,128)(2,1)S(1)} collective-permute-done((bf16[5120,128]{1,0:T(8,128)(2,1)S(1)}, bf16[5120,128]{1,0:T(8,128)(2,1)S(1)}, u32[]{:S(2)}, u32[]{:S(2)}) %collective-permute-start) | collective-permute-done | bytes 1310752 | tf_op jit(solution)/shard_map/ppermute | solution.py:369
  64.1 0.0 collective-permute-start.4
  64.1 25.7 %collective-permute-done.1.refs_6_.refs_3_ = bf16[5120,128]{1,0:T(8,128)(2,1)S(1)} collective-permute-done((bf16[5120,128]{1,0:T(8,128)(2,1)S(1)}, bf16[5120,128]{1,0:T(8,128)(2,1)S(1)}, u32[]{:S(2)}, u32[]{:S(2)}) %collective-permute-start.1) | collective-permute-done | bytes 1310752 | tf_op jit(solution)/shard_map/ppermute | solution.py:369
  89.8 0.0 collective-permute-start.5
  89.8 2.7 %fusion.2 = (bf16[64,5120]{1,0:T(8,128)(2,1)}, bf16[64,5120]{1,0:T(8,128)(2,1)S(1)}) fusion(bf16[128,5120]{1,0:T(8,128)(2,1)} %bitcast.22), kind=kLoop, calls=%fused_computation.4 | loop fusion | bytes 2621440 | tf_op jit(solution)/shard_map/slice | solution.py:388
  92.6 1.5 collective-permute-start.6
  94.0 0.0 collective-permute-done.2.refs_3_.refs_4_
  94.0 0.0 collective-permute-done.3.refs_7_.refs_5_
  94.0 15.2 %collective-permute-done.6.refs_2_ = bf16[64,5120]{1,0:T(8,128)(2,1)S(1)} collective-permute-done((bf16[64,5120]{1,0:T(8,128)(2,1)S(1)}, bf16[64,5120]{1,0:T(8,128)(2,1)S(1)}, u32[]{:S(2)}, u32[]{:S(2)}) %collective-permute-start.6) | collective-permute-done | bytes 655392 | tf_op jit(solution)/shard_map/ppermute | solution.py:369
  109.2 0.0 collective-permute-done.4.refs_4_.refs_6_
  109.2 1.1 copy-done.9
  110.4 0.0 collective-permute-done.5.refs_8_.refs_7_
  110.4 0.0 collective-permute-start.7
  110.4 1.6 collective-permute-start.9
  111.9 0.2 collective-permute-start.10
  112.1 8.2 %gate_up_part.1 = (bf16[320,256]{1,0:T(8,128)(2,1)}, bf16[320,256]{1,0:T(8,128)(2,1)}, f32[320,512]{1,0:T(8,128)}, f32[320,512]{1,0:T(8,128)}) custom-call(bf16[320,10240]{1,0:T(8,128)(2,1)} %all-gather.2.cloned.1.call-done.refs_0_.y0.x0, bf16[5120,128]{1,0:T(8,128)(2,1)} %bitcast.14, bf16[5120,128]{1,0:T(8,128)(2,1)} %copy-done.5, ...), custom_call_target="tpu_custom_call" | custom-call | tf_op jit(solution)/shard_map/gate_up_part/pallas_call | solution.py:213
  120.3 0.4 collective-permute-start.8
  120.7 2.5 %collective-permute-done.8.s1 = bf16[320,256]{1,0:T(8,128)(2,1)S(1)} collective-permute-done((bf16[320,256]{1,0:T(8,128)(2,1)}, bf16[320,256]{1,0:T(8,128)(2,1)S(1)}, u32[]{:S(2)}, u32[]{:S(2)}) %collective-permute-start.8) | collective-permute-done | bytes 163872 | tf_op jit(solution)/shard_map/ppermute | solution.py:369
  123.2 0.0 collective-permute-done.7.y1.x1
  123.2 0.7 copy-done.16
  123.9 4.5 %flat_part.2 = bf16[128,5120]{1,0:T(8,128)(2,1)} custom-call(bf16[320,10240]{1,0:T(8,128)(2,1)} %all-gather.2.cloned.1.call-done.refs_0_.y0.x0, bf16[320,10240]{1,0:T(8,128)(2,1)} %collective-permute-done.7.y1.x1, bf16[320,256]{1,0:T(8,128)(2,1)} %get-tuple-element.79.s0, bf16[320,256]{1,0:T(8,128)(2,1)} %copy-done.16), custom_call_target="tpu_custom_call" | custom-call | tf_op jit(solution)/shard_map/flat_part/pallas_call | solution.py:356
  128.4 1.1 collective-permute-start.14
  129.5 0.0 collective-permute-done.9.refs_3_
  129.5 0.2 collective-permute-start.11
  129.7 0.4 collective-permute-start.12
  130.1 0.0 collective-permute-done.10.refs_4_
  130.1 1.6 collective-permute-done.11.refs_5_
  131.7 0.9 collective-permute-done.12.refs_6_
  132.7 0.9 copy-done.14
  133.5 0.0 copy-done.12
  133.6 6.5 %back_part.1 = (bf16[320,512]{1,0:T(8,128)(2,1)}, bf16[320,512]{1,0:T(8,128)(2,1)}, bf16[320,128]{1,0:T(8,128)(2,1)}) custom-call(bf16[320,10240]{1,0:T(8,128)(2,1)} %all-gather.2.cloned.1.call-done.refs_0_.y0.x0, bf16[128,5120]{1,0:T(8,128)(2,1)} %bitcast.24, bf16[64,5120]{1,0:T(8,128)(2,1)} %copy-done.11, bf16[64,5120]{1,0:T(8,128)(2,1)} %copy-done.12, ...), custom_call_target="tpu_custom_call" | custom-call | tf_op jit(solution)/shard_map/back_part/pallas_call | solution.py:262
  140.1 0.2 collective-permute-start.13
  140.3 8.4 %input_part.1 = bf16[320,5248]{1,0:T(8,128)(2,1)} custom-call(bf16[320,512]{1,0:T(8,128)(2,1)} %get-tuple-element.82.here_ref.d0, bf16[320,512]{1,0:T(8,128)(2,1)} %get-tuple-element.70.there_ref, bf16[320,128]{1,0:T(8,128)(2,1)} %get-tuple-element.71.r_ref, bf16[5120,128]{1,0:T(8,128)(2,1)} %bitcast.15, bf16[5120,128]{1,0:T(8,128)(2,1)} %bitcast.19, ...), custom_call_target="tpu_custom_call" | custom-call | tf_op jit(solution)/shard_map/input_part/pallas_call | solution.py:301
  148.7 0.0 reduce-scatter.4.cloned.1.call-update
  148.7 0.0 collective-permute-done.13.d1
  148.7 0.0 copy-start.15
  148.7 0.7 copy-done.15
  149.4 5.5 %tall_part.2 = (bf16[5120,128]{1,0:T(8,128)(2,1)}, bf16[5120,128]{1,0:T(8,128)(2,1)}) custom-call(bf16[320,10240]{1,0:T(8,128)(2,1)} %all-gather.2.cloned.1.call-done.refs_0_.y0.x0, bf16[320,10240]{1,0:T(8,128)(2,1)} %collective-permute-done.7.y1.x1, bf16[320,512]{1,0:T(8,128)(2,1)} %get-tuple-element.82.here_ref.d0, bf16[320,512]{1,0:T(8,128)(2,1)} %copy-done.15), custom_call_target="tpu_custom_call" | custom-call | tf_op jit(solution)/shard_map/tall_part/pallas_call | solution.py:326
  155.0 0.9 collective-permute-start.15
  155.9 1.1 collective-permute-start.16
  157.0 3.3 %collective-permute-done.14.rest_0_ = bf16[128,5120]{1,0:T(8,128)(2,1)} collective-permute-done((bf16[128,5120]{1,0:T(8,128)(2,1)}, bf16[128,5120]{1,0:T(8,128)(2,1)}, u32[]{:S(2)}, u32[]{:S(2)}) %collective-permute-start.14) | collective-permute-done | bytes 1310752 | tf_op jit(solution)/shard_map/ppermute | solution.py:369
  160.3 5.0 %flat_part.3 = bf16[128,5120]{1,0:T(8,128)(2,1)} custom-call(bf16[320,10240]{1,0:T(8,128)(2,1)} %all-gather.2.cloned.1.call-done.refs_0_.y0.x0, bf16[320,10240]{1,0:T(8,128)(2,1)} %collective-permute-done.7.y1.x1, bf16[320,256]{1,0:T(8,128)(2,1)} %get-tuple-element.79.s0, bf16[320,256]{1,0:T(8,128)(2,1)} %copy-done.16, ...), custom_call_target="tpu_custom_call" | custom-call | flops 34589999104 | tf_op jit(solution)/shard_map/flat_part/pallas_call | solution.py:356
  165.3 6.0 %tall_part.3 = (f32[5120,128]{1,0:T(8,128)}, f32[5120,128]{1,0:T(8,128)}) custom-call(bf16[320,10240]{1,0:T(8,128)(2,1)} %all-gather.2.cloned.1.call-done.refs_0_.y0.x0, bf16[320,10240]{1,0:T(8,128)(2,1)} %collective-permute-done.7.y1.x1, bf16[320,512]{1,0:T(8,128)(2,1)} %get-tuple-element.82.here_ref.d0, bf16[320,512]{1,0:T(8,128)(2,1)} %copy-done.15), custom_call_target="tpu_custom_call" | custom-call | flops 34589999104 | tf_op jit(solution)/shard_map/tall_part/pallas_call | solution.py:326
  171.3 17.0 %collective-permute-done.15 = bf16[5120,128]{1,0:T(8,128)(2,1)S(1)} collective-permute-done((bf16[5120,128]{1,0:T(8,128)(2,1)}, bf16[5120,128]{1,0:T(8,128)(2,1)S(1)}, u32[]{:S(2)}, u32[]{:S(2)}) %collective-permute-start.15) | collective-permute-done | bytes 1310752 | tf_op jit(solution)/shard_map/ppermute | solution.py:369
  188.3 3.1 %fusion = bf16[1,5120,128]{2,1,0:T(8,128)(2,1)} fusion(f32[5120,128]{1,0:T(8,128)} %get-tuple-element.84, bf16[5120,128]{1,0:T(8,128)(2,1)S(1)} %collective-permute-done.15), kind=kLoop, calls=%fused_computation.2 | loop fusion | flops 1966080 | bytes 5242880 | tf_op jit(solution)/shard_map/broadcast_in_dim | solution.py:417
  191.4 9.6 %reduce-scatter.4.cloned.1.call-done.refs_0_ = bf16[40,5248]{1,0:T(8,128)(2,1)} async-done(((bf16[320,5248]{1,0:T(8,128)(2,1)}), bf16[40,5248]{1,0:T(8,128)(2,1)}) %reduce-scatter.4.cloned.1.call-update) | async-done | bytes 419856 | tf_op jit(solution)/shard_map/optimization_barrier | solution.py:373
  201.0 1.0 copy-done
  202.0 0.9 ship.1
  202.9 7.2 %all-to-all-start.1 = ((bf16[16,10,1408]{2,1,0:T(8,128)(2,1)}), bf16[16,10,1408]{2,1,0:T(8,128)(2,1)S(1)}, u32[]{:S(2)}, u32[]{:S(2)}) async-start(bf16[16,10,1408]{2,1,0:T(8,128)(2,1)} %ship.1), calls=%async_computation.1 | async-start | bytes 1441792 | tf_op jit(solution)/shard_map/all_to_all | solution.py:415
  210.1 6.3 %collective-permute-done.16 = bf16[5120,128]{1,0:T(8,128)(2,1)S(1)} collective-permute-done((bf16[5120,128]{1,0:T(8,128)(2,1)}, bf16[5120,128]{1,0:T(8,128)(2,1)S(1)}, u32[]{:S(2)}, u32[]{:S(2)}) %collective-permute-start.16) | collective-permute-done | bytes 1310752 | tf_op jit(solution)/shard_map/ppermute | solution.py:369
  216.4 3.2 %fusion.1 = bf16[1,5120,128]{2,1,0:T(8,128)(2,1)} fusion(f32[5120,128]{1,0:T(8,128)} %get-tuple-element.89, bf16[5120,128]{1,0:T(8,128)(2,1)S(1)} %collective-permute-done.16), kind=kLoop, calls=%fused_computation.3 | loop fusion | flops 1966080 | bytes 5242880 | tf_op jit(solution)/shard_map/broadcast_in_dim | solution.py:417
  219.6 5.4 %all-to-all-done.1.land_ref = bf16[16,10,1408]{2,1,0:T(8,128)(2,1)S(1)} async-done(((bf16[16,10,1408]{2,1,0:T(8,128)(2,1)}), bf16[16,10,1408]{2,1,0:T(8,128)(2,1)S(1)}, u32[]{:S(2)}, u32[]{:S(2)}) %all-to-all-start.1) | async-done | bytes 450592 | tf_op jit(solution)/shard_map/all_to_all | solution.py:415
  225.0 1.0 take_home.1
  (27 shorter events, 0.0 us)
Async XLA Ops:
  7.2 103.2 %all-gather.2.cloned.1.call-start = ((), (), s32[]{:S(2)}) async-start(), calls=%async_computation.3 | async-start | bytes 7372800 | tf_op jit(solution)/shard_map/all_gather | solution.py:392
  9.8 24.0 %copy-start.4 = (bf16[1,5120,128]{2,1,0:T(8,128)(2,1)S(1)}, bf16[1,5120,128]{2,1,0:T(8,128)(2,1)}, u32[]{:S(2)}) copy-start(bf16[1,5120,128]{2,1,0:T(8,128)(2,1)} %param.12) | copy-start | bytes 3932164
  30.8 1.6 copy-start.3
  31.9 169.1 %reduce-scatter.4.cloned.1.call-start = ((), (), s32[]{:S(2)}) async-start(), calls=%async_computation.4 | async-start | bytes 3778560
  32.4 31.7 %collective-permute-start = (bf16[5120,128]{1,0:T(8,128)(2,1)S(1)}, bf16[5120,128]{1,0:T(8,128)(2,1)S(1)}, u32[]{:S(2)}, u32[]{:S(2)}) collective-permute-start(bf16[5120,128]{1,0:T(8,128)(2,1)S(1)} %bitcast.16), channel_id=1, source_target_pairs={{0,1},{1,0},{2,3},{3,2},{4,5},{5,4},{6,7},{7,6},{8,9},{9,8},{10,11... | collective-permute-start | bytes 3932168 | tf_op jit(solution)/shard_map/ppermute | solution.py:369
  33.8 56.0 %collective-permute-start.1 = (bf16[5120,128]{1,0:T(8,128)(2,1)S(1)}, bf16[5120,128]{1,0:T(8,128)(2,1)S(1)}, u32[]{:S(2)}, u32[]{:S(2)}) collective-permute-start(bf16[5120,128]{1,0:T(8,128)(2,1)S(1)} %bitcast.20), channel_id=1, source_target_pairs={{0,1},{1,0},{2,3},{3,2},{4,5},{5,4},{6,7},{7,6},{8,9},{9,8},{10,11... | collective-permute-start | bytes 3932168 | tf_op jit(solution)/shard_map/ppermute | solution.py:369
  34.4 59.6 %collective-permute-start.2 = (bf16[5120,128]{1,0:T(8,128)(2,1)S(1)}, bf16[5120,128]{1,0:T(8,128)(2,1)S(1)}, u32[]{:S(2)}, u32[]{:S(2)}) collective-permute-start(bf16[5120,128]{1,0:T(8,128)(2,1)S(1)} %bitcast.17), channel_id=1, source_target_pairs={{0,16},{16,0},{1,17},{17,1},{2,18},{18,2},{3,19},{19,3},{4,20},{20... | collective-permute-start | bytes 3932168 | tf_op jit(solution)/shard_map/ppermute | solution.py:369
  34.4 59.6 %collective-permute-start.3 = (bf16[5120,128]{1,0:T(8,128)(2,1)S(1)}, bf16[5120,128]{1,0:T(8,128)(2,1)S(1)}, u32[]{:S(2)}, u32[]{:S(2)}) collective-permute-start(bf16[5120,128]{1,0:T(8,128)(2,1)S(1)} %bitcast.21), channel_id=1, source_target_pairs={{0,16},{16,0},{1,17},{17,1},{2,18},{18,2},{3,19},{19,3},{4,20},{20... | collective-permute-start | bytes 3932168 | tf_op jit(solution)/shard_map/ppermute | solution.py:369
  64.1 28.5 %copy-start.5 = (bf16[5120,128]{1,0:T(8,128)(2,1)}, bf16[5120,128]{1,0:T(8,128)(2,1)S(1)}, u32[]{:S(2)}) copy-start(bf16[5120,128]{1,0:T(8,128)(2,1)S(1)} %collective-permute-done.refs_2_) | copy-start | bytes 3932164
  64.1 45.1 %collective-permute-start.4 = (bf16[5120,128]{1,0:T(8,128)(2,1)S(1)}, bf16[5120,128]{1,0:T(8,128)(2,1)S(1)}, u32[]{:S(2)}, u32[]{:S(2)}) collective-permute-start(bf16[5120,128]{1,0:T(8,128)(2,1)S(1)} %collective-permute-done.refs_2_), channel_id=1, source_target_pairs={{0,16},{16,0},{1,17},{17,1},{2,18},{18,2},{3,19},{19,3},{4,20},{20... | collective-permute-start | bytes 3932168 | tf_op jit(solution)/shard_map/ppermute | solution.py:369
  89.8 2.7 %copy-start.6 = (bf16[5120,128]{1,0:T(8,128)(2,1)}, bf16[5120,128]{1,0:T(8,128)(2,1)S(1)}, u32[]{:S(2)}) copy-start(bf16[5120,128]{1,0:T(8,128)(2,1)S(1)} %collective-permute-done.1.refs_6_.refs_3_) | copy-start | bytes 3932164
  89.8 20.5 %collective-permute-start.5 = (bf16[5120,128]{1,0:T(8,128)(2,1)S(1)}, bf16[5120,128]{1,0:T(8,128)(2,1)}, u32[]{:S(2)}, u32[]{:S(2)}) collective-permute-start(bf16[5120,128]{1,0:T(8,128)(2,1)S(1)} %collective-permute-done.1.refs_6_.refs_3_), channel_id=1, source_target_pairs={{0,16},{16,0},{1,17},{17,1},{2,18},{18,2},{3,19},{19,3},{4,20},{20... | collective-permute-start | bytes 3932168 | tf_op jit(solution)/shard_map/ppermute | solution.py:369
  92.6 16.7 %collective-permute-start.6 = (bf16[64,5120]{1,0:T(8,128)(2,1)S(1)}, bf16[64,5120]{1,0:T(8,128)(2,1)S(1)}, u32[]{:S(2)}, u32[]{:S(2)}) collective-permute-start(bf16[64,5120]{1,0:T(8,128)(2,1)S(1)} %get-tuple-element.92), channel_id=1, source_target_pairs={{0,1},{1,0},{2,3},{3,2},{4,5},{5,4},{6,7},{7,6},{8,9},{9,8},{10,11... | collective-permute-start | bytes 1966088 | tf_op jit(solution)/shard_map/ppermute | solution.py:369
  94.0 15.2 %copy-start.7 = (bf16[5120,128]{1,0:T(8,128)(2,1)}, bf16[5120,128]{1,0:T(8,128)(2,1)S(1)}, u32[]{:S(2)}) copy-start(bf16[5120,128]{1,0:T(8,128)(2,1)S(1)} %collective-permute-done.2.refs_3_.refs_4_) | copy-start | bytes 3932164
  94.0 15.2 %copy-start.8 = (bf16[5120,128]{1,0:T(8,128)(2,1)}, bf16[5120,128]{1,0:T(8,128)(2,1)S(1)}, u32[]{:S(2)}) copy-start(bf16[5120,128]{1,0:T(8,128)(2,1)S(1)} %collective-permute-done.3.refs_7_.refs_5_) | copy-start | bytes 3932164
  109.2 20.3 %copy-start.11 = (bf16[64,5120]{1,0:T(8,128)(2,1)}, bf16[64,5120]{1,0:T(8,128)(2,1)S(1)}, u32[]{:S(2)}) copy-start(bf16[64,5120]{1,0:T(8,128)(2,1)S(1)} %collective-permute-done.6.refs_2_) | copy-start | bytes 1966084
  109.2 1.1 copy-start.9
  110.4 12.9 %collective-permute-start.7 = (bf16[320,10240]{1,0:T(8,128)(2,1)}, bf16[320,10240]{1,0:T(8,128)(2,1)}, u32[]{:S(2)}, u32[]{:S(2)}) collective-permute-start(bf16[320,10240]{1,0:T(8,128)(2,1)} %all-gather.2.cloned.1.call-done.refs_0_.y0.x0), channel_id=1, source_target_pairs={{0,16},{16,0},{1,17},{17,1},{2,18},{18,2},{3,19},{19,3},{4,20},{20... | collective-permute-start | bytes 19660808 | tf_op jit(solution)/shard_map/ppermute | solution.py:369
  110.4 19.2 %collective-permute-start.9 = (bf16[64,5120]{1,0:T(8,128)(2,1)}, bf16[64,5120]{1,0:T(8,128)(2,1)S(1)}, u32[]{:S(2)}, u32[]{:S(2)}) collective-permute-start(bf16[64,5120]{1,0:T(8,128)(2,1)} %get-tuple-element.91), channel_id=1, source_target_pairs={{0,1},{1,0},{2,3},{3,2},{4,5},{5,4},{6,7},{7,6},{8,9},{9,8},{10,11... | collective-permute-start | bytes 1966088 | tf_op jit(solution)/shard_map/ppermute | solution.py:369
  111.9 18.2 %collective-permute-start.10 = (bf16[128,5120]{1,0:T(8,128)(2,1)}, bf16[128,5120]{1,0:T(8,128)(2,1)S(1)}, u32[]{:S(2)}, u32[]{:S(2)}) collective-permute-start(bf16[128,5120]{1,0:T(8,128)(2,1)} %bitcast.23), channel_id=1, source_target_pairs={{0,16},{16,0},{1,17},{17,1},{2,18},{18,2},{3,19},{19,3},{4,20},{20... | collective-permute-start | bytes 3932168 | tf_op jit(solution)/shard_map/ppermute | solution.py:369
  120.3 2.9 %collective-permute-start.8 = (bf16[320,256]{1,0:T(8,128)(2,1)}, bf16[320,256]{1,0:T(8,128)(2,1)S(1)}, u32[]{:S(2)}, u32[]{:S(2)}) collective-permute-start(bf16[320,256]{1,0:T(8,128)(2,1)} %get-tuple-element.62), channel_id=1, source_target_pairs={{0,16},{16,0},{1,17},{17,1},{2,18},{18,2},{3,19},{19,3},{4,20},{20... | collective-permute-start | bytes 491528 | tf_op jit(solution)/shard_map/ppermute | solution.py:369
  123.2 0.7 copy-start.16
  128.4 31.9 %collective-permute-start.14 = (bf16[128,5120]{1,0:T(8,128)(2,1)}, bf16[128,5120]{1,0:T(8,128)(2,1)}, u32[]{:S(2)}, u32[]{:S(2)}) collective-permute-start(bf16[128,5120]{1,0:T(8,128)(2,1)} %flat_part.2), channel_id=1, source_target_pairs={{0,1},{1,0},{2,3},{3,2},{4,5},{5,4},{6,7},{7,6},{8,9},{9,8},{10,11... | collective-permute-start | bytes 3932168 | tf_op jit(solution)/shard_map/ppermute | solution.py:369
  129.5 4.0 %copy-start.12 = (bf16[64,5120]{1,0:T(8,128)(2,1)}, bf16[64,5120]{1,0:T(8,128)(2,1)S(1)}, u32[]{:S(2)}) copy-start(bf16[64,5120]{1,0:T(8,128)(2,1)S(1)} %collective-permute-done.9.refs_3_) | copy-start | bytes 1966084
  129.5 2.2 collective-permute-start.11
  129.7 3.0 %collective-permute-start.12 = (bf16[64,5120]{1,0:T(8,128)(2,1)S(1)}, bf16[64,5120]{1,0:T(8,128)(2,1)S(1)}, u32[]{:S(2)}, u32[]{:S(2)}) collective-permute-start(bf16[64,5120]{1,0:T(8,128)(2,1)S(1)} %collective-permute-done.9.refs_3_), channel_id=1, source_target_pairs={{0,16},{16,0},{1,17},{17,1},{2,18},{18,2},{3,19},{19,3},{4,20},{20... | collective-permute-start | bytes 1966088 | tf_op jit(solution)/shard_map/ppermute | solution.py:369
  130.1 3.4 %copy-start.10 = (bf16[128,5120]{1,0:T(8,128)(2,1)}, bf16[128,5120]{1,0:T(8,128)(2,1)S(1)}, u32[]{:S(2)}) copy-start(bf16[128,5120]{1,0:T(8,128)(2,1)S(1)} %collective-permute-done.10.refs_4_) | copy-start | bytes 3932164
  131.7 1.8 copy-start.13
  132.7 0.9 copy-start.14
  140.1 8.6 %collective-permute-start.13 = (bf16[320,512]{1,0:T(8,128)(2,1)}, bf16[320,512]{1,0:T(8,128)(2,1)S(1)}, u32[]{:S(2)}, u32[]{:S(2)}) collective-permute-start(bf16[320,512]{1,0:T(8,128)(2,1)} %get-tuple-element.70.there_ref), channel_id=1, source_target_pairs={{0,16},{16,0},{1,17},{17,1},{2,18},{18,2},{3,19},{19,3},{4,20},{20... | collective-permute-start | bytes 983048 | tf_op jit(solution)/shard_map/ppermute | solution.py:369
  148.7 0.7 copy-start.15
  155.0 33.3 %collective-permute-start.15 = (bf16[5120,128]{1,0:T(8,128)(2,1)}, bf16[5120,128]{1,0:T(8,128)(2,1)S(1)}, u32[]{:S(2)}, u32[]{:S(2)}) collective-permute-start(bf16[5120,128]{1,0:T(8,128)(2,1)} %get-tuple-element.74), channel_id=1, source_target_pairs={{0,1},{1,0},{2,3},{3,2},{4,5},{5,4},{6,7},{7,6},{8,9},{9,8},{10,11... | collective-permute-start | bytes 3932168 | tf_op jit(solution)/shard_map/ppermute | solution.py:369
  155.9 60.5 %collective-permute-start.16 = (bf16[5120,128]{1,0:T(8,128)(2,1)}, bf16[5120,128]{1,0:T(8,128)(2,1)S(1)}, u32[]{:S(2)}, u32[]{:S(2)}) collective-permute-start(bf16[5120,128]{1,0:T(8,128)(2,1)} %get-tuple-element.90), channel_id=1, source_target_pairs={{0,1},{1,0},{2,3},{3,2},{4,5},{5,4},{6,7},{7,6},{8,9},{9,8},{10,11... | collective-permute-start | bytes 3932168 | tf_op jit(solution)/shard_map/ppermute | solution.py:369
  201.0 1.0 copy-start
  202.9 22.1 %all-to-all-start.1 = ((bf16[16,10,1408]{2,1,0:T(8,128)(2,1)}), bf16[16,10,1408]{2,1,0:T(8,128)(2,1)S(1)}, u32[]{:S(2)}, u32[]{:S(2)}) async-start(bf16[16,10,1408]{2,1,0:T(8,128)(2,1)} %ship.1), calls=%async_computation.1 | async-start | bytes 1441792 | tf_op jit(solution)/shard_map/all_to_all | solution.py:415
  216.4 8.6 %copy-start.1 = (f32[128]{0:T(128)S(1)}, f32[128]{0:T(128)}, u32[]{:S(2)}) copy-start(f32[128]{0:T(128)} %param.9) | copy-start | bytes 1540
  216.4 8.6 %copy-start.2 = (s32[1,128]{1,0:T(1,128)S(1)}, s32[1,128]{1,0:T(1,128)}, u32[]{:S(2)}) copy-start(s32[1,128]{1,0:T(1,128)} %get-tuple-element.86.place_ref) | copy-start | bytes 1540
Sparse Core Ops, SparseCore 0:
  32.0 76.8 all-gather.1
  148.8 52.0 reduce-scatter.3

commit v5 on v4

--- a/solution.py
+++ b/solution.py
@@ -11,6 +11,9 @@
 PAD = 16
 LANES = 128
 BLOCK = 2560
+PIECE = 640
+FAR = 3
+CHUNKS = 4
 SHORT = 34_590_000_000
 INNER = (((1,), (1,)), ((), ()))
 OUTER = (((0,), (0,)), ((), ()))
@@ -18,11 +21,11 @@
 BF16 = jnp.bfloat16
 
 
-def call(kernel, name, out_shape, vmem=60, flops=0, **kw):
+def call(kernel, name, out_shape, vmem=60 << 20, flops=0, **kw):
     return pl.pallas_call(
         kernel,
         out_shape=out_shape,
-        compiler_params=pltpu.CompilerParams(vmem_limit_bytes=vmem << 20),
+        compiler_params=pltpu.CompilerParams(vmem_limit_bytes=vmem),
         cost_estimate=pl.CostEstimate(flops=flops, bytes_accessed=0, transcendentals=0),
         name=name,
         **kw,
@@ -117,7 +120,7 @@
         lambda *refs: arrange_kernel(*refs, n_ctx=n_ctx, n_tp=n_tp),
         "arrange",
         struct((n_ctx * HALF, 2 * part * n_tp), BF16),
-        vmem=16,
+        vmem=16 << 20,
     )(recv)
 
 
@@ -142,7 +145,7 @@
         lambda *refs: ship_kernel(*refs, n_ctx=n_ctx, n_tp=n_tp),
         "ship",
         struct((n_ctx * n_tp, HALF, part + LANES), BF16),
-        vmem=16,
+        vmem=16 << 20,
     )(summed)
 
 
@@ -170,7 +173,7 @@
         home_kernel,
         "take_home",
         [struct((rows, part), BF16), struct((1, rows), BF16)],
-        vmem=16,
+        vmem=16 << 20,
     )(landed, place, logit)
 
 
@@ -178,160 +181,191 @@
     return jnp.concatenate([p[...] for p in parts], axis)
 
 
-def gate_up_kernel(*refs):
-    x_ref, gates, ups = refs[0], refs[1:5], refs[5:9]
-    here_ref, there_ref, gate_ref, up_ref = refs[9:]
-    step = pl.program_id(0)
-    x = x_ref[...]
-    gate_p = jnp.dot(x, join(gates, 1), preferred_element_type=F32)
-    up_p = jnp.dot(x, join(ups, 1), preferred_element_type=F32)
-
-    @pl.when(step == 0)
-    def _():
-        gate_ref[...] = gate_p
-        up_ref[...] = up_p
-
-    @pl.when(step > 0)
-    def _():
-        gate_ref[...] += gate_p
-        up_ref[...] += up_p
-
-    @pl.when(step == pl.num_programs(0) - 1)
-    def _():
-        half = here_ref.shape[1]
-        for n, out in enumerate((here_ref, there_ref)):
-            cols = slice(n * half, (n + 1) * half)
-            gate = gate_ref[:, cols]
-            out[...] = (gate * jax.nn.sigmoid(gate) * up_ref[:, cols]).astype(BF16)
+def gate_up_kernel(both_ref, *refs):
+    weights = refs[:8]
+    here_ref, there_ref, gate_ref, up_ref, x_v, w_v, sem = refs[8:]
+    width = x_v.shape[1]
+    groups = []
+    for k in range(CHUNKS):
+        size = width // CHUNKS
+        part = slice(k * size, (k + 1) * size)
+        pairs = [(both_ref.at[:, part], x_v.at[:, part])]
+        pairs += [(w.at[part], w_v.at[n, part]) for n, w in enumerate(weights)]
+        group = []
+        for n, (source, target) in enumerate(pairs):
+            group.append(pltpu.make_async_copy(source, target, sem.at[k * 9 + n]))
+            group[-1].start()
+        groups.append((part, group))
+    for k, (part, group) in enumerate(groups):
+        for copy in group:
+            copy.wait()
+        x = x_v[:, part]
+        for first, out in ((0, gate_ref), (4, up_ref)):
+            w = jnp.concatenate([w_v[first + n, part] for n in range(4)], 1)
+            some = jnp.dot(x, w, preferred_element_type=F32)
+            out[...] = some if k == 0 else out[...] + some
+    half = here_ref.shape[1]
+    for n, out in enumerate((here_ref, there_ref)):
+        cols = slice(n * half, (n + 1) * half)
+        gate = gate_ref[:, cols]
+        out[...] = (gate * jax.nn.sigmoid(gate) * up_ref[:, cols]).astype(BF16)
 
 
 def gate_up_part(both, sets):
     rows, wide = both.shape
     width = wide // 2
     unit = sets[0][0].shape[1]
-    tall = pl.BlockSpec((BLOCK, unit), lambda i: (i, 0))
+    near = pl.BlockSpec(memory_space=pltpu.VMEM)
     return call(
         gate_up_kernel,
         "gate_up_part",
         [struct((rows, 2 * unit), BF16)] * 2 + [struct((rows, 4 * unit), F32)] * 2,
-        grid=(width // BLOCK,),
-        in_specs=[pl.BlockSpec((rows, BLOCK), lambda i: (0, i))] + [tall] * 8,
-        out_specs=[whole((rows, 2 * unit))] * 2 + [whole((rows, 4 * unit))] * 2,
+        in_specs=[pl.BlockSpec(memory_space=pl.ANY)] * 9,
+        out_specs=[near] * 4,
+        scratch_shapes=[
+            pltpu.VMEM((rows, width), BF16),
+            pltpu.VMEM((8, width, unit), BF16),
+            pltpu.SemaphoreType.DMA((9 * CHUNKS,)),
+        ],
     )(both, *[s[0] for s in sets], *[s[1] for s in sets])
 
 
-def back_kernel(*refs):
-    dy_ref, downs = refs[0], refs[1:-6]
-    gate_ref, up_ref, here_ref, there_ref, r_ref, back_a = refs[-6:]
-    step = pl.program_id(0)
-    back_p = lax.dot_general(dy_ref[...], join(downs, 0), INNER, preferred_element_type=F32)
-
-    @pl.when(step == 0)
-    def _():
-        back_a[...] = back_p
-
-    @pl.when(step > 0)
-    def _():
-        back_a[...] += back_p
-
-    @pl.when(step == pl.num_programs(0) - 1)
-    def _():
-        unit = back_a.shape[1] // 4
-        total = jnp.zeros((back_a.shape[0], 1), F32)
-        for n in range(4):
-            cols = slice(n * unit, (n + 1) * unit)
-            gate = gate_ref[:, cols]
-            up = up_ref[:, cols]
-            back = back_a[:, cols]
-            sig = jax.nn.sigmoid(gate)
-            act = gate * sig
-            out = here_ref if n < 2 else there_ref
-            base = (n % 2) * 2 * unit
-            d_gate = back * up * sig * (1.0 + gate * (1.0 - sig))
-            out[:, base : base + unit] = d_gate.astype(BF16)
-            out[:, base + unit : base + 2 * unit] = (back * act).astype(BF16)
-            total = total + jnp.sum(act * up * back, axis=1, keepdims=True)
-        r_ref[...] = jnp.broadcast_to(total, r_ref.shape).astype(BF16)
-
-
-def back_part(both, downs, gate, up):
+def back_kernel(n_down, *refs):
+    both_ref, gate_ref, up_ref = refs[:3]
+    downs, weights = refs[3 : 3 + n_down], refs[3 + n_down : 11 + n_down]
+    part_ref, here_ref, there_ref = refs[11 + n_down : 14 + n_down]
+    dy_v, down_v, gate_v, up_v, w_v, out_v, in_sem, out_sem = refs[14 + n_down :]
+    rows, width = dy_v.shape
+    unit = gate_v.shape[1] // 4
+    count = [0]
+
+    def load(source, target):
+        copy = pltpu.make_async_copy(source, target, in_sem.at[count[0]])
+        copy.start()
+        count[0] += 1
+        return copy
+
+    first = []
+    for k in range(2):
+        size = width // 2
+        cols = slice(k * size, (k + 1) * size)
+        group = [load(both_ref.at[:, pl.ds(width + k * size, size)], dy_v.at[:, cols])]
+        at = 0
+        for w in downs:
+            group.append(load(w.at[:, cols], down_v.at[at : at + w.shape[0], cols]))
+            at += w.shape[0]
+        first.append((cols, group))
+    middle = [load(gate_ref, gate_v), load(up_ref, up_v)]
+    last = []
+    for k in range(4):
+        size = width // 4
+        cols = slice(k * size, (k + 1) * size)
+        last.append((cols, [load(w.at[cols], w_v.at[n, cols]) for n, w in enumerate(weights)]))
+    back = None
+    for cols, group in first:
+        for copy in group:
+            copy.wait()
+        some = lax.dot_general(dy_v[:, cols], down_v[:, cols], INNER, preferred_element_type=F32)
+        back = some if back is None else back + some
+    for copy in middle:
+        copy.wait()
+    total = jnp.zeros((rows, 1), F32)
+    for n in range(4):
+        cols = slice(n * unit, (n + 1) * unit)
+        gate = gate_v[:, cols]
+        up = up_v[:, cols]
+        value = back[:, cols]
+        sig = jax.nn.sigmoid(gate)
+        act = gate * sig
+        out = here_ref if n < 2 else there_ref
+        base = (n % 2) * 2 * unit
+        d_gate = value * up * sig * (1.0 + gate * (1.0 - sig))
+        out[:, base : base + unit] = d_gate.astype(BF16)
+        out[:, base + unit : base + 2 * unit] = (value * act).astype(BF16)
+        total = total + jnp.sum(act * up * value, axis=1, keepdims=True)
+    out_v[:, width:] = jnp.broadcast_to(total, (rows, LANES)).astype(BF16)
+    d = jnp.concatenate([here_ref[...], there_ref[...]], 1)
+    sent = []
+
+    def store(cols, k):
+        copy = pltpu.make_async_copy(out_v.at[:, cols], part_ref.at[:, cols], out_sem.at[k])
+        copy.start()
+        sent.append(copy)
+
+    store(slice(width, width + LANES), 4)
+    for k, (cols, group) in enumerate(last):
+        for copy in group:
+            copy.wait()
+        w = jnp.concatenate([w_v[n, cols] for n in range(8)], 1)
+        out_v[:, cols] = lax.dot_general(d, w, INNER, preferred_element_type=F32).astype(BF16)
+        store(cols, k)
+    for copy in sent:
+        copy.wait()
+
+
+def back_part(both, gate, up, downs, sets):
     rows, wide = both.shape
     width = wide // 2
     unit = gate.shape[1] // 4
-    steps = width // BLOCK
-    return call(
-        back_kernel,
+    weights = [w for s in sets for w in s]
+    operands = [both, gate, up, *downs, *weights]
+    anywhere = pl.BlockSpec(memory_space=pl.ANY)
+    near = pl.BlockSpec(memory_space=pltpu.VMEM)
+    return call(
+        lambda *refs: back_kernel(len(downs), *refs),
         "back_part",
-        [struct((rows, 4 * unit), BF16)] * 2 + [struct((rows, LANES), BF16)],
+        [struct((rows, width + LANES), BF16)] + [struct((rows, 4 * unit), BF16)] * 2,
+        in_specs=[anywhere] * len(operands),
+        out_specs=[anywhere, near, near],
+        scratch_shapes=[
+            pltpu.VMEM((rows, width), BF16),
+            pltpu.VMEM((4 * unit, width), BF16),
+            pltpu.VMEM((rows, 4 * unit), F32),
+            pltpu.VMEM((rows, 4 * unit), F32),
+            pltpu.VMEM((8, width, unit), BF16),
+            pltpu.VMEM((rows, width + LANES), BF16),
+            pltpu.SemaphoreType.DMA((2 * (1 + len(downs)) + 2 + 32,)),
+            pltpu.SemaphoreType.DMA((5,)),
+        ],
+    )(*operands)
+
+
+def tall_kernel(n_part, *refs):
+    gate_ref, up_ref = refs[-2:]
+    extra = refs[2 * n_part : -2]
+    unit = gate_ref.shape[1]
+    x = join(refs[:n_part], 0)
+    d = join(refs[n_part : 2 * n_part], 0)
+    out = lax.dot_general(x, d, OUTER, preferred_element_type=F32)
+    gate, up = out[:, :unit], out[:, unit:]
+    if extra:
+        gate = gate + extra[0][...].astype(F32)
+        up = up + extra[1][...].astype(F32)
+    gate_ref[...] = gate.astype(BF16)
+    up_ref[...] = up.astype(BF16)
+
+
+def tall_part(xs, ds, unit, start, steps, rows, addends=(), into=(), flops=0):
+    n = len(xs) + len(ds) + len(addends)
+    full = rows > steps * PIECE
+    return call(
+        lambda *refs: tall_kernel(len(xs), *refs[:n], *refs[-2:]),
+        "tall_part",
+        [struct((rows, unit), BF16)] * 2,
         grid=(steps,),
-        in_specs=[pl.BlockSpec((rows, BLOCK), lambda i: (0, i + steps))]
-        + [pl.BlockSpec((w.shape[0], BLOCK), lambda i: (0, i)) for w in downs]
-        + [whole((rows, 4 * unit))] * 2,
-        out_specs=[whole((rows, 4 * unit))] * 2 + [whole((rows, LANES))],
-        scratch_shapes=[pltpu.VMEM((rows, 4 * unit), F32)],
-
-    )(both, *downs, gate, up)
-
-
-def input_kernel(here_ref, there_ref, r_ref, *refs):
-    out_ref = refs[-1]
-    step = pl.program_id(0)
-    last = pl.num_programs(0) - 1
-
-    @pl.when(step < last)
-    def _():
-        weights = jnp.concatenate([w[...] for w in refs[:-1]], 1)
-        d = jnp.concatenate([here_ref[...], there_ref[...]], 1)
-        out_ref[...] = lax.dot_general(
-            d, weights, INNER, preferred_element_type=F32
-        ).astype(BF16)
-
-    @pl.when(step == last)
-    def _():
-        out_ref[:, :LANES] = r_ref[...]
-
-
-def input_part(here, there, router, sets):
-    rows = here.shape[0]
-    width, unit = sets[0][0].shape
-    steps = width // BLOCK
-    tall = pl.BlockSpec((BLOCK, unit), lambda i: (jnp.minimum(i, steps - 1), 0))
-    strip = pl.BlockSpec((rows, BLOCK), lambda i: (0, i))
-    weights = [w for s in sets for w in s]
-    return call(
-        input_kernel,
-        "input_part",
-        struct((rows, width + LANES), BF16),
-        grid=(steps + 1,),
-        in_specs=[whole((rows, 4 * unit))] * 2 + [whole((rows, LANES))] + [tall] * 8,
-        out_specs=strip,
-    )(here, there, router, *weights)
-
-
-def tall_kernel(x0, x1, d0, d1, gate_ref, up_ref):
-    unit = gate_ref.shape[1]
-    x = jnp.concatenate([x0[...], x1[...]], 0)
-    d = jnp.concatenate([d0[...], d1[...]], 0)
-    out = lax.dot_general(x, d, OUTER, preferred_element_type=F32)
-    gate_ref[...] = out[:, :unit].astype(gate_ref.dtype)
-    up_ref[...] = out[:, unit:].astype(up_ref.dtype)
-
-
-def tall_part(both, d, which, dtype, flops=0):
-    rows, wide = both[0].shape
-    width = wide // 2
-    unit = d[0].shape[1] // 4
-    x_spec = pl.BlockSpec((rows, BLOCK), lambda i: (0, i))
-    d_spec = pl.BlockSpec((rows, 2 * unit), lambda i: (0, which))
-    return call(
-        tall_kernel,
-        "tall_part",
-        [struct((width, unit), dtype)] * 2,
-        grid=(width // BLOCK,),
-        in_specs=[x_spec] * 2 + [d_spec] * 2,
-        out_specs=[pl.BlockSpec((BLOCK, unit), lambda i: (i, 0))] * 2,
+        in_specs=[
+            pl.BlockSpec(
+                (x.shape[0], PIECE), lambda i, far=x.shape[1] == FAR * PIECE: (0, i if far else start + i)
+            )
+            for x in xs
+        ]
+        + [pl.BlockSpec((d.shape[0], 2 * unit), lambda i, at=at: (0, at)) for d, at in ds]
+        + [pl.BlockSpec((PIECE, unit), lambda i: (i, 0))] * len(addends)
+        + [pl.BlockSpec(memory_space=pl.ANY)] * len(into),
+        out_specs=[pl.BlockSpec((PIECE, unit), lambda i: (start + i if full else i, 0))] * 2,
+        input_output_aliases={n + k: k for k in range(len(into))},
         flops=flops,
-    )(*both, *d)
+    )(*xs, *[d for d, _ in ds], *addends, *into)
 
 
 def flat_kernel(y0, y1, s0, s1, *rest):
@@ -382,13 +416,18 @@
     recv = lax.all_to_all(send, ("ctx", "tp"), split_axis=0, concat_axis=0, tiled=True)
     mine = arrange(recv, tokens_in.shape[1], n_ctx, n_tp)
     own = (gate_half[0], up_half[0], down_half[0])
-    cut = own[2].shape[0] // 2
-    gate, up, down = after(own, recv)
+    cut = 3 * PAD
+    far_mine = flip(mine[:, : FAR * PIECE], "tp")
+    gate, down = after((own[0], own[2]), recv)
+    up, first, second = lax.optimization_barrier((own[1], down[:cut], down[cut:]))
+    gate, far_mine = lax.optimization_barrier((gate, far_mine))
+    across = lambda group: tuple(flip(w, "core") for w in group)
     other = (flip(gate, "tp"), flip(up, "tp"))
-    most, late = flip(down[:cut], "tp"), flip(down[cut:], "tp")
-    across = lambda group: tuple(flip(w, "core") for w in group)
     own_there = across(own)
-    sets = (own[:2], other, own_there[:2], across(other))
+    gate_there = flip(other[0], "core")
+    first, own_there, gate_there = lax.optimization_barrier((first, own_there, gate_there))
+    most, late = flip(first, "tp"), flip(second, "tp")
+    sets = (own[:2], other, own_there[:2], (gate_there, flip(other[1], "core")))
     here = lax.all_gather(mine, "z", axis=0, tiled=True)
     here, sets, most = lax.optimization_barrier((here, sets, most))
     beside = flip(here, "core")
@@ -397,25 +436,34 @@
     s = (s_here, flip(s_there, "core"))
     give_down = flat_part(both, s, 1)
     got_down = flip(give_down, "tp")
-    down = after((most, late), give_down)
-    downs = (own[2], *down, own_there[2], *across(down))
-    d_here, d_there, router = back_part(after(here, give_down), downs, gate, up)
-    part = input_part(d_here, d_there, router, sets)
+    most = after(most, s_here)
+    late = after(late, give_down)
+    downs = (own[2], most, late, own_there[2], flip(most, "core"), flip(late, "core"))
+    part, d_here, d_there = back_part(after(here, give_down), gate, up, downs, sets)
+    far = lax.all_gather(far_mine, "z", axis=0, tiled=True)
+    part, far = lax.optimization_barrier((part, far))
     summed = lax.optimization_barrier(
         lax.psum_scatter(part, "z", scatter_dimension=0, tiled=True)
     )
+    far_beside = flip(far, "core")
     d = after((d_here, flip(d_there, "core")), part)
-    give = tall_part(both, d, 1, BF16)
+    width, unit = own[0].shape
+    steps = width // PIECE - FAR
+    give = tall_part(both, [(w, 1) for w in d], unit, FAR, steps, steps * PIECE)
     got = (flip(give[0], "tp"), flip(give[1], "tp"))
+    far_d = flip(jnp.concatenate([w[:, 2 * unit :] for w in d], 0), "tp")
     s, d, got_down = lax.optimization_barrier((s, after(d, give[0]), got_down))
     down_grad = flat_part(both, s, 0, got_down, SHORT)
-    keep = tall_part(both, after(d, down_grad), 0, F32, SHORT)
-    summed = after(summed, keep[0])
+    d, far_d = after((d, far_d), down_grad)
+    around = both + (far, far_beside)
+    d_all = [(w, 0) for w in (*d, *jnp.split(far_d, 2))]
+    top = tall_part(around, d_all, unit, 0, FAR, width, flops=SHORT)
+    tall_grads = tall_part(both, d_all[:2], unit, FAR, steps, width, got, top)
+    summed = after(summed, top[0])
     shipped = ship(summed, n_ctx, n_tp)
     landed = lax.all_to_all(shipped, ("ctx", "tp"), split_axis=0, concat_axis=0, tiled=True)
     input_grad, logit_grad = take_home(landed, place, logit)
-    tall_grads = tuple((k + g.astype(F32)).astype(BF16)[None] for k, g in zip(keep, got))
-    return (input_grad, logit_grad[0], *tall_grads, down_grad[None])
+    return input_grad, logit_grad[0], tall_grads[0][None], tall_grads[1][None], down_grad[None]
 
 
 def solution(mesh):

time: 235 us -> 229 us (0.974)
  other arithmetic: 6.21 us -> 0.02 us
  waiting for transfers between devices: 117 us -> 112 us
  Pallas kernels: 49.8 us -> 53.2 us
    broadcast_in_dim x2 -> x0, other arithmetic: 6.21 us -> none  [body(): (k + g.astype(F32)).astype(BF16)[None]]
    ppermute x17 -> x20, waiting for transfers between devices: 102 us -> 96.3 us  [flip(): return lax.ppermute(value, axis, [(i, i ^ 1) for i in range(count)])]
    pallas_call x4, Pallas kernels: 26.4 us -> 30.5 us  [the longest x3 17.5 us: tall_part(): call(lambda *refs: tall_kernel(len(xs), *refs[:n], *refs[-2:]), 'tall_par...]
    all_to_all x1, waiting for transfers between devices: 5.4 us -> 2.31 us  [body(): lax.all_to_all(shipped, ('ctx', 'tp'), split_axis=0, concat_axis=0, tiled...]
    ppermute x17 -> x20, starting transfers between devices: 10.1 us -> 12.4 us  [flip(): return lax.ppermute(value, axis, [(i, i ^ 1) for i in range(count)])]
    unnamed x34 -> x44, local copies, waits for them, and re-layouts: 4.88 us -> 6.67 us
  transfers between devices with their start and end apart: 20 -> 24, of which waited for: 11 -> 14; matrix products, arithmetic and copies ran while one was open for 4% -> 1% of each run, Pallas kernels for 19% -> 21%
where the time goes in v5:
time: 229 us; the launch traced here: 228 us
  waiting for transfers between devices  112 us (49%)
  Pallas kernels  53.2 us (23%)
  blocking collectives  20.8 us (9%)
  starting transfers between devices  19.6 us (9%)
  between operations  14 us (6%)
  local copies, waits for them, and re-layouts  8.46 us (4%)
    ppermute x20, waiting for transfers between devices, flip(): return lax.ppermute(value, axis, [(i, i ^ 1) for i in range(count)])  96.3 us
    all_to_all x1, blocking collectives, body(): lax.all_to_all(send, ('ctx', 'tp'), split_axis=0, concat_axis=0, tiled=True)  20.8 us
    pallas_call x3, Pallas kernels, tall_part(): call(lambda *refs: tall_kernel(len(xs), *refs[:n], *refs[-2:]), 'tall_par...  17.5 us
    pallas_call x1, Pallas kernels, back_part(): call(lambda *refs: back_kernel(len(downs), *refs), 'back_part', [struct((...  12.9 us
    ppermute x20, starting transfers between devices, flip(): return lax.ppermute(value, axis, [(i, i ^ 1) for i in range(count)])  12.4 us
    optimization_barrier x1, waiting for transfers between devices, after(): return lax.optimization_barrier((value, first))[0]  11.9 us
    pallas_call x2, Pallas kernels, flat_part(): call(flat_kernel, 'flat_part', struct((unit, width), BF16), grid=(steps,)...  9.67 us
    pallas_call x1, Pallas kernels, gate_up_part(): call(gate_up_kernel, 'gate_up_part', [struct((rows, 2 * unit), BF16)] * 2...  7.43 us
  transfers between devices with their start and end apart: 24, of which 14 were waited for; matrix products, arithmetic and copies ran while one was open for 1% of the time, Pallas kernels for 21%

profile of v5, /device:TPU:2, one launch (start us, length us, event | category | flops | bytes accessed | tf_op | source)
XLA Modules:
  0.0 228.2 jit_solution(6729750489759102435)
XLA Ops:
  7.2 0.0 all-gather.3.cloned.1.call-start
  7.2 2.6 %spread.1 = (bf16[16,8,3200]{2,1,0:T(8,128)(2,1)}, s32[1,128]{1,0:T(1,128)}) custom-call(bf16[128,1280]{1,0:T(8,128)(2,1)} %refs_0_.1, bf16[128,1280]{1,0:T(8,128)(2,1)} %refs_1_.1, f32[1,128]{1,0:T(1,128)} %bitcast.10, s32[1,128]{1,0:T(1,128)} %bitcast.26), custom_call_target="tpu_custom_call" | custom-call | tf_op jit(solution)/shard_map/spread/pallas_call | solution.py:82
  9.8 20.8 %all_to_all.10.refs_0_ = bf16[16,8,3200]{2,1,0:T(8,128)(2,1)S(1)} all-to-all(bf16[16,8,3200]{2,1,0:T(8,128)(2,1)} %get-tuple-element.62), channel_id=1, replica_groups=mesh['z'=8,'core'=2,'ctx'=4,'tp'=4] {'ctx','tp'}, dimensions={0} | all-to-all | bytes 1638400 | tf_op jit(solution)/shard_map/all_to_all | solution.py:416
  30.6 1.1 arrange.1
  31.7 0.0 all-gather.3.cloned.1.call-update
  31.8 0.0 all-gather.5.cloned.1.call-start
  31.8 0.9 slice.20
  32.7 1.5 collective-permute-start
  34.3 3.9 %collective-permute-done = bf16[40,1920]{1,0:T(8,128)(2,1)} collective-permute-done((bf16[40,1920]{1,0:T(8,128)(2,1)S(1)}, bf16[40,1920]{1,0:T(8,128)(2,1)}, u32[]{:S(2)}, u32[]{:S(2)}) %collective-permute-start) | collective-permute-done | bytes 153632 | tf_op jit(solution)/shard_map/ppermute | solution.py:403
  38.1 1.5 collective-permute-start.1
  39.6 0.1 slice.17
  39.7 1.2 collective-permute-start.2
  40.9 0.5 collective-permute-start.4
  41.4 0.0 collective-permute-start.5
  41.4 28.4 %collective-permute-done.1.refs_1_.refs_11_ = bf16[5120,128]{1,0:T(8,128)(2,1)S(1)} collective-permute-done((bf16[5120,128]{1,0:T(8,128)(2,1)S(1)}, bf16[5120,128]{1,0:T(8,128)(2,1)S(1)}, u32[]{:S(2)}, u32[]{:S(2)}) %collective-permute-start.1) | collective-permute-done | bytes 1310752 | tf_op jit(solution)/shard_map/ppermute | solution.py:403
  69.9 0.0 collective-permute-start.6
  69.9 24.6 %collective-permute-done.2.refs_5_.refs_12_ = bf16[5120,128]{1,0:T(8,128)(2,1)S(1)} collective-permute-done((bf16[5120,128]{1,0:T(8,128)(2,1)S(1)}, bf16[5120,128]{1,0:T(8,128)(2,1)S(1)}, u32[]{:S(2)}, u32[]{:S(2)}) %collective-permute-start.2) | collective-permute-done | bytes 1310752 | tf_op jit(solution)/shard_map/ppermute | solution.py:403
  94.5 0.0 collective-permute-start.7
  94.5 0.0 copy-start.7
  94.5 1.0 copy-done.6
  95.5 1.5 collective-permute-start.8
  97.0 0.5 collective-permute-done.7.refs_7_.refs_16_
  97.5 1.1 copy-done.10
  98.6 9.7 %collective-permute-done.8.refs_4_ = bf16[48,5120]{1,0:T(8,128)(2,1)S(1)} collective-permute-done((bf16[48,5120]{1,0:T(8,128)(2,1)S(1)}, bf16[48,5120]{1,0:T(8,128)(2,1)S(1)}, u32[]{:S(2)}, u32[]{:S(2)}) %collective-permute-start.8) | collective-permute-done | bytes 491552 | tf_op jit(solution)/shard_map/ppermute | solution.py:403
  108.3 0.5 all-gather.3.cloned.1.call-done.both_ref.y0.refs_0_
  108.8 0.0 all-gather.5.cloned.1.call-update
  108.8 0.0 reduce-scatter.4.cloned.1.call-start
  108.8 1.1 collective-permute-start.11
  109.9 7.4 %gate_up_part.1 = (bf16[320,256]{1,0:T(8,128)(2,1)}, bf16[320,256]{1,0:T(8,128)(2,1)}, f32[320,512]{1,0:T(8,128)}, f32[320,512]{1,0:T(8,128)}) custom-call(bf16[320,10240]{1,0:T(8,128)(2,1)} %all-gather.3.cloned.1.call-done.both_ref.y0.refs_0_, bf16[5120,128]{1,0:T(8,128)(2,1)} %bitcast.12, bf16[5120,128]{1,0:T(8,128)(2,1)} %copy-done.5, ...), custom_call_target="tpu_custom_call" | custom-call | tf_op jit(solution)/shard_map/gate_up_part/pallas_call | solution.py:219
  117.3 0.3 collective-permute-start.10
  117.6 2.1 collective-permute-done.10.s1
  119.7 0.7 copy-done.21
  120.4 4.5 %flat_part.2 = bf16[128,5120]{1,0:T(8,128)(2,1)} custom-call(bf16[320,10240]{1,0:T(8,128)(2,1)} %all-gather.3.cloned.1.call-done.both_ref.y0.refs_0_, bf16[320,10240]{1,0:T(8,128)(2,1)} %collective-permute-done.9.y1.refs_1_, bf16[320,256]{1,0:T(8,128)(2,1)} %get-tuple-element.104.s0, bf16[320,256]{1,0:T(8,128)(2,1)} %copy-done.21), custom_call_target="tpu_custom_call" | custom-call | tf_op jit(solution)/shard_map/flat_part/pallas_call | solution.py:390
  124.9 1.0 collective-permute-start.16
  125.9 4.1 %collective-permute-done.11.refs_5_ = bf16[80,5120]{1,0:T(8,128)(2,1)S(1)} collective-permute-done((bf16[80,5120]{1,0:T(8,128)(2,1)S(1)}, bf16[80,5120]{1,0:T(8,128)(2,1)S(1)}, u32[]{:S(2)}, u32[]{:S(2)}) %collective-permute-start.11) | collective-permute-done | bytes 819232 | tf_op jit(solution)/shard_map/ppermute | solution.py:403
  130.0 0.0 collective-permute-start.13
  130.0 0.5 collective-permute-start.12
  130.5 2.5 %collective-permute-done.12.refs_7_ = bf16[48,5120]{1,0:T(8,128)(2,1)S(1)} collective-permute-done((bf16[48,5120]{1,0:T(8,128)(2,1)S(1)}, bf16[48,5120]{1,0:T(8,128)(2,1)S(1)}, u32[]{:S(2)}, u32[]{:S(2)}) %collective-permute-start.12) | collective-permute-done | bytes 491552 | tf_op jit(solution)/shard_map/ppermute | solution.py:403
  133.0 0.8 copy-done.20
  133.8 0.2 copy-done.18
  134.1 12.9 %back_part.1 = (bf16[320,5248]{1,0:T(8,128)(2,1)}, bf16[320,512]{1,0:T(8,128)(2,1)}, bf16[320,512]{1,0:T(8,128)(2,1)}) custom-call(bf16[320,10240]{1,0:T(8,128)(2,1)} %all-gather.3.cloned.1.call-done.both_ref.y0.refs_0_, f32[320,512]{1,0:T(8,128)} %get-tuple-element.84.refs_1_, f32[320,512]{1,0:T(8,128)} %get-tuple-element.85.refs_2_, ...), custom_call_target="tpu_custom_call" | custom-call | tf_op jit(solution)/shard_map/back_part/pallas_call | solution.py:314
  147.0 0.3 collective-permute-start.15
  147.2 1.1 all-gather.5.cloned.1.call-done.refs_2_
  148.3 0.0 reduce-scatter.4.cloned.1.call-update
  148.4 0.6 collective-permute-done.15.refs_3_.refs_5_
  148.9 0.4 copy-done.12
  149.4 0.3 copy-done.13
  149.7 5.9 %tall_part.3 = (bf16[3200,128]{1,0:T(8,128)(2,1)}, bf16[3200,128]{1,0:T(8,128)(2,1)}) custom-call(bf16[320,10240]{1,0:T(8,128)(2,1)} %all-gather.3.cloned.1.call-done.both_ref.y0.refs_0_, bf16[320,10240]{1,0:T(8,128)(2,1)} %collective-permute-done.9.y1.refs_1_, bf16[320,512]{1,0:T(8,128)(2,1)} %get-tuple-element.107.refs_2_.refs_4_, bf16[320,512]{1,0:T(8,128)(2,1)} %copy-done.13), custom_call_target="tpu_custom_call" | custom-call | tf_op jit(solution)/shard_map/tall_part/pallas_call | solution.py:351
  155.6 1.0 collective-permute-start.18
  156.6 1.1 collective-permute-start.17
  157.7 1.0 collective-permute-start.19
  158.7 5.2 %flat_part.3 = bf16[128,5120]{1,0:T(8,128)(2,1)} custom-call(bf16[320,10240]{1,0:T(8,128)(2,1)} %all-gather.3.cloned.1.call-done.both_ref.y0.refs_0_, bf16[320,10240]{1,0:T(8,128)(2,1)} %collective-permute-done.9.y1.refs_1_, bf16[320,256]{1,0:T(8,128)(2,1)} %get-tuple-element.104.s0, bf16[320,256]{1,0:T(8,128)(2,1)} %copy-done.21, ...), custom_call_target="tpu_custom_call" | custom-call | flops 34589999104 | tf_op jit(solution)/shard_map/flat_part/pallas_call | solution.py:390
  163.9 20.0 %collective-permute-done.17 = bf16[640,256]{1,0:T(8,128)(2,1)S(1)} collective-permute-done((bf16[640,256]{1,0:T(8,128)(2,1)S(1)}, bf16[640,256]{1,0:T(8,128)(2,1)S(1)}, u32[]{:S(2)}, u32[]{:S(2)}) %collective-permute-start.17) | collective-permute-done | bytes 327712 | tf_op jit(solution)/shard_map/ppermute | solution.py:403
  183.9 0.8 fusion
  184.7 5.2 %tall_part.4 = (bf16[5120,128]{1,0:T(8,128)(2,1)}, bf16[5120,128]{1,0:T(8,128)(2,1)}) custom-call(bf16[320,10240]{1,0:T(8,128)(2,1)} %all-gather.3.cloned.1.call-done.both_ref.y0.refs_0_, bf16[320,10240]{1,0:T(8,128)(2,1)} %collective-permute-done.9.y1.refs_1_, bf16[320,1920]{1,0:T(8,128)(2,1)} %all-gather.5.cloned.1.call-done.refs_2_, ...), custom_call_target="tpu_custom_call" | custom-call | flops 34589999104 | tf_op jit(solution)/shard_map/tall_part/pallas_call | solution.py:351
  189.9 11.9 %reduce-scatter.4.cloned.1.call-done.refs_0_ = bf16[40,5248]{1,0:T(8,128)(2,1)} async-done(((bf16[320,5248]{1,0:T(8,128)(2,1)}), bf16[40,5248]{1,0:T(8,128)(2,1)}) %reduce-scatter.4.cloned.1.call-update) | async-done | bytes 419856 | tf_op jit(solution)/shard_map/optimization_barrier | solution.py:407
  201.8 1.0 copy-done
  202.9 0.9 ship.1
  203.8 7.0 %all-to-all-start.1 = ((bf16[16,10,1408]{2,1,0:T(8,128)(2,1)}), bf16[16,10,1408]{2,1,0:T(8,128)(2,1)S(1)}, u32[]{:S(2)}, u32[]{:S(2)}) async-start(bf16[16,10,1408]{2,1,0:T(8,128)(2,1)} %ship.1), calls=%async_computation.1 | async-start | bytes 1441792 | tf_op jit(solution)/shard_map/all_to_all | solution.py:464
  210.9 0.9 copy-done.15
  211.7 0.3 copy-done.16
  212.0 6.4 %tall_part.5 = (bf16[5120,128]{1,0:T(8,128)(2,1)}, bf16[5120,128]{1,0:T(8,128)(2,1)}) custom-call(bf16[320,10240]{1,0:T(8,128)(2,1)} %all-gather.3.cloned.1.call-done.both_ref.y0.refs_0_, bf16[320,10240]{1,0:T(8,128)(2,1)} %collective-permute-done.9.y1.refs_1_, ...), custom_call_target="tpu_custom_call", output_to_operand_aliasing={{0}: (6, {}), {1}: (7, {})} | custom-call | tf_op jit(solution)/shard_map/tall_part/pallas_call | solution.py:351
  218.3 2.3 %all-to-all-done.1.land_ref = bf16[16,10,1408]{2,1,0:T(8,128)(2,1)S(1)} async-done(((bf16[16,10,1408]{2,1,0:T(8,128)(2,1)}), bf16[16,10,1408]{2,1,0:T(8,128)(2,1)S(1)}, u32[]{:S(2)}, u32[]{:S(2)}) %all-to-all-start.1) | async-done | bytes 450592 | tf_op jit(solution)/shard_map/all_to_all | solution.py:464
  220.7 1.0 take_home.1
  (50 shorter events, 0.2 us)
Async XLA Ops:
  7.2 101.6 %all-gather.3.cloned.1.call-start = ((), (), s32[]{:S(2)}) async-start(), calls=%async_computation.3 | async-start | bytes 7372800 | tf_op jit(solution)/shard_map/all_gather | solution.py:431
  30.6 7.5 %copy-start.3 = (bf16[1,5120,128]{2,1,0:T(8,128)(2,1)S(1)}, bf16[1,5120,128]{2,1,0:T(8,128)(2,1)}, u32[]{:S(2)}) copy-start(bf16[1,5120,128]{2,1,0:T(8,128)(2,1)} %param.11) | copy-start | bytes 3932164
  30.6 9.0 %copy-start.11 = (bf16[1,128,5120]{2,1,0:T(8,128)(2,1)S(1)}, bf16[1,128,5120]{2,1,0:T(8,128)(2,1)}, u32[]{:S(2)}) copy-start(bf16[1,128,5120]{2,1,0:T(8,128)(2,1)} %param.13) | copy-start | bytes 3932164
  31.8 116.6 %all-gather.5.cloned.1.call-start = ((), (), s32[]{:S(2)}) async-start(), calls=%async_computation.4 | async-start | bytes 1382400 | tf_op jit(solution)/shard_map/all_gather | solution.py:443
  32.7 5.4 %collective-permute-start = (bf16[40,1920]{1,0:T(8,128)(2,1)S(1)}, bf16[40,1920]{1,0:T(8,128)(2,1)}, u32[]{:S(2)}, u32[]{:S(2)}) collective-permute-start(bf16[40,1920]{1,0:T(8,128)(2,1)S(1)} %slice.20), channel_id=1, source_target_pairs={{0,1},{1,0},{2,3},{3,2},{4,5},{5,4},{6,7},{7,6},{8,9},{9,8},{10,11... | collective-permute-start | bytes 460808 | tf_op jit(solution)/shard_map/ppermute | solution.py:403
  38.1 1.6 copy-start.4
  38.1 31.7 %collective-permute-start.1 = (bf16[5120,128]{1,0:T(8,128)(2,1)S(1)}, bf16[5120,128]{1,0:T(8,128)(2,1)S(1)}, u32[]{:S(2)}, u32[]{:S(2)}) collective-permute-start(bf16[5120,128]{1,0:T(8,128)(2,1)S(1)} %bitcast.14), channel_id=1, source_target_pairs={{0,1},{1,0},{2,3},{3,2},{4,5},{5,4},{6,7},{7,6},{8,9},{9,8},{10,11... | collective-permute-start | bytes 3932168 | tf_op jit(solution)/shard_map/ppermute | solution.py:403
  39.7 54.7 %collective-permute-start.2 = (bf16[5120,128]{1,0:T(8,128)(2,1)S(1)}, bf16[5120,128]{1,0:T(8,128)(2,1)S(1)}, u32[]{:S(2)}, u32[]{:S(2)}) collective-permute-start(bf16[5120,128]{1,0:T(8,128)(2,1)S(1)} %bitcast.18), channel_id=1, source_target_pairs={{0,1},{1,0},{2,3},{3,2},{4,5},{5,4},{6,7},{7,6},{8,9},{9,8},{10,11... | collective-permute-start | bytes 3932168 | tf_op jit(solution)/shard_map/ppermute | solution.py:403
  40.9 53.5 %collective-permute-start.3 = (bf16[5120,128]{1,0:T(8,128)(2,1)S(1)}, bf16[5120,128]{1,0:T(8,128)(2,1)S(1)}, u32[]{:S(2)}, u32[]{:S(2)}) collective-permute-start(bf16[5120,128]{1,0:T(8,128)(2,1)S(1)} %bitcast.15), channel_id=1, source_target_pairs={{0,16},{16,0},{1,17},{17,1},{2,18},{18,2},{3,19},{19,3},{4,20},{20... | collective-permute-start | bytes 3932168 | tf_op jit(solution)/shard_map/ppermute | solution.py:403
  40.9 53.6 %collective-permute-start.4 = (bf16[5120,128]{1,0:T(8,128)(2,1)S(1)}, bf16[5120,128]{1,0:T(8,128)(2,1)S(1)}, u32[]{:S(2)}, u32[]{:S(2)}) collective-permute-start(bf16[5120,128]{1,0:T(8,128)(2,1)S(1)} %bitcast.19), channel_id=1, source_target_pairs={{0,16},{16,0},{1,17},{17,1},{2,18},{18,2},{3,19},{19,3},{4,20},{20... | collective-permute-start | bytes 3932168 | tf_op jit(solution)/shard_map/ppermute | solution.py:403
  41.4 53.1 %collective-permute-start.5 = (bf16[128,5120]{1,0:T(8,128)(2,1)S(1)}, bf16[128,5120]{1,0:T(8,128)(2,1)S(1)}, u32[]{:S(2)}, u32[]{:S(2)}) collective-permute-start(bf16[128,5120]{1,0:T(8,128)(2,1)S(1)} %bitcast.23), channel_id=1, source_target_pairs={{0,16},{16,0},{1,17},{17,1},{2,18},{18,2},{3,19},{19,3},{4,20},{20... | collective-permute-start | bytes 3932168 | tf_op jit(solution)/shard_map/ppermute | solution.py:403
  69.9 24.6 %copy-start.5 = (bf16[5120,128]{1,0:T(8,128)(2,1)}, bf16[5120,128]{1,0:T(8,128)(2,1)S(1)}, u32[]{:S(2)}) copy-start(bf16[5120,128]{1,0:T(8,128)(2,1)S(1)} %collective-permute-done.1.refs_1_.refs_11_) | copy-start | bytes 3932164
  69.9 24.7 %collective-permute-start.6 = (bf16[5120,128]{1,0:T(8,128)(2,1)S(1)}, bf16[5120,128]{1,0:T(8,128)(2,1)S(1)}, u32[]{:S(2)}, u32[]{:S(2)}) collective-permute-start(bf16[5120,128]{1,0:T(8,128)(2,1)S(1)} %collective-permute-done.1.refs_1_.refs_11_), channel_id=1, source_target_pairs={{0,16},{16,0},{1,17},{17,1},{2,18},{18,2},{3,19},{19,3},{4,20},{20... | collective-permute-start | bytes 3932168 | tf_op jit(solution)/shard_map/ppermute | solution.py:403
  94.5 1.1 copy-start.6
  94.5 3.0 %collective-permute-start.7 = (bf16[5120,128]{1,0:T(8,128)(2,1)S(1)}, bf16[5120,128]{1,0:T(8,128)(2,1)S(1)}, u32[]{:S(2)}, u32[]{:S(2)}) collective-permute-start(bf16[5120,128]{1,0:T(8,128)(2,1)S(1)} %collective-permute-done.2.refs_5_.refs_12_), channel_id=1, source_target_pairs={{0,16},{16,0},{1,17},{17,1},{2,18},{18,2},{3,19},{19,3},{4,20},{20... | collective-permute-start | bytes 3932168 | tf_op jit(solution)/shard_map/ppermute | solution.py:403
  94.5 3.0 %copy-start.7 = (bf16[5120,128]{1,0:T(8,128)(2,1)}, bf16[5120,128]{1,0:T(8,128)(2,1)S(1)}, u32[]{:S(2)}) copy-start(bf16[5120,128]{1,0:T(8,128)(2,1)S(1)} %collective-permute-done.3.refs_2_.refs_13_) | copy-start | bytes 3932164
  94.5 3.0 %copy-start.8 = (bf16[5120,128]{1,0:T(8,128)(2,1)}, bf16[5120,128]{1,0:T(8,128)(2,1)S(1)}, u32[]{:S(2)}) copy-start(bf16[5120,128]{1,0:T(8,128)(2,1)S(1)} %collective-permute-done.4.refs_6_.refs_14_) | copy-start | bytes 3932164
  94.5 3.0 %copy-start.14 = (bf16[128,5120]{1,0:T(8,128)(2,1)}, bf16[128,5120]{1,0:T(8,128)(2,1)S(1)}, u32[]{:S(2)}) copy-start(bf16[128,5120]{1,0:T(8,128)(2,1)S(1)} %collective-permute-done.5.refs_6_) | copy-start | bytes 3932164
  95.5 2.0 copy-start.9
  95.5 12.7 %collective-permute-start.8 = (bf16[48,5120]{1,0:T(8,128)(2,1)S(1)}, bf16[48,5120]{1,0:T(8,128)(2,1)S(1)}, u32[]{:S(2)}, u32[]{:S(2)}) collective-permute-start(bf16[48,5120]{1,0:T(8,128)(2,1)S(1)} %slice.16), channel_id=1, source_target_pairs={{0,1},{1,0},{2,3},{3,2},{4,5},{5,4},{6,7},{7,6},{8,9},{9,8},{10,11... | collective-permute-start | bytes 1474568 | tf_op jit(solution)/shard_map/ppermute | solution.py:403
  97.5 1.1 copy-start.10
  108.3 21.7 %copy-start.19 = (bf16[48,5120]{1,0:T(8,128)(2,1)}, bf16[48,5120]{1,0:T(8,128)(2,1)S(1)}, u32[]{:S(2)}) copy-start(bf16[48,5120]{1,0:T(8,128)(2,1)S(1)} %collective-permute-done.8.refs_4_) | copy-start | bytes 1474564
  108.7 11.0 %collective-permute-start.9 = (bf16[320,10240]{1,0:T(8,128)(2,1)}, bf16[320,10240]{1,0:T(8,128)(2,1)}, u32[]{:S(2)}, u32[]{:S(2)}) collective-permute-start(bf16[320,10240]{1,0:T(8,128)(2,1)} %all-gather.3.cloned.1.call-done.both_ref.y0.refs_0_), channel_id=1, source_target_pairs={{0,16},{16,0},{1,17},{17,1},{2,18},{18,2},{3,19},{19,3},{4,20},{20... | collective-permute-start | bytes 19660808 | tf_op jit(solution)/shard_map/ppermute | solution.py:403
  108.8 93.1 %reduce-scatter.4.cloned.1.call-start = ((), (), s32[]{:S(2)}) async-start(), calls=%async_computation.5 | async-start | bytes 3778560
  108.8 21.1 %collective-permute-start.11 = (bf16[80,5120]{1,0:T(8,128)(2,1)S(1)}, bf16[80,5120]{1,0:T(8,128)(2,1)S(1)}, u32[]{:S(2)}, u32[]{:S(2)}) collective-permute-start(bf16[80,5120]{1,0:T(8,128)(2,1)S(1)} %slice.17), channel_id=1, source_target_pairs={{0,1},{1,0},{2,3},{3,2},{4,5},{5,4},{6,7},{7,6},{8,9},{9,8},{10,11... | collective-permute-start | bytes 2457608 | tf_op jit(solution)/shard_map/ppermute | solution.py:403
  117.3 2.4 %collective-permute-start.10 = (bf16[320,256]{1,0:T(8,128)(2,1)}, bf16[320,256]{1,0:T(8,128)(2,1)S(1)}, u32[]{:S(2)}, u32[]{:S(2)}) collective-permute-start(bf16[320,256]{1,0:T(8,128)(2,1)} %get-tuple-element.82), channel_id=1, source_target_pairs={{0,16},{16,0},{1,17},{17,1},{2,18},{18,2},{3,19},{19,3},{4,20},{20... | collective-permute-start | bytes 491528 | tf_op jit(solution)/shard_map/ppermute | solution.py:403
  119.7 0.7 copy-start.21
  124.9 33.8 %collective-permute-start.16 = (bf16[128,5120]{1,0:T(8,128)(2,1)}, bf16[128,5120]{1,0:T(8,128)(2,1)}, u32[]{:S(2)}, u32[]{:S(2)}) collective-permute-start(bf16[128,5120]{1,0:T(8,128)(2,1)} %flat_part.2), channel_id=1, source_target_pairs={{0,1},{1,0},{2,3},{3,2},{4,5},{5,4},{6,7},{7,6},{8,9},{9,8},{10,11... | collective-permute-start | bytes 3932168 | tf_op jit(solution)/shard_map/ppermute | solution.py:403
  130.0 3.0 %copy-start.17 = (bf16[80,5120]{1,0:T(8,128)(2,1)}, bf16[80,5120]{1,0:T(8,128)(2,1)S(1)}, u32[]{:S(2)}) copy-start(bf16[80,5120]{1,0:T(8,128)(2,1)S(1)} %collective-permute-done.11.refs_5_) | copy-start | bytes 2457604
  130.0 3.0 %collective-permute-start.13 = (bf16[80,5120]{1,0:T(8,128)(2,1)S(1)}, bf16[80,5120]{1,0:T(8,128)(2,1)S(1)}, u32[]{:S(2)}, u32[]{:S(2)}) collective-permute-start(bf16[80,5120]{1,0:T(8,128)(2,1)S(1)} %collective-permute-done.11.refs_5_), channel_id=1, source_target_pairs={{0,16},{16,0},{1,17},{17,1},{2,18},{18,2},{3,19},{19,3},{4,20},{20... | collective-permute-start | bytes 2457608 | tf_op jit(solution)/shard_map/ppermute | solution.py:403
  130.0 3.0 %collective-permute-start.12 = (bf16[48,5120]{1,0:T(8,128)(2,1)S(1)}, bf16[48,5120]{1,0:T(8,128)(2,1)S(1)}, u32[]{:S(2)}, u32[]{:S(2)}) collective-permute-start(bf16[48,5120]{1,0:T(8,128)(2,1)S(1)} %collective-permute-done.8.refs_4_), channel_id=1, source_target_pairs={{0,16},{16,0},{1,17},{17,1},{2,18},{18,2},{3,19},{19,3},{4,20},{20... | collective-permute-start | bytes 1474568 | tf_op jit(solution)/shard_map/ppermute | solution.py:403
  133.0 0.8 copy-start.20
  133.0 1.1 copy-start.18
  147.0 1.9 collective-permute-start.15
  148.3 1.0 copy-start.12
  148.3 36.3 %collective-permute-start.14 = (bf16[320,1920]{1,0:T(8,128)(2,1)}, bf16[320,1920]{1,0:T(8,128)(2,1)}, u32[]{:S(2)}, u32[]{:S(2)}) collective-permute-start(bf16[320,1920]{1,0:T(8,128)(2,1)} %all-gather.5.cloned.1.call-done.refs_2_), channel_id=1, source_target_pairs={{0,16},{16,0},{1,17},{17,1},{2,18},{18,2},{3,19},{19,3},{4,20},{20... | collective-permute-start | bytes 3686408 | tf_op jit(solution)/shard_map/ppermute | solution.py:403
  148.9 0.7 copy-start.13
  155.6 55.2 %collective-permute-start.18 = (bf16[3200,128]{1,0:T(8,128)(2,1)}, bf16[3200,128]{1,0:T(8,128)(2,1)S(1)}, u32[]{:S(2)}, u32[]{:S(2)}) collective-permute-start(bf16[3200,128]{1,0:T(8,128)(2,1)} %get-tuple-element.99), channel_id=1, source_target_pairs={{0,1},{1,0},{2,3},{3,2},{4,5},{5,4},{6,7},{7,6},{8,9},{9,8},{10,11... | collective-permute-start | bytes 2457608 | tf_op jit(solution)/shard_map/ppermute | solution.py:403
  156.6 27.3 %collective-permute-start.17 = (bf16[640,256]{1,0:T(8,128)(2,1)S(1)}, bf16[640,256]{1,0:T(8,128)(2,1)S(1)}, u32[]{:S(2)}, u32[]{:S(2)}) collective-permute-start(bf16[640,256]{1,0:T(8,128)(2,1)S(1)} %pad_maximum_fusion), channel_id=1, source_target_pairs={{0,1},{1,0},{2,3},{3,2},{4,5},{5,4},{6,7},{7,6},{8,9},{9,8},{10,11... | collective-permute-start | bytes 983048 | tf_op jit(solution)/shard_map/ppermute | solution.py:403
  157.7 53.1 %collective-permute-start.19 = (bf16[3200,128]{1,0:T(8,128)(2,1)}, bf16[3200,128]{1,0:T(8,128)(2,1)S(1)}, u32[]{:S(2)}, u32[]{:S(2)}) collective-permute-start(bf16[3200,128]{1,0:T(8,128)(2,1)} %get-tuple-element.115), channel_id=1, source_target_pairs={{0,1},{1,0},{2,3},{3,2},{4,5},{5,4},{6,7},{7,6},{8,9},{9,8},{10,11... | collective-permute-start | bytes 2457608 | tf_op jit(solution)/shard_map/ppermute | solution.py:403
  201.8 1.0 copy-start
  203.8 16.9 %all-to-all-start.1 = ((bf16[16,10,1408]{2,1,0:T(8,128)(2,1)}), bf16[16,10,1408]{2,1,0:T(8,128)(2,1)S(1)}, u32[]{:S(2)}, u32[]{:S(2)}) async-start(bf16[16,10,1408]{2,1,0:T(8,128)(2,1)} %ship.1), calls=%async_computation.1 | async-start | bytes 1441792 | tf_op jit(solution)/shard_map/all_to_all | solution.py:464
  210.8 0.9 copy-start.15
  210.8 1.1 copy-start.16
  212.0 8.7 %copy-start.1 = (f32[128]{0:T(128)S(1)}, f32[128]{0:T(128)}, u32[]{:S(2)}) copy-start(f32[128]{0:T(128)} %param.9) | copy-start | bytes 1540
  212.0 8.7 %copy-start.2 = (s32[1,128]{1,0:T(1,128)S(1)}, s32[1,128]{1,0:T(1,128)}, u32[]{:S(2)}) copy-start(s32[1,128]{1,0:T(1,128)} %get-tuple-element.112.place_ref) | copy-start | bytes 1540
Sparse Core Ops, SparseCore 0:
  31.9 76.8 all-gather.2
  110.5 37.7 all-gather.4
  150.9 50.8 reduce-scatter.3

commit v6 on v5

--- a/solution.py
+++ b/solution.py
@@ -125,26 +125,37 @@
 
 
 def ship_kernel(sum_ref, out_ref, n_ctx, n_tp):
-    part = out_ref.shape[2] - LANES
-    width = part * n_tp
-    router = sum_ref[:, width:].astype(F32)
+    width = sum_ref.shape[1] - LANES
+    part = width // n_tp
+    pieces = MAIN // REST
+    cut = out_ref.shape[2] - part - LANES
+    group = n_ctx * REST
+    row = lax.broadcasted_iota(jnp.int32, (pieces * group, pieces * group), 0)
+    col = lax.broadcasted_iota(jnp.int32, (pieces * group, pieces * group), 1)
+    order = (col == row % pieces * group + row // pieces).astype(BF16)
+    router = sum_ref[:, width:]
+    fill = jnp.zeros((group, pieces * cut - part - LANES), BF16)
     for t in range(n_tp):
-        value = sum_ref[:, t * part : (t + 1) * part].astype(F32)
+        value = sum_ref[:, t * part : (t + 1) * part]
+        rest = jnp.concatenate([value[-group:], router[-group:], fill], 1).astype(F32)
+        rest = [rest[:, p * cut : (p + 1) * cut] for p in range(pieces)]
+        rest = jnp.concatenate(rest, 0).astype(BF16)
+        rest = jnp.dot(order, rest, preferred_element_type=F32).astype(BF16)
         for c in range(n_ctx):
             main = slice(c * MAIN, (c + 1) * MAIN)
-            rest = slice(n_ctx * MAIN + c * REST, n_ctx * MAIN + (c + 1) * REST)
-            both = jnp.concatenate([value[main], value[rest]], 0)
-            out_ref[c * n_tp + t, :, :part] = both.astype(BF16)
-            both = jnp.concatenate([router[main], router[rest]], 0)
-            out_ref[c * n_tp + t, :, part:] = both.astype(BF16)
+            out_ref[c * n_tp + t, :, :part] = value[main]
+            out_ref[c * n_tp + t, :, part : part + cut] = rest[main]
+            out_ref[c * n_tp + t, :, part + cut :] = router[main]
 
 
 def ship(summed, n_ctx, n_tp):
     part = (summed.shape[1] - LANES) // n_tp
+    pieces = MAIN // REST
+    cut = -(-(part + LANES) // (pieces * LANES)) * LANES
     return call(
         lambda *refs: ship_kernel(*refs, n_ctx=n_ctx, n_tp=n_tp),
         "ship",
-        struct((n_ctx * n_tp, HALF, part + LANES), BF16),
+        struct((n_ctx * n_tp, MAIN, part + cut + LANES), BF16),
         vmem=16 << 20,
     )(summed)
 
@@ -152,23 +163,32 @@
 def home_kernel(land_ref, place_ref, logit_ref, input_ref, grad_ref):
     n_dev, _, wide = land_ref.shape
     rows, part = input_ref.shape
-    fill = jnp.zeros((PAD - HALF, wide), F32)
-    flat = []
-    for t in range(n_dev):
-        flat += [land_ref[t].astype(F32), fill]
-    flat = jnp.concatenate(flat, 0).astype(BF16)
-    slot = lax.broadcasted_iota(jnp.int32, (n_dev * PAD, rows), 0)
-    pick = (slot == place_ref[...]).astype(BF16)
-    home = lax.dot_general(pick, flat[:, :part], OUTER, preferred_element_type=F32)
-    input_ref[...] = home.astype(BF16)
-    router = lax.dot_general(flat[:, part:], pick, OUTER, preferred_element_type=F32)
+    pieces = MAIN // REST
+    cut = wide - part - LANES
+    flat = jnp.concatenate([land_ref[t].astype(F32) for t in range(n_dev)], 0).astype(BF16)
+    slot = lax.broadcasted_iota(jnp.int32, (n_dev * MAIN, rows), 0)
+    target, r = slot // MAIN, slot % MAIN
+    place = place_ref[...]
+    take = lambda chosen, value: lax.dot_general(
+        chosen, value, OUTER, preferred_element_type=F32
+    )
+    main = (target * PAD + r == place).astype(BF16)
+    rest_row = target * PAD + MAIN + r // pieces == place
+    tail = flat[:, part : part + cut]
+    rest = []
+    for p in range(pieces):
+        chosen = (rest_row & (r % pieces == p)).astype(BF16)
+        rest.append(take(chosen, tail))
+    rest = jnp.concatenate(rest, 1)
+    input_ref[...] = (take(main, flat[:, :part]) + rest[:, :part]).astype(BF16)
+    first = part % cut
+    router = take(flat[:, part + cut :], main) + take(tail[:, first : first + LANES], chosen)
     weight = jax.nn.sigmoid(logit_ref[...]).astype(BF16).astype(F32)
     grad_ref[...] = (router[:1] * (1.0 - weight)).astype(BF16)
 
 
-def take_home(landed, place, logit):
+def take_home(landed, place, logit, part):
     rows = place.shape[1]
-    part = landed.shape[2] - LANES
     return call(
         home_kernel,
         "take_home",
@@ -462,7 +482,7 @@
     summed = after(summed, top[0])
     shipped = ship(summed, n_ctx, n_tp)
     landed = lax.all_to_all(shipped, ("ctx", "tp"), split_axis=0, concat_axis=0, tiled=True)
-    input_grad, logit_grad = take_home(landed, place, logit)
+    input_grad, logit_grad = take_home(landed, place, logit, tokens_in.shape[1])
     return input_grad, logit_grad[0], tall_grads[0][None], tall_grads[1][None], down_grad[None]
 
 

time: 229 us -> 227 us (level)
  waiting for transfers between devices: 112 us -> 109 us
    unnamed x44 -> x46, local copies, waits for them, and re-layouts: 6.67 us -> 7.71 us
where the time goes in v6:
time: 227 us
  waiting for transfers between devices  109 us (48%)
  Pallas kernels  53.6 us (24%)
  blocking collectives  20.8 us (9%)
  starting transfers between devices  19.9 us (9%)
  between operations  14 us (6%)
  local copies, waits for them, and re-layouts  9.5 us (4%)
    ppermute x20, waiting for transfers between devices, flip(): return lax.ppermute(value, axis, [(i, i ^ 1) for i in range(count)])  96.3 us
    all_to_all x1, blocking collectives, body(): lax.all_to_all(send, ('ctx', 'tp'), split_axis=0, concat_axis=0, tiled=True)  20.8 us
    pallas_call x3, Pallas kernels, tall_part(): call(lambda *refs: tall_kernel(len(xs), *refs[:n], *refs[-2:]), 'tall_par...  17.6 us
    pallas_call x1, Pallas kernels, back_part(): call(lambda *refs: back_kernel(len(downs), *refs), 'back_part', [struct((...  13 us
    ppermute x20, starting transfers between devices, flip(): return lax.ppermute(value, axis, [(i, i ^ 1) for i in range(count)])  12.4 us
    optimization_barrier x1, waiting for transfers between devices, after(): return lax.optimization_barrier((value, first))[0]  10.2 us
    pallas_call x2, Pallas kernels, flat_part(): call(flat_kernel, 'flat_part', struct((unit, width), BF16), grid=(steps,)...  9.73 us
    unnamed x46, local copies, waits for them, and re-layouts  7.71 us
  transfers between devices with their start and end apart: 24, of which 14 were waited for; matrix products, arithmetic and copies ran while one was open for 1% of the time, Pallas kernels for 21%

profile of v6, /device:TPU:2, one launch (start us, length us, event | category | flops | bytes accessed | tf_op | source)
XLA Modules:
  0.0 226.7 jit_solution(1382609029266039595)
XLA Ops:
  7.2 0.0 all-gather.3.cloned.1.call-start
  7.2 2.6 %spread.1 = (bf16[16,8,3200]{2,1,0:T(8,128)(2,1)}, s32[1,128]{1,0:T(1,128)}) custom-call(bf16[128,1280]{1,0:T(8,128)(2,1)} %refs_0_.1, bf16[128,1280]{1,0:T(8,128)(2,1)} %refs_1_.1, f32[1,128]{1,0:T(1,128)} %bitcast.10, s32[1,128]{1,0:T(1,128)} %bitcast.26), custom_call_target="tpu_custom_call" | custom-call | tf_op jit(solution)/shard_map/spread/pallas_call | solution.py:82
  9.8 20.8 %all_to_all.10.refs_0_ = bf16[16,8,3200]{2,1,0:T(8,128)(2,1)S(1)} all-to-all(bf16[16,8,3200]{2,1,0:T(8,128)(2,1)} %get-tuple-element.62), channel_id=1, replica_groups=mesh['z'=8,'core'=2,'ctx'=4,'tp'=4] {'ctx','tp'}, dimensions={0} | all-to-all | bytes 1638400 | tf_op jit(solution)/shard_map/all_to_all | solution.py:436
  30.6 1.1 arrange.1
  31.7 0.0 all-gather.3.cloned.1.call-update
  31.8 0.0 all-gather.5.cloned.1.call-start
  31.8 0.9 slice.20
  32.7 1.5 collective-permute-start
  34.3 3.9 %collective-permute-done = bf16[40,1920]{1,0:T(8,128)(2,1)} collective-permute-done((bf16[40,1920]{1,0:T(8,128)(2,1)S(1)}, bf16[40,1920]{1,0:T(8,128)(2,1)}, u32[]{:S(2)}, u32[]{:S(2)}) %collective-permute-start) | collective-permute-done | bytes 153632 | tf_op jit(solution)/shard_map/ppermute | solution.py:423
  38.1 1.5 collective-permute-start.1
  39.6 0.1 slice.17
  39.7 1.2 collective-permute-start.2
  40.9 0.0 collective-permute-start.3
  40.9 0.5 collective-permute-start.4
  41.4 28.4 %collective-permute-done.1.refs_1_.refs_11_ = bf16[5120,128]{1,0:T(8,128)(2,1)S(1)} collective-permute-done((bf16[5120,128]{1,0:T(8,128)(2,1)S(1)}, bf16[5120,128]{1,0:T(8,128)(2,1)S(1)}, u32[]{:S(2)}, u32[]{:S(2)}) %collective-permute-start.1) | collective-permute-done | bytes 1310752 | tf_op jit(solution)/shard_map/ppermute | solution.py:423
  69.9 24.6 %collective-permute-done.2.refs_5_.refs_12_ = bf16[5120,128]{1,0:T(8,128)(2,1)S(1)} collective-permute-done((bf16[5120,128]{1,0:T(8,128)(2,1)S(1)}, bf16[5120,128]{1,0:T(8,128)(2,1)S(1)}, u32[]{:S(2)}, u32[]{:S(2)}) %collective-permute-start.2) | collective-permute-done | bytes 1310752 | tf_op jit(solution)/shard_map/ppermute | solution.py:423
  94.5 0.0 copy-start.7
  94.5 0.0 collective-permute-done.4.refs_6_.refs_14_
  94.5 1.0 copy-done.6
  95.5 1.5 collective-permute-start.8
  97.0 0.5 collective-permute-done.7.refs_7_.refs_16_
  97.5 1.1 copy-done.10
  98.6 9.7 %collective-permute-done.8.refs_4_ = bf16[48,5120]{1,0:T(8,128)(2,1)S(1)} collective-permute-done((bf16[48,5120]{1,0:T(8,128)(2,1)S(1)}, bf16[48,5120]{1,0:T(8,128)(2,1)S(1)}, u32[]{:S(2)}, u32[]{:S(2)}) %collective-permute-start.8) | collective-permute-done | bytes 491552 | tf_op jit(solution)/shard_map/ppermute | solution.py:423
  108.3 0.5 all-gather.3.cloned.1.call-done.both_ref.y0.refs_0_
  108.7 0.0 all-gather.5.cloned.1.call-update
  108.8 0.0 reduce-scatter.4.cloned.1.call-start
  108.8 1.1 collective-permute-start.11
  109.9 7.4 %gate_up_part.1 = (bf16[320,256]{1,0:T(8,128)(2,1)}, bf16[320,256]{1,0:T(8,128)(2,1)}, f32[320,512]{1,0:T(8,128)}, f32[320,512]{1,0:T(8,128)}) custom-call(bf16[320,10240]{1,0:T(8,128)(2,1)} %all-gather.3.cloned.1.call-done.both_ref.y0.refs_0_, bf16[5120,128]{1,0:T(8,128)(2,1)} %bitcast.12, bf16[5120,128]{1,0:T(8,128)(2,1)} %copy-done.5, ...), custom_call_target="tpu_custom_call" | custom-call | tf_op jit(solution)/shard_map/gate_up_part/pallas_call | solution.py:239
  117.3 0.3 collective-permute-start.10
  117.7 2.1 collective-permute-done.10.s1
  119.7 0.7 copy-done.21
  120.4 4.6 %flat_part.2 = bf16[128,5120]{1,0:T(8,128)(2,1)} custom-call(bf16[320,10240]{1,0:T(8,128)(2,1)} %all-gather.3.cloned.1.call-done.both_ref.y0.refs_0_, bf16[320,10240]{1,0:T(8,128)(2,1)} %collective-permute-done.9.y1.refs_1_, bf16[320,256]{1,0:T(8,128)(2,1)} %get-tuple-element.104.s0, bf16[320,256]{1,0:T(8,128)(2,1)} %copy-done.21), custom_call_target="tpu_custom_call" | custom-call | tf_op jit(solution)/shard_map/flat_part/pallas_call | solution.py:410
  124.9 1.0 collective-permute-start.16
  125.9 4.0 %collective-permute-done.11.refs_5_ = bf16[80,5120]{1,0:T(8,128)(2,1)S(1)} collective-permute-done((bf16[80,5120]{1,0:T(8,128)(2,1)S(1)}, bf16[80,5120]{1,0:T(8,128)(2,1)S(1)}, u32[]{:S(2)}, u32[]{:S(2)}) %collective-permute-start.11) | collective-permute-done | bytes 819232 | tf_op jit(solution)/shard_map/ppermute | solution.py:423
  129.9 0.0 collective-permute-start.13
  130.0 0.5 collective-permute-start.12
  130.5 2.5 %collective-permute-done.12.refs_7_ = bf16[48,5120]{1,0:T(8,128)(2,1)S(1)} collective-permute-done((bf16[48,5120]{1,0:T(8,128)(2,1)S(1)}, bf16[48,5120]{1,0:T(8,128)(2,1)S(1)}, u32[]{:S(2)}, u32[]{:S(2)}) %collective-permute-start.12) | collective-permute-done | bytes 491552 | tf_op jit(solution)/shard_map/ppermute | solution.py:423
  133.0 0.8 copy-done.20
  133.8 0.3 copy-done.18
  134.0 13.0 %back_part.1 = (bf16[320,5248]{1,0:T(8,128)(2,1)}, bf16[320,512]{1,0:T(8,128)(2,1)}, bf16[320,512]{1,0:T(8,128)(2,1)}) custom-call(bf16[320,10240]{1,0:T(8,128)(2,1)} %all-gather.3.cloned.1.call-done.both_ref.y0.refs_0_, f32[320,512]{1,0:T(8,128)} %get-tuple-element.84.refs_1_, f32[320,512]{1,0:T(8,128)} %get-tuple-element.85.refs_2_, ...), custom_call_target="tpu_custom_call" | custom-call | tf_op jit(solution)/shard_map/back_part/pallas_call | solution.py:334
  147.1 0.3 collective-permute-start.15
  147.3 1.0 all-gather.5.cloned.1.call-done.refs_2_
  148.3 0.0 reduce-scatter.4.cloned.1.call-update
  148.4 0.6 collective-permute-done.15.refs_3_.refs_5_
  149.0 0.3 copy-done.12
  149.3 0.4 copy-done.13
  149.7 5.9 %tall_part.3 = (bf16[3200,128]{1,0:T(8,128)(2,1)}, bf16[3200,128]{1,0:T(8,128)(2,1)}) custom-call(bf16[320,10240]{1,0:T(8,128)(2,1)} %all-gather.3.cloned.1.call-done.both_ref.y0.refs_0_, bf16[320,10240]{1,0:T(8,128)(2,1)} %collective-permute-done.9.y1.refs_1_, bf16[320,512]{1,0:T(8,128)(2,1)} %get-tuple-element.107.refs_2_.refs_4_, bf16[320,512]{1,0:T(8,128)(2,1)} %copy-done.13), custom_call_target="tpu_custom_call" | custom-call | tf_op jit(solution)/shard_map/tall_part/pallas_call | solution.py:371
  155.7 1.0 collective-permute-start.18
  156.7 1.1 collective-permute-start.17
  157.8 1.0 collective-permute-start.19
  158.8 5.2 %flat_part.3 = bf16[128,5120]{1,0:T(8,128)(2,1)} custom-call(bf16[320,10240]{1,0:T(8,128)(2,1)} %all-gather.3.cloned.1.call-done.both_ref.y0.refs_0_, bf16[320,10240]{1,0:T(8,128)(2,1)} %collective-permute-done.9.y1.refs_1_, bf16[320,256]{1,0:T(8,128)(2,1)} %get-tuple-element.104.s0, bf16[320,256]{1,0:T(8,128)(2,1)} %copy-done.21, ...), custom_call_target="tpu_custom_call" | custom-call | flops 34589999104 | tf_op jit(solution)/shard_map/flat_part/pallas_call | solution.py:410
  164.0 20.0 %collective-permute-done.17 = bf16[640,256]{1,0:T(8,128)(2,1)S(1)} collective-permute-done((bf16[640,256]{1,0:T(8,128)(2,1)S(1)}, bf16[640,256]{1,0:T(8,128)(2,1)S(1)}, u32[]{:S(2)}, u32[]{:S(2)}) %collective-permute-start.17) | collective-permute-done | bytes 327712 | tf_op jit(solution)/shard_map/ppermute | solution.py:423
  184.0 0.7 fusion
  184.8 1.0 copy-done.22
  185.8 5.3 %tall_part.4 = (bf16[5120,128]{1,0:T(8,128)(2,1)}, bf16[5120,128]{1,0:T(8,128)(2,1)}) custom-call(bf16[320,10240]{1,0:T(8,128)(2,1)} %all-gather.3.cloned.1.call-done.both_ref.y0.refs_0_, bf16[320,10240]{1,0:T(8,128)(2,1)} %collective-permute-done.9.y1.refs_1_, bf16[320,1920]{1,0:T(8,128)(2,1)} %all-gather.5.cloned.1.call-done.refs_2_, ...), custom_call_target="tpu_custom_call" | custom-call | flops 34589999104 | tf_op jit(solution)/shard_map/tall_part/pallas_call | solution.py:371
  191.1 10.2 %reduce-scatter.4.cloned.1.call-done.refs_0_ = bf16[40,5248]{1,0:T(8,128)(2,1)} async-done(((bf16[320,5248]{1,0:T(8,128)(2,1)}), bf16[40,5248]{1,0:T(8,128)(2,1)}) %reduce-scatter.4.cloned.1.call-update) | async-done | bytes 419856 | tf_op jit(solution)/shard_map/optimization_barrier | solution.py:427
  201.3 1.0 copy-done
  202.3 0.9 ship.1
  203.3 7.4 %all-to-all-start.1 = ((bf16[16,8,1792]{2,1,0:T(8,128)(2,1)}), bf16[16,8,1792]{2,1,0:T(8,128)(2,1)S(1)}, u32[]{:S(2)}, u32[]{:S(2)}) async-start(bf16[16,8,1792]{2,1,0:T(8,128)(2,1)} %ship.1), calls=%async_computation.1 | async-start | bytes 917504 | tf_op jit(solution)/shard_map/all_to_all | solution.py:484
  210.7 0.9 copy-done.15
  211.5 0.3 copy-done.16
  211.8 6.4 %tall_part.5 = (bf16[5120,128]{1,0:T(8,128)(2,1)}, bf16[5120,128]{1,0:T(8,128)(2,1)}) custom-call(bf16[320,10240]{1,0:T(8,128)(2,1)} %all-gather.3.cloned.1.call-done.both_ref.y0.refs_0_, bf16[320,10240]{1,0:T(8,128)(2,1)} %collective-permute-done.9.y1.refs_1_, ...), custom_call_target="tpu_custom_call", output_to_operand_aliasing={{0}: (6, {}), {1}: (7, {})} | custom-call | tf_op jit(solution)/shard_map/tall_part/pallas_call | solution.py:371
  218.2 0.9 all-to-all-done.1.land_ref
  219.0 1.2 take_home.1
  (52 shorter events, 0.2 us)
Async XLA Ops:
  7.2 101.6 %all-gather.3.cloned.1.call-start = ((), (), s32[]{:S(2)}) async-start(), calls=%async_computation.3 | async-start | bytes 7372800 | tf_op jit(solution)/shard_map/all_gather | solution.py:451
  30.6 7.5 %copy-start.3 = (bf16[1,5120,128]{2,1,0:T(8,128)(2,1)S(1)}, bf16[1,5120,128]{2,1,0:T(8,128)(2,1)}, u32[]{:S(2)}) copy-start(bf16[1,5120,128]{2,1,0:T(8,128)(2,1)} %param.11) | copy-start | bytes 3932164
  30.6 9.0 %copy-start.11 = (bf16[1,128,5120]{2,1,0:T(8,128)(2,1)S(1)}, bf16[1,128,5120]{2,1,0:T(8,128)(2,1)}, u32[]{:S(2)}) copy-start(bf16[1,128,5120]{2,1,0:T(8,128)(2,1)} %param.13) | copy-start | bytes 3932164
  31.8 116.6 %all-gather.5.cloned.1.call-start = ((), (), s32[]{:S(2)}) async-start(), calls=%async_computation.4 | async-start | bytes 1382400 | tf_op jit(solution)/shard_map/all_gather | solution.py:463
  32.7 5.4 %collective-permute-start = (bf16[40,1920]{1,0:T(8,128)(2,1)S(1)}, bf16[40,1920]{1,0:T(8,128)(2,1)}, u32[]{:S(2)}, u32[]{:S(2)}) collective-permute-start(bf16[40,1920]{1,0:T(8,128)(2,1)S(1)} %slice.20), channel_id=1, source_target_pairs={{0,1},{1,0},{2,3},{3,2},{4,5},{5,4},{6,7},{7,6},{8,9},{9,8},{10,11... | collective-permute-start | bytes 460808 | tf_op jit(solution)/shard_map/ppermute | solution.py:423
  38.1 1.6 copy-start.4
  38.1 31.7 %collective-permute-start.1 = (bf16[5120,128]{1,0:T(8,128)(2,1)S(1)}, bf16[5120,128]{1,0:T(8,128)(2,1)S(1)}, u32[]{:S(2)}, u32[]{:S(2)}) collective-permute-start(bf16[5120,128]{1,0:T(8,128)(2,1)S(1)} %bitcast.14), channel_id=1, source_target_pairs={{0,1},{1,0},{2,3},{3,2},{4,5},{5,4},{6,7},{7,6},{8,9},{9,8},{10,11... | collective-permute-start | bytes 3932168 | tf_op jit(solution)/shard_map/ppermute | solution.py:423
  39.7 54.7 %collective-permute-start.2 = (bf16[5120,128]{1,0:T(8,128)(2,1)S(1)}, bf16[5120,128]{1,0:T(8,128)(2,1)S(1)}, u32[]{:S(2)}, u32[]{:S(2)}) collective-permute-start(bf16[5120,128]{1,0:T(8,128)(2,1)S(1)} %bitcast.18), channel_id=1, source_target_pairs={{0,1},{1,0},{2,3},{3,2},{4,5},{5,4},{6,7},{7,6},{8,9},{9,8},{10,11... | collective-permute-start | bytes 3932168 | tf_op jit(solution)/shard_map/ppermute | solution.py:423
  40.9 53.5 %collective-permute-start.3 = (bf16[5120,128]{1,0:T(8,128)(2,1)S(1)}, bf16[5120,128]{1,0:T(8,128)(2,1)S(1)}, u32[]{:S(2)}, u32[]{:S(2)}) collective-permute-start(bf16[5120,128]{1,0:T(8,128)(2,1)S(1)} %bitcast.15), channel_id=1, source_target_pairs={{0,16},{16,0},{1,17},{17,1},{2,18},{18,2},{3,19},{19,3},{4,20},{20... | collective-permute-start | bytes 3932168 | tf_op jit(solution)/shard_map/ppermute | solution.py:423
  40.9 53.6 %collective-permute-start.4 = (bf16[5120,128]{1,0:T(8,128)(2,1)S(1)}, bf16[5120,128]{1,0:T(8,128)(2,1)S(1)}, u32[]{:S(2)}, u32[]{:S(2)}) collective-permute-start(bf16[5120,128]{1,0:T(8,128)(2,1)S(1)} %bitcast.19), channel_id=1, source_target_pairs={{0,16},{16,0},{1,17},{17,1},{2,18},{18,2},{3,19},{19,3},{4,20},{20... | collective-permute-start | bytes 3932168 | tf_op jit(solution)/shard_map/ppermute | solution.py:423
  41.4 53.1 %collective-permute-start.5 = (bf16[128,5120]{1,0:T(8,128)(2,1)S(1)}, bf16[128,5120]{1,0:T(8,128)(2,1)S(1)}, u32[]{:S(2)}, u32[]{:S(2)}) collective-permute-start(bf16[128,5120]{1,0:T(8,128)(2,1)S(1)} %bitcast.23), channel_id=1, source_target_pairs={{0,16},{16,0},{1,17},{17,1},{2,18},{18,2},{3,19},{19,3},{4,20},{20... | collective-permute-start | bytes 3932168 | tf_op jit(solution)/shard_map/ppermute | solution.py:423
  69.9 24.6 %copy-start.5 = (bf16[5120,128]{1,0:T(8,128)(2,1)}, bf16[5120,128]{1,0:T(8,128)(2,1)S(1)}, u32[]{:S(2)}) copy-start(bf16[5120,128]{1,0:T(8,128)(2,1)S(1)} %collective-permute-done.1.refs_1_.refs_11_) | copy-start | bytes 3932164
  69.9 24.7 %collective-permute-start.6 = (bf16[5120,128]{1,0:T(8,128)(2,1)S(1)}, bf16[5120,128]{1,0:T(8,128)(2,1)S(1)}, u32[]{:S(2)}, u32[]{:S(2)}) collective-permute-start(bf16[5120,128]{1,0:T(8,128)(2,1)S(1)} %collective-permute-done.1.refs_1_.refs_11_), channel_id=1, source_target_pairs={{0,16},{16,0},{1,17},{17,1},{2,18},{18,2},{3,19},{19,3},{4,20},{20... | collective-permute-start | bytes 3932168 | tf_op jit(solution)/shard_map/ppermute | solution.py:423
  94.4 1.1 copy-start.6
  94.4 3.0 %collective-permute-start.7 = (bf16[5120,128]{1,0:T(8,128)(2,1)S(1)}, bf16[5120,128]{1,0:T(8,128)(2,1)S(1)}, u32[]{:S(2)}, u32[]{:S(2)}) collective-permute-start(bf16[5120,128]{1,0:T(8,128)(2,1)S(1)} %collective-permute-done.2.refs_5_.refs_12_), channel_id=1, source_target_pairs={{0,16},{16,0},{1,17},{17,1},{2,18},{18,2},{3,19},{19,3},{4,20},{20... | collective-permute-start | bytes 3932168 | tf_op jit(solution)/shard_map/ppermute | solution.py:423
  94.5 3.0 %copy-start.7 = (bf16[5120,128]{1,0:T(8,128)(2,1)}, bf16[5120,128]{1,0:T(8,128)(2,1)S(1)}, u32[]{:S(2)}) copy-start(bf16[5120,128]{1,0:T(8,128)(2,1)S(1)} %collective-permute-done.3.refs_2_.refs_13_) | copy-start | bytes 3932164
  94.5 3.0 %copy-start.8 = (bf16[5120,128]{1,0:T(8,128)(2,1)}, bf16[5120,128]{1,0:T(8,128)(2,1)S(1)}, u32[]{:S(2)}) copy-start(bf16[5120,128]{1,0:T(8,128)(2,1)S(1)} %collective-permute-done.4.refs_6_.refs_14_) | copy-start | bytes 3932164
  94.5 3.0 %copy-start.14 = (bf16[128,5120]{1,0:T(8,128)(2,1)}, bf16[128,5120]{1,0:T(8,128)(2,1)S(1)}, u32[]{:S(2)}) copy-start(bf16[128,5120]{1,0:T(8,128)(2,1)S(1)} %collective-permute-done.5.refs_6_) | copy-start | bytes 3932164
  95.5 2.0 copy-start.9
  95.5 12.7 %collective-permute-start.8 = (bf16[48,5120]{1,0:T(8,128)(2,1)S(1)}, bf16[48,5120]{1,0:T(8,128)(2,1)S(1)}, u32[]{:S(2)}, u32[]{:S(2)}) collective-permute-start(bf16[48,5120]{1,0:T(8,128)(2,1)S(1)} %slice.16), channel_id=1, source_target_pairs={{0,1},{1,0},{2,3},{3,2},{4,5},{5,4},{6,7},{7,6},{8,9},{9,8},{10,11... | collective-permute-start | bytes 1474568 | tf_op jit(solution)/shard_map/ppermute | solution.py:423
  97.5 1.1 copy-start.10
  108.3 21.7 %copy-start.19 = (bf16[48,5120]{1,0:T(8,128)(2,1)}, bf16[48,5120]{1,0:T(8,128)(2,1)S(1)}, u32[]{:S(2)}) copy-start(bf16[48,5120]{1,0:T(8,128)(2,1)S(1)} %collective-permute-done.8.refs_4_) | copy-start | bytes 1474564
  108.7 11.0 %collective-permute-start.9 = (bf16[320,10240]{1,0:T(8,128)(2,1)}, bf16[320,10240]{1,0:T(8,128)(2,1)}, u32[]{:S(2)}, u32[]{:S(2)}) collective-permute-start(bf16[320,10240]{1,0:T(8,128)(2,1)} %all-gather.3.cloned.1.call-done.both_ref.y0.refs_0_), channel_id=1, source_target_pairs={{0,16},{16,0},{1,17},{17,1},{2,18},{18,2},{3,19},{19,3},{4,20},{20... | collective-permute-start | bytes 19660808 | tf_op jit(solution)/shard_map/ppermute | solution.py:423
  108.8 92.6 %reduce-scatter.4.cloned.1.call-start = ((), (), s32[]{:S(2)}) async-start(), calls=%async_computation.5 | async-start | bytes 3778560
  108.8 21.1 %collective-permute-start.11 = (bf16[80,5120]{1,0:T(8,128)(2,1)S(1)}, bf16[80,5120]{1,0:T(8,128)(2,1)S(1)}, u32[]{:S(2)}, u32[]{:S(2)}) collective-permute-start(bf16[80,5120]{1,0:T(8,128)(2,1)S(1)} %slice.17), channel_id=1, source_target_pairs={{0,1},{1,0},{2,3},{3,2},{4,5},{5,4},{6,7},{7,6},{8,9},{9,8},{10,11... | collective-permute-start | bytes 2457608 | tf_op jit(solution)/shard_map/ppermute | solution.py:423
  117.3 2.4 %collective-permute-start.10 = (bf16[320,256]{1,0:T(8,128)(2,1)}, bf16[320,256]{1,0:T(8,128)(2,1)S(1)}, u32[]{:S(2)}, u32[]{:S(2)}) collective-permute-start(bf16[320,256]{1,0:T(8,128)(2,1)} %get-tuple-element.82), channel_id=1, source_target_pairs={{0,16},{16,0},{1,17},{17,1},{2,18},{18,2},{3,19},{19,3},{4,20},{20... | collective-permute-start | bytes 491528 | tf_op jit(solution)/shard_map/ppermute | solution.py:423
  119.7 0.7 copy-start.21
  124.9 33.9 %collective-permute-start.16 = (bf16[128,5120]{1,0:T(8,128)(2,1)}, bf16[128,5120]{1,0:T(8,128)(2,1)}, u32[]{:S(2)}, u32[]{:S(2)}) collective-permute-start(bf16[128,5120]{1,0:T(8,128)(2,1)} %flat_part.2), channel_id=1, source_target_pairs={{0,1},{1,0},{2,3},{3,2},{4,5},{5,4},{6,7},{7,6},{8,9},{9,8},{10,11... | collective-permute-start | bytes 3932168 | tf_op jit(solution)/shard_map/ppermute | solution.py:423
  129.9 3.0 %copy-start.17 = (bf16[80,5120]{1,0:T(8,128)(2,1)}, bf16[80,5120]{1,0:T(8,128)(2,1)S(1)}, u32[]{:S(2)}) copy-start(bf16[80,5120]{1,0:T(8,128)(2,1)S(1)} %collective-permute-done.11.refs_5_) | copy-start | bytes 2457604
  129.9 3.0 %collective-permute-start.13 = (bf16[80,5120]{1,0:T(8,128)(2,1)S(1)}, bf16[80,5120]{1,0:T(8,128)(2,1)S(1)}, u32[]{:S(2)}, u32[]{:S(2)}) collective-permute-start(bf16[80,5120]{1,0:T(8,128)(2,1)S(1)} %collective-permute-done.11.refs_5_), channel_id=1, source_target_pairs={{0,16},{16,0},{1,17},{17,1},{2,18},{18,2},{3,19},{19,3},{4,20},{20... | collective-permute-start | bytes 2457608 | tf_op jit(solution)/shard_map/ppermute | solution.py:423
  130.0 3.0 %collective-permute-start.12 = (bf16[48,5120]{1,0:T(8,128)(2,1)S(1)}, bf16[48,5120]{1,0:T(8,128)(2,1)S(1)}, u32[]{:S(2)}, u32[]{:S(2)}) collective-permute-start(bf16[48,5120]{1,0:T(8,128)(2,1)S(1)} %collective-permute-done.8.refs_4_), channel_id=1, source_target_pairs={{0,16},{16,0},{1,17},{17,1},{2,18},{18,2},{3,19},{19,3},{4,20},{20... | collective-permute-start | bytes 1474568 | tf_op jit(solution)/shard_map/ppermute | solution.py:423
  133.0 0.8 copy-start.20
  133.0 1.1 copy-start.18
  147.1 1.9 collective-permute-start.15
  148.3 1.0 copy-start.12
  148.3 36.4 %collective-permute-start.14 = (bf16[320,1920]{1,0:T(8,128)(2,1)}, bf16[320,1920]{1,0:T(8,128)(2,1)S(1)}, u32[]{:S(2)}, u32[]{:S(2)}) collective-permute-start(bf16[320,1920]{1,0:T(8,128)(2,1)} %all-gather.5.cloned.1.call-done.refs_2_), channel_id=1, source_target_pairs={{0,16},{16,0},{1,17},{17,1},{2,18},{18,2},{3,19},{19,3},{4,20},{20... | collective-permute-start | bytes 3686408 | tf_op jit(solution)/shard_map/ppermute | solution.py:423
  149.0 0.7 copy-start.13
  155.7 55.0 %collective-permute-start.18 = (bf16[3200,128]{1,0:T(8,128)(2,1)}, bf16[3200,128]{1,0:T(8,128)(2,1)S(1)}, u32[]{:S(2)}, u32[]{:S(2)}) collective-permute-start(bf16[3200,128]{1,0:T(8,128)(2,1)} %get-tuple-element.99), channel_id=1, source_target_pairs={{0,1},{1,0},{2,3},{3,2},{4,5},{5,4},{6,7},{7,6},{8,9},{9,8},{10,11... | collective-permute-start | bytes 2457608 | tf_op jit(solution)/shard_map/ppermute | solution.py:423
  156.7 27.3 %collective-permute-start.17 = (bf16[640,256]{1,0:T(8,128)(2,1)S(1)}, bf16[640,256]{1,0:T(8,128)(2,1)S(1)}, u32[]{:S(2)}, u32[]{:S(2)}) collective-permute-start(bf16[640,256]{1,0:T(8,128)(2,1)S(1)} %pad_maximum_fusion), channel_id=1, source_target_pairs={{0,1},{1,0},{2,3},{3,2},{4,5},{5,4},{6,7},{7,6},{8,9},{9,8},{10,11... | collective-permute-start | bytes 983048 | tf_op jit(solution)/shard_map/ppermute | solution.py:423
  157.8 52.8 %collective-permute-start.19 = (bf16[3200,128]{1,0:T(8,128)(2,1)}, bf16[3200,128]{1,0:T(8,128)(2,1)S(1)}, u32[]{:S(2)}, u32[]{:S(2)}) collective-permute-start(bf16[3200,128]{1,0:T(8,128)(2,1)} %get-tuple-element.115), channel_id=1, source_target_pairs={{0,1},{1,0},{2,3},{3,2},{4,5},{5,4},{6,7},{7,6},{8,9},{9,8},{10,11... | collective-permute-start | bytes 2457608 | tf_op jit(solution)/shard_map/ppermute | solution.py:423
  184.8 1.0 copy-start.22
  201.3 1.0 copy-start
  203.3 15.8 %all-to-all-start.1 = ((bf16[16,8,1792]{2,1,0:T(8,128)(2,1)}), bf16[16,8,1792]{2,1,0:T(8,128)(2,1)S(1)}, u32[]{:S(2)}, u32[]{:S(2)}) async-start(bf16[16,8,1792]{2,1,0:T(8,128)(2,1)} %ship.1), calls=%async_computation.1 | async-start | bytes 917504 | tf_op jit(solution)/shard_map/all_to_all | solution.py:484
  210.7 0.9 copy-start.15
  210.7 1.1 copy-start.16
  211.8 7.2 %copy-start.1 = (f32[128]{0:T(128)S(1)}, f32[128]{0:T(128)}, u32[]{:S(2)}) copy-start(f32[128]{0:T(128)} %param.9) | copy-start | bytes 1540
  211.8 7.2 %copy-start.2 = (s32[1,128]{1,0:T(1,128)S(1)}, s32[1,128]{1,0:T(1,128)}, u32[]{:S(2)}) copy-start(s32[1,128]{1,0:T(1,128)} %get-tuple-element.112.place_ref) | copy-start | bytes 1540
Sparse Core Ops, SparseCore 0:
  31.9 76.8 all-gather.2
  110.5 37.7 all-gather.4
  150.9 50.3 reduce-scatter.3

commit v7 on v6

--- a/solution.py
+++ b/solution.py
@@ -439,8 +439,9 @@
     cut = 3 * PAD
     far_mine = flip(mine[:, : FAR * PIECE], "tp")
     gate, down = after((own[0], own[2]), recv)
-    up, first, second = lax.optimization_barrier((own[1], down[:cut], down[cut:]))
-    gate, far_mine = lax.optimization_barrier((gate, far_mine))
+    up, first, second, far_mine = lax.optimization_barrier(
+        (own[1], down[:cut], down[cut:], far_mine)
+    )
     across = lambda group: tuple(flip(w, "core") for w in group)
     other = (flip(gate, "tp"), flip(up, "tp"))
     own_there = across(own)

time: 227 us -> 228 us (level)
  local copies, waits for them, and re-layouts: 9.5 us -> 13 us
    ppermute x20, waiting for transfers between devices: 96.3 us -> 92.3 us  [flip(): return lax.ppermute(value, axis, [(i, i ^ 1) for i in range(count)])]
    unnamed x46 -> x42, local copies, waits for them, and re-layouts: 7.71 us -> 8.19 us
  transfers between devices with their start and end apart: 24 -> 24, of which waited for: 14 -> 13; matrix products, arithmetic and copies ran while one was open for 1% -> 2% of each run, Pallas kernels for 21% -> 21%
where the time goes in v7:
time: 228 us; the launch traced here: 227 us
  waiting for transfers between devices  107 us (47%)
  Pallas kernels  53.5 us (23%)
  blocking collectives  20.8 us (9%)
  starting transfers between devices  18.5 us (8%)
  between operations  13.9 us (6%)
  local copies, waits for them, and re-layouts  13 us (6%)
    ppermute x20, waiting for transfers between devices, flip(): return lax.ppermute(value, axis, [(i, i ^ 1) for i in range(count)])  92.3 us
    all_to_all x1, blocking collectives, body(): lax.all_to_all(send, ('ctx', 'tp'), split_axis=0, concat_axis=0, tiled=True)  20.8 us
    pallas_call x3, Pallas kernels, tall_part(): call(lambda *refs: tall_kernel(len(xs), *refs[:n], *refs[-2:]), 'tall_par...  17.5 us
    pallas_call x1, Pallas kernels, back_part(): call(lambda *refs: back_kernel(len(downs), *refs), 'back_part', [struct((...  13 us
    optimization_barrier x1, waiting for transfers between devices, after(): return lax.optimization_barrier((value, first))[0]  11.9 us
    ppermute x20, starting transfers between devices, flip(): return lax.ppermute(value, axis, [(i, i ^ 1) for i in range(count)])  11.1 us
    pallas_call x2, Pallas kernels, flat_part(): call(flat_kernel, 'flat_part', struct((unit, width), BF16), grid=(steps,)...  9.71 us
    unnamed x42, local copies, waits for them, and re-layouts  8.19 us
  transfers between devices with their start and end apart: 24, of which 13 were waited for; matrix products, arithmetic and copies ran while one was open for 2% of the time, Pallas kernels for 21%

profile of v7, /device:TPU:2, one launch (start us, length us, event | category | flops | bytes accessed | tf_op | source)
XLA Modules:
  0.0 227.1 jit_solution(2515261745794902272)
XLA Ops:
  7.2 0.0 all-gather.3.cloned.1.call-start
  7.2 2.6 %spread.1 = (bf16[16,8,3200]{2,1,0:T(8,128)(2,1)}, s32[1,128]{1,0:T(1,128)}) custom-call(bf16[128,1280]{1,0:T(8,128)(2,1)} %refs_0_.1, bf16[128,1280]{1,0:T(8,128)(2,1)} %refs_1_.1, f32[1,128]{1,0:T(1,128)} %bitcast.10, s32[1,128]{1,0:T(1,128)} %bitcast.26), custom_call_target="tpu_custom_call" | custom-call | tf_op jit(solution)/shard_map/spread/pallas_call | solution.py:82
  9.8 20.8 %all_to_all.10.refs_0_ = bf16[16,8,3200]{2,1,0:T(8,128)(2,1)S(1)} all-to-all(bf16[16,8,3200]{2,1,0:T(8,128)(2,1)} %get-tuple-element.61), channel_id=1, replica_groups=mesh['z'=8,'core'=2,'ctx'=4,'tp'=4] {'ctx','tp'}, dimensions={0} | all-to-all | bytes 1638400 | tf_op jit(solution)/shard_map/all_to_all | solution.py:436
  30.6 1.1 arrange.1
  31.7 0.0 all-gather.3.cloned.1.call-update
  31.7 0.0 all-gather.5.cloned.1.call-start
  31.8 0.4 copy-done.3
  32.2 1.5 collective-permute-start
  33.7 0.9 slice.20
  34.6 0.0 copy-start.4
  34.6 0.7 collective-permute-start.1
  35.3 1.2 slice.16
  36.5 1.9 slice.15
  38.4 26.6 %collective-permute-done.1 = bf16[40,1920]{1,0:T(8,128)(2,1)} collective-permute-done((bf16[40,1920]{1,0:T(8,128)(2,1)S(1)}, bf16[40,1920]{1,0:T(8,128)(2,1)}, u32[]{:S(2)}, u32[]{:S(2)}) %collective-permute-start.1) | collective-permute-done | bytes 153632 | tf_op jit(solution)/shard_map/ppermute | solution.py:423
  65.0 1.5 collective-permute-start.2
  66.5 0.5 collective-permute-start.4
  67.0 0.5 collective-permute-start.6
  67.5 26.0 %collective-permute-done.2.refs_5_.refs_12_ = bf16[5120,128]{1,0:T(8,128)(2,1)S(1)} collective-permute-done((bf16[5120,128]{1,0:T(8,128)(2,1)S(1)}, bf16[5120,128]{1,0:T(8,128)(2,1)S(1)}, u32[]{:S(2)}, u32[]{:S(2)}) %collective-permute-start.2) | collective-permute-done | bytes 1310752 | tf_op jit(solution)/shard_map/ppermute | solution.py:423
  93.5 1.0 copy-done.5
  94.5 0.0 copy-start.8
  94.5 1.5 collective-permute-start.8
  96.1 0.4 collective-permute-done.7.refs_7_.refs_16_
  96.5 1.1 copy-done.9
  97.6 9.9 %collective-permute-done.8.refs_4_ = bf16[48,5120]{1,0:T(8,128)(2,1)S(1)} collective-permute-done((bf16[48,5120]{1,0:T(8,128)(2,1)}, bf16[48,5120]{1,0:T(8,128)(2,1)S(1)}, u32[]{:S(2)}, u32[]{:S(2)}) %collective-permute-start.8) | collective-permute-done | bytes 491552 | tf_op jit(solution)/shard_map/ppermute | solution.py:423
  107.5 1.3 all-gather.3.cloned.1.call-done.both_ref.y0.refs_0_
  108.7 0.0 all-gather.5.cloned.1.call-update
  108.8 0.0 reduce-scatter.4.cloned.1.call-start
  108.8 0.6 collective-permute-start.11
  109.5 7.5 %gate_up_part.1 = (bf16[320,256]{1,0:T(8,128)(2,1)}, bf16[320,256]{1,0:T(8,128)(2,1)}, f32[320,512]{1,0:T(8,128)}, f32[320,512]{1,0:T(8,128)}) custom-call(bf16[320,10240]{1,0:T(8,128)(2,1)} %all-gather.3.cloned.1.call-done.both_ref.y0.refs_0_, bf16[5120,128]{1,0:T(8,128)(2,1)} %bitcast.12, bf16[5120,128]{1,0:T(8,128)(2,1)} %collective-permute-done.refs_1_.refs_11_, ...), custom_call_target="tpu_custom_call" | custom-call | tf_op jit(solution)/shard_map/gate_up_part/pallas_call | solution.py:239
  117.0 0.3 collective-permute-start.10
  117.3 2.4 %collective-permute-done.10.s1 = bf16[320,256]{1,0:T(8,128)(2,1)S(1)} collective-permute-done((bf16[320,256]{1,0:T(8,128)(2,1)}, bf16[320,256]{1,0:T(8,128)(2,1)S(1)}, u32[]{:S(2)}, u32[]{:S(2)}) %collective-permute-start.10) | collective-permute-done | bytes 163872 | tf_op jit(solution)/shard_map/ppermute | solution.py:423
  119.7 0.7 copy-done.19
  120.4 4.5 %flat_part.2 = bf16[128,5120]{1,0:T(8,128)(2,1)} custom-call(bf16[320,10240]{1,0:T(8,128)(2,1)} %all-gather.3.cloned.1.call-done.both_ref.y0.refs_0_, bf16[320,10240]{1,0:T(8,128)(2,1)} %collective-permute-done.9.y1.refs_1_, bf16[320,256]{1,0:T(8,128)(2,1)} %get-tuple-element.102.s0, bf16[320,256]{1,0:T(8,128)(2,1)} %copy-done.19), custom_call_target="tpu_custom_call" | custom-call | tf_op jit(solution)/shard_map/flat_part/pallas_call | solution.py:410
  124.9 0.6 collective-permute-start.16
  125.4 4.5 %collective-permute-done.11.refs_5_ = bf16[80,5120]{1,0:T(8,128)(2,1)S(1)} collective-permute-done((bf16[80,5120]{1,0:T(8,128)(2,1)S(1)}, bf16[80,5120]{1,0:T(8,128)(2,1)S(1)}, u32[]{:S(2)}, u32[]{:S(2)}) %collective-permute-start.11) | collective-permute-done | bytes 819232 | tf_op jit(solution)/shard_map/ppermute | solution.py:423
  129.9 0.5 collective-permute-start.12
  130.5 2.5 %collective-permute-done.12.refs_7_ = bf16[48,5120]{1,0:T(8,128)(2,1)S(1)} collective-permute-done((bf16[48,5120]{1,0:T(8,128)(2,1)S(1)}, bf16[48,5120]{1,0:T(8,128)(2,1)S(1)}, u32[]{:S(2)}, u32[]{:S(2)}) %collective-permute-start.12) | collective-permute-done | bytes 491552 | tf_op jit(solution)/shard_map/ppermute | solution.py:423
  133.0 0.8 copy-done.18
  133.8 0.3 copy-done.16
  134.0 13.0 %back_part.1 = (bf16[320,5248]{1,0:T(8,128)(2,1)}, bf16[320,512]{1,0:T(8,128)(2,1)}, bf16[320,512]{1,0:T(8,128)(2,1)}) custom-call(bf16[320,10240]{1,0:T(8,128)(2,1)} %all-gather.3.cloned.1.call-done.both_ref.y0.refs_0_, f32[320,512]{1,0:T(8,128)} %get-tuple-element.82.refs_1_, f32[320,512]{1,0:T(8,128)} %get-tuple-element.83.refs_2_, ...), custom_call_target="tpu_custom_call" | custom-call | tf_op jit(solution)/shard_map/back_part/pallas_call | solution.py:334
  147.0 0.3 collective-permute-start.15
  147.3 1.1 all-gather.5.cloned.1.call-done.refs_2_
  148.3 0.0 reduce-scatter.4.cloned.1.call-update
  148.4 0.6 collective-permute-done.15.refs_3_.refs_5_
  148.9 0.4 copy-done.10
  149.3 0.3 copy-done.11
  149.7 5.9 %tall_part.3 = (bf16[3200,128]{1,0:T(8,128)(2,1)}, bf16[3200,128]{1,0:T(8,128)(2,1)}) custom-call(bf16[320,10240]{1,0:T(8,128)(2,1)} %all-gather.3.cloned.1.call-done.both_ref.y0.refs_0_, bf16[320,10240]{1,0:T(8,128)(2,1)} %collective-permute-done.9.y1.refs_1_, bf16[320,512]{1,0:T(8,128)(2,1)} %get-tuple-element.105.refs_2_.refs_4_, bf16[320,512]{1,0:T(8,128)(2,1)} %copy-done.11), custom_call_target="tpu_custom_call" | custom-call | tf_op jit(solution)/shard_map/tall_part/pallas_call | solution.py:371
  155.6 0.6 collective-permute-start.18
  156.2 1.6 collective-permute-start.17
  157.7 0.6 collective-permute-start.19
  158.3 1.1 copy-done.20
  159.3 5.2 %flat_part.3 = bf16[128,5120]{1,0:T(8,128)(2,1)} custom-call(bf16[320,10240]{1,0:T(8,128)(2,1)} %all-gather.3.cloned.1.call-done.both_ref.y0.refs_0_, bf16[320,10240]{1,0:T(8,128)(2,1)} %collective-permute-done.9.y1.refs_1_, bf16[320,256]{1,0:T(8,128)(2,1)} %get-tuple-element.102.s0, bf16[320,256]{1,0:T(8,128)(2,1)} %copy-done.19, bf16[128,5120]{1,0:T(8,128)(2,1)} %copy-done.20), custom_call_target="tpu_custom_call" | custom-call | flops 34589999104 | tf_op jit(solution)/shard_map/flat_part/pallas_call | solution.py:410
  164.6 19.4 %collective-permute-done.17 = bf16[640,256]{1,0:T(8,128)(2,1)S(1)} collective-permute-done((bf16[640,256]{1,0:T(8,128)(2,1)S(1)}, bf16[640,256]{1,0:T(8,128)(2,1)S(1)}, u32[]{:S(2)}, u32[]{:S(2)}) %collective-permute-start.17) | collective-permute-done | bytes 327712 | tf_op jit(solution)/shard_map/ppermute | solution.py:423
  183.9 0.7 fusion
  184.7 5.2 %tall_part.4 = (bf16[5120,128]{1,0:T(8,128)(2,1)}, bf16[5120,128]{1,0:T(8,128)(2,1)}) custom-call(bf16[320,10240]{1,0:T(8,128)(2,1)} %all-gather.3.cloned.1.call-done.both_ref.y0.refs_0_, bf16[320,10240]{1,0:T(8,128)(2,1)} %collective-permute-done.9.y1.refs_1_, bf16[320,1920]{1,0:T(8,128)(2,1)} %all-gather.5.cloned.1.call-done.refs_2_, ...), custom_call_target="tpu_custom_call" | custom-call | flops 34589999104 | tf_op jit(solution)/shard_map/tall_part/pallas_call | solution.py:371
  189.9 11.9 %reduce-scatter.4.cloned.1.call-done.refs_0_ = bf16[40,5248]{1,0:T(8,128)(2,1)} async-done(((bf16[320,5248]{1,0:T(8,128)(2,1)}), bf16[40,5248]{1,0:T(8,128)(2,1)}) %reduce-scatter.4.cloned.1.call-update) | async-done | bytes 419856 | tf_op jit(solution)/shard_map/optimization_barrier | solution.py:427
  201.8 1.0 copy-done
  202.8 0.9 ship.1
  203.7 7.3 %all-to-all-start.1 = ((bf16[16,8,1792]{2,1,0:T(8,128)(2,1)}), bf16[16,8,1792]{2,1,0:T(8,128)(2,1)S(1)}, u32[]{:S(2)}, u32[]{:S(2)}) async-start(bf16[16,8,1792]{2,1,0:T(8,128)(2,1)} %ship.1), calls=%async_computation.1 | async-start | bytes 917504 | tf_op jit(solution)/shard_map/all_to_all | solution.py:485
  211.0 0.9 copy-done.13
  211.9 0.3 copy-done.14
  212.2 6.3 %tall_part.5 = (bf16[5120,128]{1,0:T(8,128)(2,1)}, bf16[5120,128]{1,0:T(8,128)(2,1)}) custom-call(bf16[320,10240]{1,0:T(8,128)(2,1)} %all-gather.3.cloned.1.call-done.both_ref.y0.refs_0_, bf16[320,10240]{1,0:T(8,128)(2,1)} %collective-permute-done.9.y1.refs_1_, ...), custom_call_target="tpu_custom_call", output_to_operand_aliasing={{0}: (6, {}), {1}: (7, {})} | custom-call | tf_op jit(solution)/shard_map/tall_part/pallas_call | solution.py:371
  218.5 0.9 all-to-all-done.1.land_ref
  219.4 1.2 take_home.1
  (48 shorter events, 0.1 us)
Async XLA Ops:
  7.2 101.6 %all-gather.3.cloned.1.call-start = ((), (), s32[]{:S(2)}) async-start(), calls=%async_computation.3 | async-start | bytes 7372800 | tf_op jit(solution)/shard_map/all_gather | solution.py:452
  30.6 1.6 copy-start.3
  31.7 116.6 %all-gather.5.cloned.1.call-start = ((), (), s32[]{:S(2)}) async-start(), calls=%async_computation.4 | async-start | bytes 1382400 | tf_op jit(solution)/shard_map/all_gather | solution.py:464
  32.2 34.7 %collective-permute-start = (bf16[5120,128]{1,0:T(8,128)(2,1)S(1)}, bf16[5120,128]{1,0:T(8,128)(2,1)}, u32[]{:S(2)}, u32[]{:S(2)}) collective-permute-start(bf16[5120,128]{1,0:T(8,128)(2,1)S(1)} %bitcast.14), channel_id=1, source_target_pairs={{0,1},{1,0},{2,3},{3,2},{4,5},{5,4},{6,7},{7,6},{8,9},{9,8},{10,11... | collective-permute-start | bytes 3932168 | tf_op jit(solution)/shard_map/ppermute | solution.py:423
  34.6 30.4 %copy-start.4 = (bf16[1,5120,128]{2,1,0:T(8,128)(2,1)S(1)}, bf16[1,5120,128]{2,1,0:T(8,128)(2,1)}, u32[]{:S(2)}) copy-start(bf16[1,5120,128]{2,1,0:T(8,128)(2,1)} %param.12) | copy-start | bytes 3932164
  34.6 30.4 %collective-permute-start.1 = (bf16[40,1920]{1,0:T(8,128)(2,1)S(1)}, bf16[40,1920]{1,0:T(8,128)(2,1)}, u32[]{:S(2)}, u32[]{:S(2)}) collective-permute-start(bf16[40,1920]{1,0:T(8,128)(2,1)S(1)} %slice.20), channel_id=1, source_target_pairs={{0,1},{1,0},{2,3},{3,2},{4,5},{5,4},{6,7},{7,6},{8,9},{9,8},{10,11... | collective-permute-start | bytes 460808 | tf_op jit(solution)/shard_map/ppermute | solution.py:423
  65.0 28.4 %collective-permute-start.2 = (bf16[5120,128]{1,0:T(8,128)(2,1)S(1)}, bf16[5120,128]{1,0:T(8,128)(2,1)S(1)}, u32[]{:S(2)}, u32[]{:S(2)}) collective-permute-start(bf16[5120,128]{1,0:T(8,128)(2,1)S(1)} %bitcast.18), channel_id=1, source_target_pairs={{0,1},{1,0},{2,3},{3,2},{4,5},{5,4},{6,7},{7,6},{8,9},{9,8},{10,11... | collective-permute-start | bytes 3932168 | tf_op jit(solution)/shard_map/ppermute | solution.py:423
  66.5 27.0 %collective-permute-start.3 = (bf16[5120,128]{1,0:T(8,128)(2,1)S(1)}, bf16[5120,128]{1,0:T(8,128)(2,1)S(1)}, u32[]{:S(2)}, u32[]{:S(2)}) collective-permute-start(bf16[5120,128]{1,0:T(8,128)(2,1)S(1)} %bitcast.15), channel_id=1, source_target_pairs={{0,16},{16,0},{1,17},{17,1},{2,18},{18,2},{3,19},{19,3},{4,20},{20... | collective-permute-start | bytes 3932168 | tf_op jit(solution)/shard_map/ppermute | solution.py:423
  66.5 27.0 %collective-permute-start.4 = (bf16[5120,128]{1,0:T(8,128)(2,1)S(1)}, bf16[5120,128]{1,0:T(8,128)(2,1)S(1)}, u32[]{:S(2)}, u32[]{:S(2)}) collective-permute-start(bf16[5120,128]{1,0:T(8,128)(2,1)S(1)} %bitcast.19), channel_id=1, source_target_pairs={{0,16},{16,0},{1,17},{17,1},{2,18},{18,2},{3,19},{19,3},{4,20},{20... | collective-permute-start | bytes 3932168 | tf_op jit(solution)/shard_map/ppermute | solution.py:423
  67.0 27.5 %collective-permute-start.5 = (bf16[128,5120]{1,0:T(8,128)(2,1)}, bf16[128,5120]{1,0:T(8,128)(2,1)S(1)}, u32[]{:S(2)}, u32[]{:S(2)}) collective-permute-start(bf16[128,5120]{1,0:T(8,128)(2,1)} %bitcast.22), channel_id=1, source_target_pairs={{0,16},{16,0},{1,17},{17,1},{2,18},{18,2},{3,19},{19,3},{4,20},{20... | collective-permute-start | bytes 3932168 | tf_op jit(solution)/shard_map/ppermute | solution.py:423
  67.0 27.5 %collective-permute-start.6 = (bf16[5120,128]{1,0:T(8,128)(2,1)}, bf16[5120,128]{1,0:T(8,128)(2,1)S(1)}, u32[]{:S(2)}, u32[]{:S(2)}) collective-permute-start(bf16[5120,128]{1,0:T(8,128)(2,1)} %collective-permute-done.refs_1_.refs_11_), channel_id=1, source_target_pairs={{0,16},{16,0},{1,17},{17,1},{2,18},{18,2},{3,19},{19,3},{4,20},{20... | collective-permute-start | bytes 3932168 | tf_op jit(solution)/shard_map/ppermute | solution.py:423
  93.4 1.1 copy-start.5
  93.4 3.0 %collective-permute-start.7 = (bf16[5120,128]{1,0:T(8,128)(2,1)S(1)}, bf16[5120,128]{1,0:T(8,128)(2,1)S(1)}, u32[]{:S(2)}, u32[]{:S(2)}) collective-permute-start(bf16[5120,128]{1,0:T(8,128)(2,1)S(1)} %collective-permute-done.2.refs_5_.refs_12_), channel_id=1, source_target_pairs={{0,16},{16,0},{1,17},{17,1},{2,18},{18,2},{3,19},{19,3},{4,20},{20... | collective-permute-start | bytes 3932168 | tf_op jit(solution)/shard_map/ppermute | solution.py:423
  93.5 3.0 %copy-start.6 = (bf16[5120,128]{1,0:T(8,128)(2,1)}, bf16[5120,128]{1,0:T(8,128)(2,1)S(1)}, u32[]{:S(2)}) copy-start(bf16[5120,128]{1,0:T(8,128)(2,1)S(1)} %collective-permute-done.3.refs_2_.refs_13_) | copy-start | bytes 3932164
  94.5 2.0 copy-start.7
  94.5 2.0 copy-start.12
  94.5 2.0 copy-start.8
  94.5 12.9 %collective-permute-start.8 = (bf16[48,5120]{1,0:T(8,128)(2,1)}, bf16[48,5120]{1,0:T(8,128)(2,1)S(1)}, u32[]{:S(2)}, u32[]{:S(2)}) collective-permute-start(bf16[48,5120]{1,0:T(8,128)(2,1)} %slice.15), channel_id=1, source_target_pairs={{0,1},{1,0},{2,3},{3,2},{4,5},{5,4},{6,7},{7,6},{8,9},{9,8},{10,11... | collective-permute-start | bytes 1474568 | tf_op jit(solution)/shard_map/ppermute | solution.py:423
  96.5 1.1 copy-start.9
  107.5 22.5 %copy-start.17 = (bf16[48,5120]{1,0:T(8,128)(2,1)}, bf16[48,5120]{1,0:T(8,128)(2,1)S(1)}, u32[]{:S(2)}) copy-start(bf16[48,5120]{1,0:T(8,128)(2,1)S(1)} %collective-permute-done.8.refs_4_) | copy-start | bytes 1474564
  108.7 11.0 %collective-permute-start.9 = (bf16[320,10240]{1,0:T(8,128)(2,1)}, bf16[320,10240]{1,0:T(8,128)(2,1)}, u32[]{:S(2)}, u32[]{:S(2)}) collective-permute-start(bf16[320,10240]{1,0:T(8,128)(2,1)} %all-gather.3.cloned.1.call-done.both_ref.y0.refs_0_), channel_id=1, source_target_pairs={{0,16},{16,0},{1,17},{17,1},{2,18},{18,2},{3,19},{19,3},{4,20},{20... | collective-permute-start | bytes 19660808 | tf_op jit(solution)/shard_map/ppermute | solution.py:423
  108.8 93.0 %reduce-scatter.4.cloned.1.call-start = ((), (), s32[]{:S(2)}) async-start(), calls=%async_computation.5 | async-start | bytes 3778560
  108.8 21.1 %collective-permute-start.11 = (bf16[80,5120]{1,0:T(8,128)(2,1)S(1)}, bf16[80,5120]{1,0:T(8,128)(2,1)S(1)}, u32[]{:S(2)}, u32[]{:S(2)}) collective-permute-start(bf16[80,5120]{1,0:T(8,128)(2,1)S(1)} %slice.16), channel_id=1, source_target_pairs={{0,1},{1,0},{2,3},{3,2},{4,5},{5,4},{6,7},{7,6},{8,9},{9,8},{10,11... | collective-permute-start | bytes 2457608 | tf_op jit(solution)/shard_map/ppermute | solution.py:423
  117.0 2.8 %collective-permute-start.10 = (bf16[320,256]{1,0:T(8,128)(2,1)}, bf16[320,256]{1,0:T(8,128)(2,1)S(1)}, u32[]{:S(2)}, u32[]{:S(2)}) collective-permute-start(bf16[320,256]{1,0:T(8,128)(2,1)} %get-tuple-element.80), channel_id=1, source_target_pairs={{0,16},{16,0},{1,17},{17,1},{2,18},{18,2},{3,19},{19,3},{4,20},{20... | collective-permute-start | bytes 491528 | tf_op jit(solution)/shard_map/ppermute | solution.py:423
  119.7 0.7 copy-start.19
  124.9 33.4 %collective-permute-start.16 = (bf16[128,5120]{1,0:T(8,128)(2,1)}, bf16[128,5120]{1,0:T(8,128)(2,1)S(1)}, u32[]{:S(2)}, u32[]{:S(2)}) collective-permute-start(bf16[128,5120]{1,0:T(8,128)(2,1)} %flat_part.2), channel_id=1, source_target_pairs={{0,1},{1,0},{2,3},{3,2},{4,5},{5,4},{6,7},{7,6},{8,9},{9,8},{10,11... | collective-permute-start | bytes 3932168 | tf_op jit(solution)/shard_map/ppermute | solution.py:423
  129.9 3.0 %copy-start.15 = (bf16[80,5120]{1,0:T(8,128)(2,1)}, bf16[80,5120]{1,0:T(8,128)(2,1)S(1)}, u32[]{:S(2)}) copy-start(bf16[80,5120]{1,0:T(8,128)(2,1)S(1)} %collective-permute-done.11.refs_5_) | copy-start | bytes 2457604
  129.9 3.0 %collective-permute-start.13 = (bf16[80,5120]{1,0:T(8,128)(2,1)S(1)}, bf16[80,5120]{1,0:T(8,128)(2,1)S(1)}, u32[]{:S(2)}, u32[]{:S(2)}) collective-permute-start(bf16[80,5120]{1,0:T(8,128)(2,1)S(1)} %collective-permute-done.11.refs_5_), channel_id=1, source_target_pairs={{0,16},{16,0},{1,17},{17,1},{2,18},{18,2},{3,19},{19,3},{4,20},{20... | collective-permute-start | bytes 2457608 | tf_op jit(solution)/shard_map/ppermute | solution.py:423
  129.9 3.0 %collective-permute-start.12 = (bf16[48,5120]{1,0:T(8,128)(2,1)S(1)}, bf16[48,5120]{1,0:T(8,128)(2,1)S(1)}, u32[]{:S(2)}, u32[]{:S(2)}) collective-permute-start(bf16[48,5120]{1,0:T(8,128)(2,1)S(1)} %collective-permute-done.8.refs_4_), channel_id=1, source_target_pairs={{0,16},{16,0},{1,17},{17,1},{2,18},{18,2},{3,19},{19,3},{4,20},{20... | collective-permute-start | bytes 1474568 | tf_op jit(solution)/shard_map/ppermute | solution.py:423
  133.0 0.8 copy-start.18
  133.0 1.1 copy-start.16
  147.0 1.9 collective-permute-start.15
  148.3 1.0 copy-start.10
  148.3 36.3 %collective-permute-start.14 = (bf16[320,1920]{1,0:T(8,128)(2,1)}, bf16[320,1920]{1,0:T(8,128)(2,1)}, u32[]{:S(2)}, u32[]{:S(2)}) collective-permute-start(bf16[320,1920]{1,0:T(8,128)(2,1)} %all-gather.5.cloned.1.call-done.refs_2_), channel_id=1, source_target_pairs={{0,16},{16,0},{1,17},{17,1},{2,18},{18,2},{3,19},{19,3},{4,20},{20... | collective-permute-start | bytes 3686408 | tf_op jit(solution)/shard_map/ppermute | solution.py:423
  148.9 0.7 copy-start.11
  155.6 55.4 %collective-permute-start.18 = (bf16[3200,128]{1,0:T(8,128)(2,1)}, bf16[3200,128]{1,0:T(8,128)(2,1)S(1)}, u32[]{:S(2)}, u32[]{:S(2)}) collective-permute-start(bf16[3200,128]{1,0:T(8,128)(2,1)} %get-tuple-element.97), channel_id=1, source_target_pairs={{0,1},{1,0},{2,3},{3,2},{4,5},{5,4},{6,7},{7,6},{8,9},{9,8},{10,11... | collective-permute-start | bytes 2457608 | tf_op jit(solution)/shard_map/ppermute | solution.py:423
  156.2 27.7 %collective-permute-start.17 = (bf16[640,256]{1,0:T(8,128)(2,1)S(1)}, bf16[640,256]{1,0:T(8,128)(2,1)S(1)}, u32[]{:S(2)}, u32[]{:S(2)}) collective-permute-start(bf16[640,256]{1,0:T(8,128)(2,1)S(1)} %pad_maximum_fusion), channel_id=1, source_target_pairs={{0,1},{1,0},{2,3},{3,2},{4,5},{5,4},{6,7},{7,6},{8,9},{9,8},{10,11... | collective-permute-start | bytes 983048 | tf_op jit(solution)/shard_map/ppermute | solution.py:423
  157.7 53.3 %collective-permute-start.19 = (bf16[3200,128]{1,0:T(8,128)(2,1)}, bf16[3200,128]{1,0:T(8,128)(2,1)S(1)}, u32[]{:S(2)}, u32[]{:S(2)}) collective-permute-start(bf16[3200,128]{1,0:T(8,128)(2,1)} %get-tuple-element.113), channel_id=1, source_target_pairs={{0,1},{1,0},{2,3},{3,2},{4,5},{5,4},{6,7},{7,6},{8,9},{9,8},{10,11... | collective-permute-start | bytes 2457608 | tf_op jit(solution)/shard_map/ppermute | solution.py:423
  158.3 1.1 copy-start.20
  201.8 1.0 copy-start
  203.7 15.7 %all-to-all-start.1 = ((bf16[16,8,1792]{2,1,0:T(8,128)(2,1)}), bf16[16,8,1792]{2,1,0:T(8,128)(2,1)S(1)}, u32[]{:S(2)}, u32[]{:S(2)}) async-start(bf16[16,8,1792]{2,1,0:T(8,128)(2,1)} %ship.1), calls=%async_computation.1 | async-start | bytes 917504 | tf_op jit(solution)/shard_map/all_to_all | solution.py:485
  211.0 0.9 copy-start.13
  211.0 1.1 copy-start.14
  212.2 7.2 %copy-start.1 = (f32[128]{0:T(128)S(1)}, f32[128]{0:T(128)}, u32[]{:S(2)}) copy-start(f32[128]{0:T(128)} %param.9) | copy-start | bytes 1540
  212.2 7.2 %copy-start.2 = (s32[1,128]{1,0:T(1,128)S(1)}, s32[1,128]{1,0:T(1,128)}, u32[]{:S(2)}) copy-start(s32[1,128]{1,0:T(1,128)} %get-tuple-element.110.place_ref) | copy-start | bytes 1540
Sparse Core Ops, SparseCore 0:
  31.9 76.8 all-gather.2
  110.5 37.7 all-gather.4
  150.9 50.8 reduce-scatter.3
